TPU v7x, 32 devices: a whole 2x2x4 slice. The times are simulated.
32 devices in a mesh: ctx: 4 (over z), fsdp: 8 (over y, x, core).
Axes of the slice: x: 2, y: 2, z: 4, core: 2. Of those that a mesh axis runs over, the one named last changes fastest.
Arguments:
- hidden_in: bfloat16 [8, 1024, 1536], P('fsdp', 'ctx'), may hold values from -6 to 6
- w_qkv: bfloat16 [1536, 2048], P('fsdp'), may hold values from -0.15625 to 0.15625
- b_qkv: bfloat16 [2048], P('fsdp'), may hold values from -3 to 3
- w_out: bfloat16 [1536, 1536], P('fsdp'), may hold values from -1 to 1
- w_gate_up: bfloat16 [1536, 17920], P('fsdp'), may hold values from -0.15625 to 0.15625
- w_down: bfloat16 [8960, 1536], P('fsdp'), may hold values from -0.0625 to 0.0625
- gain_attn: bfloat16 [1536], P('fsdp'), may hold values from 0.5 to 1.5
- gain_mlp: bfloat16 [1536], P('fsdp'), may hold values from 0.5 to 1.5
- block_order: int32 [8, 8], P('fsdp'), may hold values from 0 to 7, as said below
- cotangent: bfloat16 [8, 1024, 1536], P('fsdp', 'ctx'), may hold values from -6 to 6
Outputs:
- hidden_out: bfloat16 [8, 1024, 1536], P('fsdp', 'ctx')
- grad_hidden: bfloat16 [8, 1024, 1536], P('fsdp', 'ctx')
- grad_w_qkv: float32 [1536, 2048], P('fsdp')
- grad_b_qk: float32 [1792], P('fsdp')
- grad_b_v: float32 [256], P('fsdp')
- grad_w_out: float32 [1536, 1536], P('fsdp')
- grad_w_gate_up: float32 [1536, 17920], P('fsdp')
- grad_w_down: float32 [8960, 1536], P('fsdp')
- grad_gain_attn: float32 [1536], P('fsdp')
- grad_gain_mlp: float32 [1536], P('fsdp')
Inputs may be any that keep to these rules, and one draw needn't show every extreme that they name: `block_order`: each row holds every number below 8 once: the places of the stored blocks of a sequence of 128 tokens each.
All inputs are finite; a program needn't handle non-finite values.
Results may differ from a plain program's by a relative error of at most 0.025.
Values may be sent and summed in bfloat16 or wider, within the bound.
A program may use at most 448 MiB of HBM per device.

v0:
```python
import jax
import jax.numpy as jnp
from jax import lax
from jax.sharding import PartitionSpec as P

HEADS = 12
KV_HEADS = 2
HEAD_DIM = 128
FF = 8960


EPSILON = 1e-06
THETA = 1000000.0
MASKED = -1e30


def from_behind(block, axis, distance):
    devices = range(lax.axis_size(axis))
    route = [((i - distance) % len(devices), i) for i in devices]
    return lax.ppermute(block, axis, route)


def angle_tables(places):
    half_dim = HEAD_DIM // 2
    freqs = THETA ** (-(jnp.arange(half_dim).astype(jnp.float32) * 2.0 / HEAD_DIM))
    angles = places.astype(jnp.float32)[:, None] * freqs[None, :]
    return (jnp.cos(angles), jnp.sin(angles))


def rotate(values_in, cosine, sine_table):
    half_dim = HEAD_DIM // 2
    shape = (cosine.shape[0],) + (1,) * (values_in.ndim - 2) + (half_dim,)
    cos_b = cosine.reshape(shape)
    sin_b = sine_table.reshape(shape)
    first = values_in[..., :half_dim]
    second = values_in[..., half_dim:]
    return jnp.concatenate([first * cos_b - second * sin_b, second * cos_b + first * sin_b], -1)


def add_rows(left, piece):
    return jnp.dot(left, piece, preferred_element_type=jnp.float32)


def against(left, piece):
    return lax.dot_general(
        left, piece, (((1,), (1,)), ((), ())), preferred_element_type=jnp.float32
    )


def shards(
    hidden_in, w_qkv, b_qkv, w_out, w_gate_up, w_down, gain_attn, gain_mlp, block_order, cotangent
):
    members = lax.axis_size("ctx")
    my_index = lax.axis_index("ctx")
    groups = HEADS // KV_HEADS
    query_width = HEADS * HEAD_DIM
    key_width = KV_HEADS * HEAD_DIM
    tok_rows = hidden_in.shape[1]
    piece_len = tok_rows // 2
    score_scale = HEAD_DIM ** (-0.5)
    order_row = block_order[0]
    row_ids = jnp.arange(tok_rows, dtype=jnp.int32)

    def places(owner_index):
        picked = lax.dynamic_slice_in_dim(order_row, 2 * owner_index, 2)
        return (
            jnp.where(row_ids < piece_len, picked[0], picked[1]) * piece_len + row_ids % piece_len
        )

    query_places = places(my_index)
    cosine, sine_table = angle_tables(query_places)
    whole_qkv, whole_bias, whole_out, gain_one, gain_two = (
        lax.all_gather(w_qkv, "fsdp", axis=0, tiled=True),
        lax.all_gather(b_qkv, "fsdp", axis=0, tiled=True),
        lax.all_gather(w_out, "fsdp", axis=0, tiled=True),
        lax.all_gather(gain_attn, "fsdp", axis=0, tiled=True),
        lax.all_gather(gain_mlp, "fsdp", axis=0, tiled=True),
    )
    inputs = hidden_in[0].astype(jnp.float32)
    inverse_one = lax.rsqrt(jnp.mean(inputs * inputs, -1, keepdims=True) + EPSILON)
    gain_first = gain_one.astype(jnp.float32)
    normed = (inputs * inverse_one * gain_first).astype(jnp.bfloat16)
    projected = jnp.dot(normed, whole_qkv, preferred_element_type=jnp.float32) + whole_bias.astype(
        jnp.float32
    )
    queries = rotate(
        projected[:, :query_width].reshape(tok_rows, KV_HEADS, groups, HEAD_DIM), cosine, sine_table
    ).astype(jnp.bfloat16)
    rotated_keys = rotate(
        projected[:, query_width : query_width + key_width].reshape(tok_rows, KV_HEADS, HEAD_DIM),
        cosine,
        sine_table,
    ).astype(jnp.bfloat16)
    values_low = (
        projected[:, query_width + key_width :]
        .reshape(tok_rows, KV_HEADS, HEAD_DIM)
        .astype(jnp.bfloat16)
    )
    paired = jnp.stack([rotated_keys, values_low])
    row_top = jnp.full((KV_HEADS, groups, tok_rows, 1), MASKED, jnp.float32)
    row_total = jnp.zeros((KV_HEADS, groups, tok_rows, 1), jnp.float32)
    weighted = jnp.zeros((KV_HEADS, groups, tok_rows, HEAD_DIM), jnp.float32)
    moving = paired
    for turn_index in range(members):
        key_places = places((my_index - turn_index) % members)
        visible = key_places[None, :] <= query_places[:, None]
        scores = (
            jnp.einsum("qkgd,tkd->kgqt", queries, moving[0], preferred_element_type=jnp.float32)
            * score_scale
        )
        scores = jnp.where(visible, scores, MASKED)
        new_top = jnp.maximum(row_top, jnp.max(scores, -1, keepdims=True))
        weights_now = jnp.where(visible, jnp.exp(scores - new_top), 0.0)
        fade_factor = jnp.exp(row_top - new_top)
        row_total = row_total * fade_factor + jnp.sum(weights_now, -1, keepdims=True)
        weighted = weighted * fade_factor + jnp.einsum(
            "kgqt,tkd->kgqd",
            weights_now.astype(jnp.bfloat16),
            moving[1],
            preferred_element_type=jnp.float32,
        )
        row_top = new_top
        if turn_index < members - 1:
            moving = from_behind(moving, "ctx", 1)
    attn_heads = weighted / row_total
    log_total = row_top + jnp.log(row_total)
    attn_low = attn_heads.transpose(2, 0, 1, 3).reshape(tok_rows, query_width).astype(jnp.bfloat16)
    middle = inputs + jnp.dot(attn_low, whole_out, preferred_element_type=jnp.float32)
    inverse_two = lax.rsqrt(jnp.mean(middle * middle, -1, keepdims=True) + EPSILON)
    gain_second = gain_two.astype(jnp.float32)
    normed_two = (middle * inverse_two * gain_second).astype(jnp.bfloat16)
    mixed = add_rows(normed_two, lax.all_gather(w_gate_up, "fsdp", axis=0, tiled=True))
    gate_part = mixed[:, :FF]
    up_part = mixed[:, FF:]
    sigmoid_gate = jax.nn.sigmoid(gate_part)
    activated = (gate_part * sigmoid_gate * up_part).astype(jnp.bfloat16)
    down_result = add_rows(activated, lax.all_gather(w_down, "fsdp", axis=0, tiled=True))
    hidden_out = (middle + down_result).astype(jnp.bfloat16)[None]
    grad_low = cotangent[0]
    grad_full = grad_low.astype(jnp.float32)
    grad_act = against(grad_low, lax.all_gather(w_down, "fsdp", axis=0, tiled=True))
    picked = activated
    grad_down = lax.psum_scatter(
        lax.dot_general(
            picked, grad_low, (((0,), (0,)), ((), ())), preferred_element_type=jnp.float32
        ).astype(jnp.bfloat16),
        "fsdp",
        scatter_dimension=0,
        tiled=True,
    )
    grad_gate = grad_act * up_part * (sigmoid_gate * (1.0 + gate_part * (1.0 - sigmoid_gate)))
    grad_up = grad_act * gate_part * sigmoid_gate
    grad_mixed = jnp.concatenate([grad_gate, grad_up], 1).astype(jnp.bfloat16)
    picked = normed_two
    grad_gate_up = lax.psum_scatter(
        lax.dot_general(
            picked, grad_mixed, (((0,), (0,)), ((), ())), preferred_element_type=jnp.float32
        ).astype(jnp.bfloat16),
        "fsdp",
        scatter_dimension=0,
        tiled=True,
    )
    grad_normed_two = against(grad_mixed, lax.all_gather(w_gate_up, "fsdp", axis=0, tiled=True))
    scaled_two = gain_second * grad_normed_two
    gain_two_local = jnp.sum(grad_normed_two * middle * inverse_two, 0)
    grad_middle = (
        grad_full
        + inverse_two * scaled_two
        - middle
        * (inverse_two * inverse_two * inverse_two)
        * jnp.mean(scaled_two * middle, -1, keepdims=True)
    )
    grad_branch = grad_middle.astype(jnp.bfloat16)
    out_local = lax.dot_general(
        attn_low, grad_branch, (((0,), (0,)), ((), ())), preferred_element_type=jnp.float32
    )
    grad_attn = against(grad_branch, whole_out).astype(jnp.bfloat16)
    grad_heads = grad_attn.reshape(tok_rows, KV_HEADS, groups, HEAD_DIM).transpose(1, 2, 0, 3)
    row_delta = jnp.sum(grad_heads.astype(jnp.float32) * attn_heads, -1, keepdims=True)
    grad_queries = jnp.zeros((KV_HEADS, groups, tok_rows, HEAD_DIM), jnp.float32)
    owed = jnp.zeros((2, tok_rows, KV_HEADS, HEAD_DIM), jnp.float32)
    moving = paired
    for turn_index in range(members):
        key_places = places((my_index - turn_index) % members)
        visible = key_places[None, :] <= query_places[:, None]
        scores = (
            jnp.einsum("qkgd,tkd->kgqt", queries, moving[0], preferred_element_type=jnp.float32)
            * score_scale
        )
        probs = jnp.where(visible, jnp.exp(scores - log_total), 0.0)
        grad_values = jnp.einsum(
            "kgqt,kgqd->tkd",
            probs.astype(jnp.bfloat16),
            grad_heads,
            preferred_element_type=jnp.float32,
        )
        grad_probs = jnp.einsum(
            "kgqd,tkd->kgqt", grad_heads, moving[1], preferred_element_type=jnp.float32
        )
        grad_scores = (probs * (grad_probs - row_delta)).astype(jnp.bfloat16)
        grad_queries = (
            grad_queries
            + jnp.einsum(
                "kgqt,tkd->kgqd", grad_scores, moving[0], preferred_element_type=jnp.float32
            )
            * score_scale
        )
        grad_keys = (
            jnp.einsum("kgqt,qkgd->tkd", grad_scores, queries, preferred_element_type=jnp.float32)
            * score_scale
        )
        owed = owed + jnp.stack([grad_keys, grad_values])
        if turn_index < members - 1:
            moving = from_behind(moving, "ctx", 1)
        owed = from_behind(owed.astype(jnp.bfloat16), "ctx", 1).astype(owed.dtype)
    query_back = rotate(grad_queries.transpose(2, 0, 1, 3), cosine, -sine_table).reshape(
        tok_rows, query_width
    )
    key_back = rotate(owed[0], cosine, -sine_table).reshape(tok_rows, key_width)
    value_back = owed[1].reshape(tok_rows, key_width)
    grad_projected = jnp.concatenate([query_back, key_back, value_back], 1).astype(jnp.bfloat16)
    bias_local = jnp.sum(grad_projected.astype(jnp.float32), 0)
    qk_bias_local = bias_local[: query_width + key_width]
    value_bias_local = bias_local[query_width + key_width :]
    qkv_local = lax.dot_general(
        normed, grad_projected, (((0,), (0,)), ((), ())), preferred_element_type=jnp.float32
    )
    grad_normed = against(grad_projected, whole_qkv)
    scaled_one = gain_first * grad_normed
    gain_one_local = jnp.sum(grad_normed * inputs * inverse_one, 0)
    grad_inputs = (
        grad_middle
        + inverse_one * scaled_one
        - inputs
        * (inverse_one * inverse_one * inverse_one)
        * jnp.mean(scaled_one * inputs, -1, keepdims=True)
    )
    shard_qkv, shard_qk_bias, shard_value_bias, shard_out, shard_gain_one, shard_gain_two = (
        lax.psum_scatter(
            qkv_local.astype(jnp.bfloat16), "fsdp", scatter_dimension=0, tiled=True
        ).astype(jnp.float32),
        lax.psum_scatter(
            qk_bias_local.astype(jnp.bfloat16), "fsdp", scatter_dimension=0, tiled=True
        ).astype(jnp.float32),
        lax.psum_scatter(
            value_bias_local.astype(jnp.bfloat16), "fsdp", scatter_dimension=0, tiled=True
        ).astype(jnp.float32),
        lax.psum_scatter(
            out_local.astype(jnp.bfloat16), "fsdp", scatter_dimension=0, tiled=True
        ).astype(jnp.float32),
        lax.psum_scatter(
            gain_one_local.astype(jnp.bfloat16), "fsdp", scatter_dimension=0, tiled=True
        ).astype(jnp.float32),
        lax.psum_scatter(
            gain_two_local.astype(jnp.bfloat16), "fsdp", scatter_dimension=0, tiled=True
        ).astype(jnp.float32),
    )
    summed = (
        lax.psum(shard_qkv.astype(jnp.bfloat16), "ctx").astype(jnp.float32),
        lax.psum(shard_qk_bias.astype(jnp.bfloat16), "ctx").astype(jnp.float32),
        lax.psum(shard_value_bias.astype(jnp.bfloat16), "ctx").astype(jnp.float32),
        lax.psum(shard_out.astype(jnp.bfloat16), "ctx").astype(jnp.float32),
        lax.psum(grad_gate_up, "ctx").astype(jnp.float32),
        lax.psum(grad_down, "ctx").astype(jnp.float32),
        lax.psum(shard_gain_one.astype(jnp.bfloat16), "ctx").astype(jnp.float32),
        lax.psum(shard_gain_two.astype(jnp.bfloat16), "ctx").astype(jnp.float32),
    )
    return (
        hidden_out,
        grad_inputs.astype(jnp.bfloat16)[None],
        summed[0],
        summed[1],
        summed[2],
        summed[3],
        summed[4],
        summed[5],
        summed[6],
        summed[7],
    )


def solution(mesh):
    placed = (
        P("fsdp", "ctx", None),
        P("fsdp", None),
        P("fsdp"),
        P("fsdp", None),
        P("fsdp", None),
        P("fsdp", None),
        P("fsdp"),
        P("fsdp"),
        P("fsdp", None),
        P("fsdp", "ctx", None),
    )
    return jax.shard_map(
        shards,
        mesh=mesh,
        in_specs=placed,
        out_specs=(
            P("fsdp", "ctx", None),
            P("fsdp", "ctx", None),
            P("fsdp", None),
            P("fsdp"),
            P("fsdp"),
            P("fsdp", None),
            P("fsdp", None),
            P("fsdp", None),
            P("fsdp"),
            P("fsdp"),
        ),
        check_vma=False,
    )
```

profile of v0, /device:TPU:0, one launch (start us, length us, event | category | flops | bytes accessed | tf_op | source)
XLA Modules:
  0.0 1584.3 jit_solution(9242171332256071598)
XLA Ops:
  12.0 15.7 all-reduce.7
  27.7 7.9 all-gather
  49.4 8.9 all-gather.6.cloned.1.call-done
  58.3 4.6 convolution_add_fusion.1
  85.9 2.8 collective-permute-done.1
  89.5 7.9 collective-permute-done.2
  105.0 4.4 multiply_reduce_fusion.3
  110.3 242.7 %all-gather.10.cloned.1.call-done = bf16[1536,17920]{1,0:T(8,128)(2,1)} async-done(((bf16[192,17920]{1,0:T(8,128)(2,1)}), bf16[1536,17920]{1,0:T(8,128)(2,1)}) %all-gather.10.cloned.1.call-update) | async-done | bytes 55050256 | tf_op jit(solution)/shard_map/all_gather | solution.py:132
  353.0 29.5 %fusion.163 = f32[256,17920]{1,0:T(8,128)} fusion(bf16[1536,17920]{1,0:T(8,128)(2,1)} %all-gather.10.cloned.1.call-done, f32[256,1536]{1,0:T(8,128)S(1)} %get-tuple-element.99, f32[1536]{0:T(1024)S(1)} %convert_element_type.220, f32[256]{0:T(256)S(1)} %get-tuple-element.66), kind=kOutput, calls=%fused_computation.258 | convolution fusion | flops 14094041088 | bytes 74980352 | tf_op jit(solution)/shard_map/dot_general | solution.py:41
  382.5 107.6 %all-gather.12.cloned.1.call-done = bf16[8960,1536]{1,0:T(8,128)(2,1)} async-done(((bf16[1120,1536]{1,0:T(8,128)(2,1)}), bf16[8960,1536]{1,0:T(8,128)(2,1)}) %all-gather.12.cloned.1.call-update) | async-done | bytes 27525136 | tf_op jit(solution)/shard_map/all_gather | solution.py:137
  490.1 21.6 %multiply_convert_fusion.1 = (bf16[256,8960]{1,0:T(8,128)(2,1)}, bf16[256,8960]{1,0:T(8,128)(2,1)}, bf16[256,8960]{1,0:T(8,128)(2,1)}) fusion(f32[256,17920]{1,0:T(8,128)} %fusion.163, bf16[8960,1536]{1,0:T(8,128)(2,1)} %all-gather.12.cloned.1.call-done, bf16[1,256,1536]{2,1,0:T(8,128)(2,1)} %param.19), kind=kOutput, calls=%fused_computation.4 | convolution fusion | flops 7083130880 | bytes 60424192 | tf_op jit(solution)/shard_map/dot_general | solution.py:45
  511.7 26.0 %multiply_reduce_fusion = (bf16[1536]{0:T(1024)(128)(2,1)}, f32[256]{0:T(256)}, f32[256,1536]{1,0:T(8,128)}) fusion(f32[256,1536]{1,0:T(8,128)S(1)} %get-tuple-element.99, f32[256]{0:T(256)S(1)} %get-tuple-element.66, f32[1536]{0:T(1024)S(1)} %convert_element_type.220, bf16[1536,17920]{1,0:T(8,128)(2,1)} %all-gather.10.cloned.1.call-done, ...), kind=kOutput, calls=%fused_computation.84 | convolution fusion | flops 14113568768 | bytes 67382272 | tf_op jit(solution)/shard_map/dot_general | solution.py:45
  540.9 3.6 convolution_convert_fusion.3
  544.5 4.6 convolution_convert_fusion.4
  551.5 4.1 multiply_reduce_fusion.1
  573.9 7.3 collective-permute-done.4
  582.6 8.0 collective-permute-done.5
  594.9 5.3 collective-permute-done.6
  601.7 5.4 convolution_convert_fusion.2
  607.2 18.1 %convolution_convert_fusion.1 = bf16[8960,1536]{1,0:T(8,128)(2,1)} fusion(bf16[256,8960]{1,0:T(8,128)(2,1)} %get-tuple-element.41, bf16[1,256,1536]{2,1,0:T(8,128)(2,1)} %param.19), kind=kOutput, calls=%fused_computation.1 | convolution fusion | flops 7060193280 | bytes 32899072 | tf_op jit(solution)/shard_map/dot_general | solution.py:144
  625.4 26.2 %convolution_convert_fusion = bf16[1536,17920]{1,0:T(8,128)(2,1)} fusion(bf16[256,8960]{1,0:T(8,128)(2,1)} %get-tuple-element.40, bf16[256,8960]{1,0:T(8,128)(2,1)} %get-tuple-element.39, f32[256,1536]{1,0:T(8,128)} %copy-done.1, f32[1536]{0:T(1024)S(1)} %convert_element_type.220, f32[256]{0:T(256)S(1)} %get-tuple-element.66), kind=kOutput, calls=%fused_computation | convolution fusion | flops 14139916288 | bytes 65805312 | tf_op jit(solution)/shard_map/dot_general | solution.py:156
  651.9 19.5 %reduce-scatter.5.cloned.1.call-done = bf16[192,2048]{1,0:T(8,128)(2,1)} async-done(((bf16[1536,2048]{1,0:T(8,128)(2,1)}), bf16[192,2048]{1,0:T(8,128)(2,1)}) %reduce-scatter.5.cloned.1.call-update) | async-done | bytes 786448 | tf_op jit(solution)/shard_map/reduce_scatter | solution.py:239
  671.4 172.8 %reduce-scatter.11.cloned.1.call-done = bf16[1120,1536]{1,0:T(8,128)(2,1)} async-done(((bf16[8960,1536]{1,0:T(8,128)(2,1)}), bf16[1120,1536]{1,0:T(8,128)(2,1)}) %reduce-scatter.11.cloned.1.call-update) | async-done | bytes 3440656 | tf_op jit(solution)/shard_map/reduce_scatter | solution.py:143
  844.2 314.0 %reduce-scatter.9.cloned.1.call-done = bf16[192,17920]{1,0:T(8,128)(2,1)} async-done(((bf16[1536,17920]{1,0:T(8,128)(2,1)}), bf16[192,17920]{1,0:T(8,128)(2,1)}) %reduce-scatter.9.cloned.1.call-update) | async-done | bytes 6881296 | tf_op jit(solution)/shard_map/reduce_scatter | solution.py:155
  1159.9 16.2 %fusion.14 = bf16[1,256,1536]{2,1,0:T(8,128)(2,1)} fusion(f32[256,1536]{1,0:T(8,128)} %copy-done.1, bf16[256,8960]{1,0:T(8,128)(2,1)} %get-tuple-element.41, bf16[8960,1536]{1,0:T(8,128)(2,1)} %all-gather.12.cloned.1.call-done), kind=kOutput, calls=%fused_computation.48 | convolution fusion | flops 7047217152 | bytes 34471936 | tf_op jit(solution)/shard_map/dot_general | solution.py:41
  1176.5 6.0 fusion.43
  1182.5 24.7 %all-reduce.6 = (bf16[1792]{0:T(1024)(128)(2,1)S(1)}, bf16[256]{0:T(256)(128)(2,1)S(1)}, bf16[1536]{0:T(1024)(128)(2,1)S(1)}, bf16[1536]{0:T(1024)(128)(2,1)S(1)}) all-reduce(bf16[1792]{0:T(1024)(128)(2,1)S(1)} %bitcast.460, bf16[256]{0:T(256)(128)(2,1)S(1)} %slice.185, ...), channel_id=3, replica_groups=mesh['ctx'=4,'fsdp'=8] {'fsdp'}, use_global_device_ids=true, to_apply=%region_16.17.clone | all-reduce | flops 5120 | bytes 20480
  1207.5 13.7 all-reduce.8
  1223.3 2.8 fusion.108
  1226.1 335.4 %all-reduce.12.cloned.1.call-done = (bf16[192,2048]{1,0:T(8,128)(2,1)}, bf16[192,1536]{1,0:T(8,128)(2,1)}, bf16[192,17920]{1,0:T(8,128)(2,1)}, bf16[1120,1536]{1,0:T(8,128)(2,1)}) async-done(((bf16[192,2048]{1,0:T(8,128)(2,1)}, bf16[192,1536]{1,0:T(8,128)(2,1)}, bf16[192,17920]{1,0:T(8,128)(2,1)}, bf16[1120,1536]{1,0:T(8,128)(2,1)}), (bf16[192,2048]{1,0:T(8,128)(2,1)}, bf16[192,1536]{1,0:T(8,128)(2,1)}, ...) | async-done | bytes 11698192 | tf_op jit(solution)/shard_map/psum | solution.py:259
  1566.8 3.8 convert_element_type.253
  1570.6 6.7 convert_element_type.251
  (257 shorter events, 88.7 us)
Async XLA Ops:
  7.2 51.1 %all-gather.6.cloned.1.call-start = ((), (), s32[]{:S(2)}) async-start(), calls=%async_computation.4 | async-start | bytes 7077888 | tf_op jit(solution)/shard_map/all_gather | solution.py:73
  7.9 97.1 %all-gather.8.cloned.1.call-start = ((), (), s32[]{:S(2)}) async-start(), calls=%async_computation.5 | async-start | bytes 5308416 | tf_op jit(solution)/shard_map/all_gather | solution.py:75
  8.7 344.3 %all-gather.10.cloned.1.call-start = ((), (), s32[]{:S(2)}) async-start(), calls=%async_computation.6 | async-start | bytes 61931520 | tf_op jit(solution)/shard_map/all_gather | solution.py:132
  9.4 26.2 %copy-start.54 = (s32[1,8]{1,0:T(1,128)S(1)}, s32[1,8]{1,0:T(1,128)}, u32[]{:S(2)}) copy-start(s32[1,8]{1,0:T(1,128)} %param.18) | copy-start | bytes 100
  9.4 37.0 %copy-start = (bf16[1,256,1536]{2,1,0:T(8,128)(2,1)S(1)}, bf16[1,256,1536]{2,1,0:T(8,128)(2,1)}, u32[]{:S(2)}) copy-start(bf16[1,256,1536]{2,1,0:T(8,128)(2,1)} %param.10) | copy-start | bytes 2359300
  9.5 480.6 %all-gather.12.cloned.1.call-start = ((), (), s32[]{:S(2)}) async-start(), calls=%async_computation.7 | async-start | bytes 30965760 | tf_op jit(solution)/shard_map/all_gather | solution.py:137
  10.0 641.9 %reduce-scatter.7.cloned.1.call-start = ((), (), s32[]{:S(2)}) async-start(), calls=%async_computation.9 | async-start | bytes 5308416 | tf_op jit(solution)/shard_map/reduce_scatter | solution.py:248
  27.7 30.5 %copy-start.49 = (f32[1536]{0:T(1024)}, f32[1536]{0:T(1024)S(1)}, u32[]{:S(2)}) copy-start(f32[1536]{0:T(1024)S(1)} %convert_element_type.206) | copy-start | bytes 18436
  47.3 11.0 copy-start.51
  49.4 18.2 %copy-start.18 = (f32[256,64]{1,0:T(8,128)}, f32[256,64]{1,0:T(8,128)S(1)}, u32[]{:S(2)}) copy-start(f32[256,64]{1,0:T(8,128)S(1)} %get-tuple-element.61) | copy-start | bytes 196612
  68.4 10.6 collective-permute-start
  77.2 22.4 %copy-start.31 = (f32[2,6,256]{2,1,0:T(8,128)}, f32[2,6,256]{2,1,0:T(8,128)S(1)}, u32[]{:S(2)}) copy-start(f32[2,6,256]{2,1,0:T(8,128)S(1)} %get-tuple-element.90) | copy-start | bytes 36868
  79.0 9.7 collective-permute-start.1
  81.3 16.7 %copy-start.29 = (f32[2,6,256]{2,1,0:T(8,128)}, f32[2,6,256]{2,1,0:T(8,128)S(1)}, u32[]{:S(2)}) copy-start(f32[2,6,256]{2,1,0:T(8,128)S(1)} %get-tuple-element.29) | copy-start | bytes 36868
  82.1 17.6 %copy-start.39 = (f32[2,6,256]{2,1,0:T(8,128)}, f32[2,6,256]{2,1,0:T(8,128)S(1)}, u32[]{:S(2)}) copy-start(f32[2,6,256]{2,1,0:T(8,128)S(1)} %fusion.19) | copy-start | bytes 36868
  83.1 18.2 %copy-start.14 = (f32[2,6,256,128]{2,3,1,0:T(8,128)}, f32[2,6,256,128]{2,3,1,0:T(8,128)S(1)}, u32[]{:S(2)}) copy-start(f32[2,6,256,128]{2,3,1,0:T(8,128)S(1)} %fusion.33) | copy-start | bytes 4718596
  85.1 16.2 %copy-start.15 = (f32[2,6,256,128]{2,3,1,0:T(8,128)}, f32[2,6,256,128]{2,3,1,0:T(8,128)S(1)}, u32[]{:S(2)}) copy-start(f32[2,6,256,128]{2,3,1,0:T(8,128)S(1)} %fusion.31) | copy-start | bytes 4718596
  85.1 12.3 copy-start.19
  85.9 13.8 copy-start.41
  88.7 11.6 copy-start.33
  88.7 8.7 collective-permute-start.2
  109.4 402.3 %copy-start.1 = (f32[256,1536]{1,0:T(8,128)}, f32[256,1536]{1,0:T(8,128)S(1)}, u32[]{:S(2)}) copy-start(f32[256,1536]{1,0:T(8,128)S(1)} %get-tuple-element.99) | copy-start | bytes 4718596
  551.4 120.0 %reduce-scatter.5.cloned.1.call-start = ((), (), s32[]{:S(2)}) async-start(), calls=%async_computation.8 | async-start | bytes 7077888 | tf_op jit(solution)/shard_map/reduce_scatter | solution.py:239
  558.0 12.9 collective-permute-start.3
  571.1 10.2 collective-permute-start.4
  581.3 9.3 collective-permute-start.5
  591.4 8.8 collective-permute-start.6
  607.1 237.1 %reduce-scatter.11.cloned.1.call-start = ((), (), s32[]{:S(2)}) async-start(), calls=%async_computation.11 | async-start | bytes 30965760 | tf_op jit(solution)/shard_map/reduce_scatter | solution.py:143
  625.3 532.9 %reduce-scatter.9.cloned.1.call-start = ((), (), s32[]{:S(2)}) async-start(), calls=%async_computation.10 | async-start | bytes 61931520 | tf_op jit(solution)/shard_map/reduce_scatter | solution.py:155
  651.6 910.0 %all-reduce.12.cloned.1.call-start = ((), (), s32[]{:S(2)}) async-start(), calls=%async_computation.12 | async-start | bytes 23396352 | tf_op jit(solution)/shard_map/psum | solution.py:259
  1159.9 16.6 %copy-start.50 = (f32[1536]{0:T(1024)S(1)}, f32[1536]{0:T(1024)}, u32[]{:S(2)}) copy-start(f32[1536]{0:T(1024)} %copy-done.49) | copy-start | bytes 18436
  1176.5 46.8 %copy-start.55 = (f32[256]{0:T(256)S(1)}, f32[256]{0:T(256)}, u32[]{:S(2)}) copy-start(f32[256]{0:T(256)} %get-tuple-element.63) | copy-start | bytes 3076
  (48 other events, 181.1 us)
Sparse Core Ops, SparseCore 0:
  9.9 48.3 all-gather.5
  60.2 38.9 all-gather.7
  101.0 251.9 all-gather.9
  354.7 135.2 all-gather.11
  551.6 53.8 reduce-scatter.6
  609.6 61.7 reduce-scatter.4
  675.0 169.1 reduce-scatter.10
  847.9 310.3 reduce-scatter.8
  1161.4 400.0 all-reduce.11
where the time goes:
time: 1590 us; the launch traced here: 1580 us
  waiting for transfers between devices  1240 us (78%)
  matrix products  190 us (12%)
  blocking collectives  61.9 us (4%)
  other arithmetic  51.1 us (3%)
  local copies, waits for them, and re-layouts  20.8 us (1%)
  between operations  18 us (1%)
    psum x1, waiting for transfers between devices, shards(): lax.psum(shard_qkv.astype(jnp.bfloat16), 'ctx').astype(jnp.float32)  335 us
    reduce_scatter x1, waiting for transfers between devices, shards(): lax.psum_scatter(lax.dot_general(picked, grad_mixed, (((0,), (0,)), ((),...  314 us
    all_gather x1, waiting for transfers between devices, shards(): lax.all_gather(w_gate_up, 'fsdp', axis=0, tiled=True)  243 us
    reduce_scatter x1, waiting for transfers between devices, shards(): lax.psum_scatter(lax.dot_general(picked, grad_low, (((0,), (0,)), ((), ()...  173 us
    all_gather x1, waiting for transfers between devices, shards(): lax.all_gather(w_down, 'fsdp', axis=0, tiled=True)  108 us
    dot_general x4, matrix products, against(): lax.dot_general(left, piece, (((1,), (1,)), ((), ())), preferred_element_...  58.1 us
    dot_general x2, matrix products, add_rows(): return jnp.dot(left, piece, preferred_element_type=jnp.float32)  45.7 us
    unnamed x2, blocking collectives  40.4 us
  transfers between devices with their start and end apart: 16, of which 13 were waited for; matrix products, arithmetic and copies ran while one was open for 11% of the time, Pallas kernels for 0%

commit v1 on v0

v1 whole, which is shorter than its diff:
```python
import functools

import jax
import jax.numpy as jnp
from jax import lax
from jax.experimental import pallas as pl
from jax.experimental.pallas import tpu as pltpu
from jax.sharding import PartitionSpec as P

HEADS = 12
KV_HEADS = 2
HEAD_DIM = 128
EPSILON = 1e-06
THETA = 1000000.0
MASKED = -1e30
BF = jnp.bfloat16
F32 = jnp.float32


def dot(a, b):
    return jnp.dot(a, b, preferred_element_type=F32)


def dot_bt(a, b):
    return lax.dot_general(a, b, (((1,), (1,)), ((), ())), preferred_element_type=F32)


def dot_at(a, b):
    return lax.dot_general(a, b, (((0,), (0,)), ((), ())), preferred_element_type=F32)


def angle_tables(places):
    half_dim = HEAD_DIM // 2
    freqs = THETA ** (-(jnp.arange(half_dim).astype(F32) * 2.0 / HEAD_DIM))
    angles = places.astype(F32)[:, None] * freqs[None, :]
    return (jnp.cos(angles), jnp.sin(angles))


def rotate(values_in, cosine, sine_table):
    half_dim = HEAD_DIM // 2
    shape = (cosine.shape[0],) + (1,) * (values_in.ndim - 2) + (half_dim,)
    cos_b = cosine.reshape(shape)
    sin_b = sine_table.reshape(shape)
    first = values_in[..., :half_dim]
    second = values_in[..., half_dim:]
    return jnp.concatenate([first * cos_b - second * sin_b, second * cos_b + first * sin_b], -1)


def flip(x, bit):
    n = lax.axis_size("fsdp")
    return lax.ppermute(x, "fsdp", [(i, i ^ bit) for i in range(n)])


def shift(x, distance):
    n = lax.axis_size("ctx")
    return lax.ppermute(x, "ctx", [(i, (i + distance) % n) for i in range(n)])


def place(pieces, index, total):
    rows = pieces[0][1].shape[0]
    out = jnp.zeros((total * rows,) + pieces[0][1].shape[1:], pieces[0][1].dtype)
    for block, piece in pieces:
        start = (block * rows,) + (0,) * (piece.ndim - 1)
        out = lax.dynamic_update_slice(out, piece, start)
    return out


def half_rows(rows):
    return -(-rows // 32) * 16


def plane_gather(shard):
    n = lax.axis_size("fsdp")
    me = lax.axis_index("fsdp")
    pieces = {0: shard}
    if n == 8:
        cut = half_rows(shard.shape[0])
        along_x, along_y = flip(shard, 2), flip(shard, 4)
        pieces[2], pieces[4] = along_x, along_y
        pieces[6] = jnp.concatenate([flip(along_x[:cut], 4), flip(along_y[cut:], 2)], 0)
    else:
        for k in range(2, n, 2):
            pieces[k] = flip(shard, k)
    for k in range(0, n, 2):
        pieces[k + 1] = flip(pieces[k], 1)
    return place([(me ^ k, piece) for k, piece in pieces.items()], me, n)


def plane_scatter(blocks):
    n = lax.axis_size("fsdp")
    me = lax.axis_index("fsdp")
    chip, core = me // 2, me % 2
    low = blocks.astype(BF).reshape((n // 2, 2) + blocks.shape[1:])
    kept = lax.dynamic_index_in_dim(low, core, 1, keepdims=False)
    given = lax.dynamic_index_in_dim(low, 1 - core, 1, keepdims=False)
    acc = (kept.astype(F32) + flip(given, 1).astype(F32)).astype(BF)

    def pick(k):
        return lax.dynamic_index_in_dim(acc, chip ^ k, 0, keepdims=False)

    if n == 8:
        rows = blocks.shape[1]
        cut = half_rows(rows) if rows > 1 else 0
        to_x, to_y, to_far = pick(1), pick(2), pick(3)
        if cut:
            first = flip(to_far[:cut], 2)
            from_x = [flip(to_x[:cut], 2)]
            second = flip(to_far[cut:], 4)
            from_y = [flip(to_y[cut:], 4)]
            from_x.append(flip((to_x[cut:].astype(F32) + second.astype(F32)).astype(BF), 2))
            from_y.insert(0, flip((to_y[:cut].astype(F32) + first.astype(F32)).astype(BF), 4))
            from_x, from_y = jnp.concatenate(from_x, 0), jnp.concatenate(from_y, 0)
            return pick(0).astype(F32) + from_x.astype(F32) + from_y.astype(F32)
    total = pick(0).astype(F32)
    for k in range(1, n // 2):
        total = total + flip(pick(k), 2 * k).astype(F32)
    return total


def ctx_gather(block):
    n = lax.axis_size("ctx")
    me = lax.axis_index("ctx")
    pieces = [(me, block)]
    for d in range(1, n):
        pieces.append(((me - d) % n, shift(block, d)))
    return place(pieces, me, n)


def ctx_chain(block):
    n = lax.axis_size("ctx")
    me = lax.axis_index("ctx")
    up, down = [block], [block]
    for t in range(1, n):
        up.append(lax.ppermute(up[-1], "ctx", [(i, i + 1) for i in range(t - 1, n - 1)]))
        down.append(lax.ppermute(down[-1], "ctx", [(i, i - 1) for i in range(1, n - t + 1)]))
    parts = []
    for j in range(n):
        part = block
        for i in range(n):
            if i != j:
                held = up[i - j] if i > j else down[j - i]
                part = jnp.where(me == i, held, part)
        parts.append(part)
    return parts


def ctx_scatter(blocks):
    n = lax.axis_size("ctx")
    me = lax.axis_index("ctx")
    total = lax.dynamic_index_in_dim(blocks, me, 0, keepdims=False).astype(F32)
    low = blocks.astype(BF)
    for d in range(1, n):
        part = lax.dynamic_index_in_dim(low, (me + d) % n, 0, keepdims=False)
        total = total + shift(part, d).astype(F32)
    return total


def ctx_sum(block):
    n = lax.axis_size("ctx")
    part = ctx_scatter(block.reshape((n, block.shape[0] // n) + block.shape[1:]))
    return ctx_gather(part.astype(BF)).astype(F32)


def lane_pad(n):
    return -(-n // 128) * 128


def pack_kernel(nz, nf, ff, wide, z_ref, w_ref, out_ref):
    unit = ff // (nf * nz)
    pad = wide - nf * unit
    for k in range(nz):

        @pl.when(z_ref[0] == k)
        def _():
            for h in range(2):
                for f in range(nf):
                    src = h * ff + f * (ff // nf) + k * unit
                    dst = h * wide + f * unit
                    out_ref[:, dst : dst + unit] = w_ref[:, src : src + unit]
                if pad:
                    out_ref[:, (h + 1) * wide - pad : (h + 1) * wide] = jnp.zeros(
                        (out_ref.shape[0], pad), out_ref.dtype
                    )


def pack(w, nz, nf, z):
    rows, ff = w.shape[0], w.shape[1] // 2
    wide = lane_pad(ff // nz)
    step = 32
    return pl.pallas_call(
        functools.partial(pack_kernel, nz, nf, ff, wide),
        grid=(rows // step,),
        in_specs=[
            pl.BlockSpec(memory_space=pltpu.SMEM),
            pl.BlockSpec((step, 2 * ff), lambda i: (i, 0)),
        ],
        out_specs=pl.BlockSpec((step, 2 * wide), lambda i: (i, 0)),
        out_shape=jax.ShapeDtypeStruct((rows, 2 * wide), w.dtype),
    )(z.reshape(1).astype(jnp.int32), w)


def unpack_kernel(nz, nf, ff, wide, *refs):
    unit = ff // (nf * nz)
    out_ref = refs[-1]
    for k in range(nz):
        for h in range(2):
            for f in range(nf):
                src = h * wide + f * unit
                dst = h * ff + f * (ff // nf) + k * unit
                out_ref[:, dst : dst + unit] = refs[k][:, src : src + unit].astype(F32)


def unpack(parts, nz, nf, ff):
    rows, wide = parts[0].shape[0], parts[0].shape[1] // 2
    step = 32
    return pl.pallas_call(
        functools.partial(unpack_kernel, nz, nf, ff, wide),
        grid=(rows // step,),
        in_specs=[pl.BlockSpec((step, 2 * wide), lambda i: (i, 0))] * nz,
        out_specs=pl.BlockSpec((step, 2 * ff), lambda i: (i, 0)),
        out_shape=jax.ShapeDtypeStruct((rows, 2 * ff), F32),
    )(*parts)


def shards(
    hidden_in, w_qkv, b_qkv, w_out, w_gate_up, w_down, gain_attn, gain_mlp, block_order, cotangent
):
    nz, nf = lax.axis_size("ctx"), lax.axis_size("fsdp")
    z, me = lax.axis_index("ctx"), lax.axis_index("fsdp")
    groups = HEADS // KV_HEADS
    q_width, k_width = HEADS * HEAD_DIM, KV_HEADS * HEAD_DIM
    rows = hidden_in.shape[1]
    piece_len = rows // 2
    ff = w_gate_up.shape[1] // 2
    unit = ff // (nf * nz)
    quarter = ff // nz
    wide = lane_pad(quarter)
    scale = HEAD_DIM ** (-0.5)
    order_row = block_order[0]
    all_places = (
        order_row[:, None] * piece_len + jnp.arange(piece_len, dtype=jnp.int32)[None, :]
    ).reshape(-1)
    my_places = lax.dynamic_slice_in_dim(all_places, z * rows, rows)
    visible = all_places[None, :] <= my_places[:, None]
    cosine, sine_table = angle_tables(my_places)

    whole_qkv = plane_gather(w_qkv)
    small = jnp.concatenate([b_qkv, gain_attn, gain_mlp]).reshape(1, -1)
    smalls = plane_gather(small)
    nb, ng = b_qkv.shape[0], gain_attn.shape[0]
    bias = smalls[:, :nb].reshape(-1).astype(F32)
    gain_first = smalls[:, nb : nb + ng].reshape(-1).astype(F32)
    gain_second = smalls[:, nb + ng :].reshape(-1).astype(F32)

    packed = pack(w_gate_up, nz, nf, z)
    down_mine = lax.dynamic_slice_in_dim(w_down, z * unit, unit)
    packed, down_mine, w_out, whole_qkv = lax.optimization_barrier(
        (packed, down_mine, w_out, whole_qkv)
    )
    whole_out = plane_gather(w_out)
    gu = plane_gather(packed)
    down = jnp.pad(plane_gather(down_mine), ((0, wide - quarter), (0, 0)))
    grad_low = cotangent[0]
    grad_all = ctx_gather(grad_low)

    inputs = hidden_in[0].astype(F32)
    inverse_one = lax.rsqrt(jnp.mean(inputs * inputs, -1, keepdims=True) + EPSILON)
    normed = (inputs * inverse_one * gain_first).astype(BF)
    projected = dot(normed, whole_qkv) + bias
    queries = rotate(
        projected[:, :q_width].reshape(rows, KV_HEADS, groups, HEAD_DIM), cosine, sine_table
    ).astype(BF)
    keys = rotate(
        projected[:, q_width : q_width + k_width].reshape(rows, KV_HEADS, HEAD_DIM),
        cosine,
        sine_table,
    ).astype(BF)
    kv = jnp.concatenate(
        [keys.reshape(rows, k_width), projected[:, q_width + k_width :].astype(BF)], 1
    )
    kv_all = ctx_gather(kv)
    keys_all = kv_all[:, :k_width].reshape(-1, KV_HEADS, HEAD_DIM)
    values_all = kv_all[:, k_width:].reshape(-1, KV_HEADS, HEAD_DIM)
    scores = jnp.einsum("qkgd,tkd->kgqt", queries, keys_all, preferred_element_type=F32) * scale
    scores = jnp.where(visible, scores, MASKED)
    row_top = jnp.max(scores, -1, keepdims=True)
    weights = jnp.exp(scores - row_top)
    row_total = jnp.sum(weights, -1, keepdims=True)
    attn_heads = (
        jnp.einsum("kgqt,tkd->kgqd", weights.astype(BF), values_all, preferred_element_type=F32)
        / row_total
    )
    log_total = row_top + jnp.log(row_total)
    attn_low = attn_heads.transpose(2, 0, 1, 3).reshape(rows, q_width).astype(BF)
    middle = inputs + dot(attn_low, whole_out)
    inverse_two = lax.rsqrt(jnp.mean(middle * middle, -1, keepdims=True) + EPSILON)
    normed_two = (middle * inverse_two * gain_second).astype(BF)

    x_all = ctx_gather(normed_two)
    gate = dot(x_all, gu[:, :wide])
    up = dot(x_all, gu[:, wide:])
    sigmoid_gate = jax.nn.sigmoid(gate)
    act = (gate * sigmoid_gate * up).astype(BF)
    grad_act = dot_bt(grad_all, down)
    grad_gate = grad_act * up * (sigmoid_gate * (1.0 + gate * (1.0 - sigmoid_gate)))
    grad_up = grad_act * gate * sigmoid_gate
    grad_mixed = jnp.concatenate([grad_gate, grad_up], 1).astype(BF)
    grad_normed_two = ctx_scatter(dot_bt(grad_mixed, gu).reshape(nz, rows, -1))
    down_sum = ctx_scatter(dot(act, down).reshape(nz, rows, -1))
    hidden_out = (middle + down_sum).astype(BF)[None]

    down_local = dot_at(act, grad_all)[:quarter].reshape(nf, unit, -1)
    gate_up_local = dot_at(x_all, grad_mixed).reshape(nf, -1, 2 * wide)
    grad_down = jnp.concatenate(ctx_chain(plane_scatter(down_local).astype(BF)), 0).astype(F32)
    grad_gate_up = unpack(ctx_chain(plane_scatter(gate_up_local).astype(BF)), nz, nf, ff)

    grad_full = grad_low.astype(F32)
    scaled_two = gain_second * grad_normed_two
    gain_two_local = jnp.sum(grad_normed_two * middle * inverse_two, 0)
    grad_middle = (
        grad_full
        + inverse_two * scaled_two
        - middle
        * (inverse_two * inverse_two * inverse_two)
        * jnp.mean(scaled_two * middle, -1, keepdims=True)
    )
    grad_branch = grad_middle.astype(BF)
    out_local = dot_at(attn_low, grad_branch)
    grad_out = ctx_sum(plane_scatter(out_local.reshape(nf, -1, out_local.shape[1])))
    grad_attn = dot_bt(grad_branch, whole_out).astype(BF)
    grad_heads = grad_attn.reshape(rows, KV_HEADS, groups, HEAD_DIM).transpose(1, 2, 0, 3)
    row_delta = jnp.sum(grad_heads.astype(F32) * attn_heads, -1, keepdims=True)
    scores = jnp.einsum("qkgd,tkd->kgqt", queries, keys_all, preferred_element_type=F32) * scale
    probs = jnp.where(visible, jnp.exp(scores - log_total), 0.0)
    grad_values = jnp.einsum(
        "kgqt,kgqd->tkd", probs.astype(BF), grad_heads, preferred_element_type=F32
    )
    grad_probs = jnp.einsum("kgqd,tkd->kgqt", grad_heads, values_all, preferred_element_type=F32)
    grad_scores = (probs * (grad_probs - row_delta)).astype(BF)
    grad_queries = (
        jnp.einsum("kgqt,tkd->kgqd", grad_scores, keys_all, preferred_element_type=F32) * scale
    )
    grad_keys = (
        jnp.einsum("kgqt,qkgd->tkd", grad_scores, queries, preferred_element_type=F32) * scale
    )
    kv_grads = jnp.concatenate(
        [grad_keys.reshape(nz, rows, k_width), grad_values.reshape(nz, rows, k_width)], -1
    )
    kv_grad = ctx_scatter(kv_grads)
    query_back = rotate(grad_queries.transpose(2, 0, 1, 3), cosine, -sine_table).reshape(
        rows, q_width
    )
    key_back = rotate(
        kv_grad[:, :k_width].reshape(rows, KV_HEADS, HEAD_DIM), cosine, -sine_table
    ).reshape(rows, k_width)
    grad_projected = jnp.concatenate([query_back, key_back, kv_grad[:, k_width:]], 1).astype(BF)
    bias_local = jnp.sum(grad_projected.astype(F32), 0)
    qkv_local = dot_at(normed, grad_projected)
    grad_qkv = ctx_sum(plane_scatter(qkv_local.reshape(nf, -1, qkv_local.shape[1])))
    grad_normed = dot_bt(grad_projected, whole_qkv)
    scaled_one = gain_first * grad_normed
    gain_one_local = jnp.sum(grad_normed * inputs * inverse_one, 0)
    grad_inputs = (
        grad_middle
        + inverse_one * scaled_one
        - inputs
        * (inverse_one * inverse_one * inverse_one)
        * jnp.mean(scaled_one * inputs, -1, keepdims=True)
    )
    cut = q_width + k_width
    tiny = jnp.concatenate(
        [
            bias_local[:cut].reshape(nf, -1),
            bias_local[cut:].reshape(nf, -1),
            gain_one_local.reshape(nf, -1),
            gain_two_local.reshape(nf, -1),
        ],
        1,
    ).reshape(nf, 1, -1)
    tiny = plane_scatter(tiny).reshape(nz, -1)
    tiny = ctx_sum(tiny).reshape(-1)
    e1 = cut // nf
    e2 = e1 + k_width // nf
    e3 = e2 + ng
    return (
        hidden_out,
        grad_inputs.astype(BF)[None],
        grad_qkv,
        tiny[:e1],
        tiny[e1:e2],
        grad_out,
        grad_gate_up,
        grad_down,
        tiny[e2:e3],
        tiny[e3:],
    )


def solution(mesh):
    placed = (
        P("fsdp", "ctx", None),
        P("fsdp", None),
        P("fsdp"),
        P("fsdp", None),
        P("fsdp", None),
        P("fsdp", None),
        P("fsdp"),
        P("fsdp"),
        P("fsdp", None),
        P("fsdp", "ctx", None),
    )
    return jax.shard_map(
        shards,
        mesh=mesh,
        in_specs=placed,
        out_specs=(
            P("fsdp", "ctx", None),
            P("fsdp", "ctx", None),
            P("fsdp", None),
            P("fsdp"),
            P("fsdp"),
            P("fsdp", None),
            P("fsdp", None),
            P("fsdp", None),
            P("fsdp"),
            P("fsdp"),
        ),
        check_vma=False,
    )
```

time: 1590 us -> 1020 us (0.64)
  waiting for transfers between devices: 1240 us -> 439 us
  starting transfers between devices: 5.88 us -> 164 us
  local copies, waits for them, and re-layouts: 20.8 us -> 168 us
  blocking collectives: 61.9 us -> 0 us
  matrix products: 190 us -> 157 us
  other arithmetic: 51.1 us -> 68.2 us
    reduce_scatter x4 -> x0, waiting for transfers between devices: 506 us -> none  [the longest x1 314 us: shards(): lax.psum_scatter(lax.dot_general(picked, grad_mixed, (((0,), (0,)), ((),...]
    ppermute x7 -> x119, waiting for transfers between devices: 33.1 us -> 439 us  [the longest x36 287 us: shift(): return lax.ppermute(x, 'ctx', [(i, (i + distance) % n) for i in range(n)])]
    all_gather x4 -> x0, waiting for transfers between devices: 359 us -> none  [the longest x1 243 us: shards(): lax.all_gather(w_gate_up, 'fsdp', axis=0, tiled=True)]
    psum x1 -> x0, waiting for transfers between devices: 335 us -> none  [shards(): lax.psum(shard_qkv.astype(jnp.bfloat16), 'ctx').astype(jnp.float32)]
    ppermute x7 -> x119, starting transfers between devices: 5.27 us -> 164 us  [the longest x36 86.1 us: shift(): return lax.ppermute(x, 'ctx', [(i, (i + distance) % n) for i in range(n)])]
    dynamic_update_slice x0 -> x61, local copies, waits for them, and re-layouts: none -> 55.6 us  [place(): out = lax.dynamic_update_slice(out, piece, start)]
    unnamed x2 -> x0, blocking collectives: 40.4 us -> none
    dot_general x32 -> x18, matrix products: 188 us -> 154 us  [the longest x5 46.9 us: dot(): return jnp.dot(a, b, preferred_element_type=F32)]
  transfers between devices with their start and end apart: 16 -> 119, of which waited for: 13 -> 45; matrix products, arithmetic and copies ran while one was open for 11% -> 29% of each run, Pallas kernels for 0% -> 1%
where the time goes in v1:
time: 1020 us; the launch traced here: 1010 us
  waiting for transfers between devices  439 us (43%)
  local copies, waits for them, and re-layouts  168 us (16%)
  starting transfers between devices  164 us (16%)
  matrix products  157 us (15%)
  other arithmetic  68.2 us (7%)
  Pallas kernels  15.8 us (2%)
    ppermute x36, waiting for transfers between devices, shift(): return lax.ppermute(x, 'ctx', [(i, (i + distance) % n) for i in range(n)])  287 us
    ppermute x71, waiting for transfers between devices, flip(): return lax.ppermute(x, 'fsdp', [(i, i ^ bit) for i in range(n)])  131 us
    ppermute x36, starting transfers between devices, shift(): return lax.ppermute(x, 'ctx', [(i, (i + distance) % n) for i in range(n)])  86.1 us
    ppermute x71, starting transfers between devices, flip(): return lax.ppermute(x, 'fsdp', [(i, i ^ bit) for i in range(n)])  60.2 us
    dynamic_update_slice x61, local copies, waits for them, and re-layouts, place(): out = lax.dynamic_update_slice(out, piece, start)  55.6 us
    dot_general x5, matrix products, dot(): return jnp.dot(a, b, preferred_element_type=F32)  46.9 us
    dot_general x4, matrix products, dot_bt(): lax.dot_general(a, b, (((1,), (1,)), ((), ())), preferred_element_type=F32)  42.6 us
    dot_general x4, matrix products, dot_at(): lax.dot_general(a, b, (((0,), (0,)), ((), ())), preferred_element_type=F32)  35.9 us
  transfers between devices with their start and end apart: 119, of which 45 were waited for; matrix products, arithmetic and copies ran while one was open for 29% of the time, Pallas kernels for 1%

profile of v1, /device:TPU:0, one launch (start us, length us, event | category | flops | bytes accessed | tf_op | source)
XLA Modules:
  0.0 1013.8 jit_solution(3523992702147143319)
XLA Ops:
  50.3 9.6 collective-permute-done.49
  62.0 14.4 %collective-permute-done.50 = bf16[256,1536]{1,0:T(8,128)(2,1)} collective-permute-done((bf16[256,1536]{1,0:T(8,128)(2,1)S(1)}, bf16[256,1536]{1,0:T(8,128)(2,1)}, u32[]{:S(2)}, u32[]{:S(2)}) %collective-permute-start.50) | collective-permute-done | bytes 786464 | tf_op jit(solution)/shard_map/ppermute | solution.py:56
  171.3 31.8 %collective-permute-done.20 = bf16[96,1536]{1,0:T(8,128)(2,1)S(1)} collective-permute-done((bf16[96,1536]{1,0:T(8,128)(2,1)S(1)}, bf16[96,1536]{1,0:T(8,128)(2,1)S(1)}, u32[]{:S(2)}, u32[]{:S(2)}) %collective-permute-start.20) | collective-permute-done | bytes 294944 | tf_op jit(solution)/shard_map/ppermute | solution.py:51
  210.4 8.8 collective-permute-done.39
  240.8 13.8 %fusion.12 = f32[1024,2304]{1,0:T(8,128)} fusion(bf16[1024,1536]{1,0:T(8,128)(2,1)} %constant_dynamic-update-slice_fusion.8, bf16[2240,1536]{1,0:T(8,128)(2,1)} %constant_dynamic-update-slice_fusion.12), kind=kOutput, calls=%fused_computation.26 | convolution fusion | flops 7247757312 | bytes 19464192 | tf_op jit(solution)/shard_map/dot_general | solution.py:25
  259.4 29.2 %collective-permute-done.27 = bf16[256,1536]{1,0:T(8,128)(2,1)} collective-permute-done((bf16[256,1536]{1,0:T(8,128)(2,1)}, bf16[256,1536]{1,0:T(8,128)(2,1)}, u32[]{:S(2)}, u32[]{:S(2)}) %collective-permute-start.27) | collective-permute-done | bytes 786464 | tf_op jit(solution)/shard_map/ppermute | solution.py:56
  303.4 9.9 fusion.7
  313.3 18.8 %multiply_convert_fusion.2 = (bf16[1024,2304]{1,0:T(8,128)(2,1)}, bf16[1024,2304]{1,0:T(8,128)(2,1)}, bf16[1024,2304]{1,0:T(8,128)(2,1)}) fusion(f32[1024,2304]{1,0:T(8,128)} %fusion.12, f32[1024,2304]{1,0:T(8,128)} %fusion.7, bf16[1024,1536]{1,0:T(8,128)(2,1)S(1)} %copy-done.29, bf16[1536,4608]{1,0:T(8,128)(2,1)} %copy-done.9), kind=kOutput, calls=%fused_computation.16 | convolution fusion | flops 7285506048 | bytes 43253760 | tf_op jit(solution)/shard_map/dot_general | solution.py:21
  332.1 19.0 %fusion.23 = f32[1024,1536]{1,0:T(8,128)S(1)} fusion(bf16[1536,4608]{1,0:T(8,128)(2,1)} %copy-done.9, bf16[1024,2304]{1,0:T(8,128)(2,1)} %get-tuple-element.37, bf16[1024,2304]{1,0:T(8,128)(2,1)} %get-tuple-element.35), kind=kOutput, calls=%fused_computation.36 | convolution fusion | flops 14514388992 | bytes 29884416 | tf_op jit(solution)/shard_map/dot_general | solution.py:25
  351.1 21.2 %convolution_convert_fusion = bf16[1536,4608]{1,0:T(8,128)(2,1)} fusion(bf16[1024,1536]{1,0:T(8,128)(2,1)S(1)} %copy-done.29, bf16[1024,2304]{1,0:T(8,128)(2,1)} %get-tuple-element.37, bf16[1024,2304]{1,0:T(8,128)(2,1)} %get-tuple-element.35), kind=kOutput, calls=%fused_computation | convolution fusion | flops 14521466880 | bytes 26738688 | tf_op jit(solution)/shard_map/dot_general | solution.py:29
  373.8 17.6 %collective-permute-start.53 = (bf16[256,1536]{1,0:T(8,128)(2,1)S(1)}, bf16[256,1536]{1,0:T(8,128)(2,1)S(1)}, u32[]{:S(2)}, u32[]{:S(2)}) collective-permute-start(bf16[256,1536]{1,0:T(8,128)(2,1)S(1)} %get-tuple-element.61), channel_id=1, source_target_pairs={{0,24},{8,0},{16,8},{24,16},{1,25},{9,1},{17,9},{25,17},{2,26},{10... | collective-permute-start | bytes 2359304 | tf_op jit(solution)/shard_map/ppermute | solution.py:56
  391.4 11.5 %fusion.119 = bf16[2304,1536]{1,0:T(8,128)(2,1)} fusion(bf16[1024,2304]{1,0:T(8,128)(2,1)S(1)} %copy-done.60, bf16[1024,1536]{1,0:T(8,128)(2,1)} %constant_dynamic-update-slice_fusion.8), kind=kOutput, calls=%fused_computation.333 | convolution fusion | flops 7247757312 | bytes 14942208 | tf_op jit(solution)/shard_map/dot_general | solution.py:29
  402.9 9.7 fusion.14
  431.8 34.7 %collective-permute-done.52 = bf16[256,1536]{1,0:T(8,128)(2,1)S(1)} collective-permute-done((bf16[256,1536]{1,0:T(8,128)(2,1)}, bf16[256,1536]{1,0:T(8,128)(2,1)S(1)}, u32[]{:S(2)}, u32[]{:S(2)}) %collective-permute-start.52) | collective-permute-done | bytes 786464 | tf_op jit(solution)/shard_map/ppermute | solution.py:56
  469.5 63.9 %collective-permute-done.46 = bf16[256,1536]{1,0:T(8,128)(2,1)S(1)} collective-permute-done((bf16[256,1536]{1,0:T(8,128)(2,1)S(1)}, bf16[256,1536]{1,0:T(8,128)(2,1)S(1)}, u32[]{:S(2)}, u32[]{:S(2)}) %collective-permute-start.46) | collective-permute-done | bytes 786464 | tf_op jit(solution)/shard_map/ppermute | solution.py:56
  544.1 8.3 fusion.47
  552.4 7.4 multiply_convert_fusion
  605.9 8.9 collective-permute-done.55
  694.7 9.8 fusion
  716.4 8.6 collective-permute-done.97
  742.2 17.0 %collective-permute-done.94 = bf16[96,4608]{1,0:T(8,128)(2,1)S(1)} collective-permute-done((bf16[96,4608]{1,0:T(8,128)(2,1)S(1)}, bf16[96,4608]{1,0:T(8,128)(2,1)S(1)}, u32[]{:S(2)}, u32[]{:S(2)}) %collective-permute-start.94) | collective-permute-done | bytes 884768 | tf_op jit(solution)/shard_map/ppermute | solution.py:51
  762.6 15.5 %collective-permute-done.96 = bf16[96,4608]{1,0:T(8,128)(2,1)S(1)} collective-permute-done((bf16[96,4608]{1,0:T(8,128)(2,1)S(1)}, bf16[96,4608]{1,0:T(8,128)(2,1)S(1)}, u32[]{:S(2)}, u32[]{:S(2)}) %collective-permute-start.96) | collective-permute-done | bytes 884768 | tf_op jit(solution)/shard_map/ppermute | solution.py:51
  795.4 7.5 collective-permute-done.63
  813.6 23.7 %collective-permute-done.90 = bf16[48,1536]{1,0:T(8,128)(2,1)S(1)} collective-permute-done((bf16[48,1536]{1,0:T(8,128)(2,1)S(1)}, bf16[48,1536]{1,0:T(8,128)(2,1)S(1)}, u32[]{:S(2)}, u32[]{:S(2)}) %collective-permute-start.90) | collective-permute-done | bytes 147488 | tf_op jit(solution)/shard_map/ppermute | solution.py:56
  839.3 14.7 %collective-permute-done.91 = bf16[48,1536]{1,0:T(8,128)(2,1)S(1)} collective-permute-done((bf16[48,1536]{1,0:T(8,128)(2,1)S(1)}, bf16[48,1536]{1,0:T(8,128)(2,1)S(1)}, u32[]{:S(2)}, u32[]{:S(2)}) %collective-permute-start.91) | collective-permute-done | bytes 147488 | tf_op jit(solution)/shard_map/ppermute | solution.py:56
  854.0 10.5 %collective-permute-start.66 = (bf16[48,2048]{1,0:T(8,128)(2,1)S(1)}, bf16[48,2048]{1,0:T(8,128)(2,1)S(1)}, u32[]{:S(2)}, u32[]{:S(2)}) collective-permute-start(bf16[48,2048]{1,0:T(8,128)(2,1)S(1)} %get-tuple-element.90), channel_id=1, source_target_pairs={{0,24},{8,0},{16,8},{24,16},{1,25},{9,1},{17,9},{25,17},{2,26},{10... | collective-permute-start | bytes 589832 | tf_op jit(solution)/shard_map/ppermute | solution.py:56
  870.8 41.1 %collective-permute-done.65 = bf16[48,2048]{1,0:T(8,128)(2,1)S(1)} collective-permute-done((bf16[48,2048]{1,0:T(8,128)(2,1)S(1)}, bf16[48,2048]{1,0:T(8,128)(2,1)S(1)}, u32[]{:S(2)}, u32[]{:S(2)}) %collective-permute-start.65) | collective-permute-done | bytes 196640 | tf_op jit(solution)/shard_map/ppermute | solution.py:56
  927.6 11.6 %collective-permute-done.92 = bf16[48,1536]{1,0:T(8,128)(2,1)S(1)} collective-permute-done((bf16[48,1536]{1,0:T(8,128)(2,1)S(1)}, bf16[48,1536]{1,0:T(8,128)(2,1)S(1)}, u32[]{:S(2)}, u32[]{:S(2)}) %collective-permute-start.92) | collective-permute-done | bytes 147488 | tf_op jit(solution)/shard_map/ppermute | solution.py:56
  950.3 7.1 collective-permute-done.68
  960.6 13.5 %collective-permute-done.69 = bf16[48,2048]{1,0:T(8,128)(2,1)S(1)} collective-permute-done((bf16[48,2048]{1,0:T(8,128)(2,1)S(1)}, bf16[48,2048]{1,0:T(8,128)(2,1)S(1)}, u32[]{:S(2)}, u32[]{:S(2)}) %collective-permute-start.69) | collective-permute-done | bytes 196640 | tf_op jit(solution)/shard_map/ppermute | solution.py:56
  979.0 21.4 %collective-permute-done.105 = bf16[192,4608]{1,0:T(8,128)(2,1)S(1)} collective-permute-done((bf16[192,4608]{1,0:T(8,128)(2,1)S(1)}, bf16[192,4608]{1,0:T(8,128)(2,1)S(1)}, u32[]{:S(2)}, u32[]{:S(2)}) %collective-permute-start.105) | collective-permute-done | bytes 1769504 | tf_op jit(solution)/shard_map/ppermute | solution.py:135
  1003.8 9.6 shard_map.178
  (580 shorter events, 460.9 us)
Async XLA Ops:
  0.7 42.3 %collective-permute-start.7 = (bf16[192,2048]{1,0:T(8,128)(2,1)}, bf16[192,2048]{1,0:T(8,128)(2,1)}, u32[]{:S(2)}, u32[]{:S(2)}) collective-permute-start(bf16[192,2048]{1,0:T(8,128)(2,1)} %param.11), channel_id=1, source_target_pairs={{0,2},{1,3},{2,0},{3,1},{4,6},{5,7},{6,4},{7,5},{8,10},{9,11},{10,... | collective-permute-start | bytes 2359304 | tf_op jit(solution)/shard_map/ppermute | solution.py:51
  6.8 53.2 %collective-permute-start.49 = (bf16[256,1536]{1,0:T(8,128)(2,1)}, bf16[256,1536]{1,0:T(8,128)(2,1)}, u32[]{:S(2)}, u32[]{:S(2)}) collective-permute-start(bf16[256,1536]{1,0:T(8,128)(2,1)} %bitcast.408), channel_id=1, source_target_pairs={{0,16},{8,24},{16,0},{24,8},{1,17},{9,25},{17,1},{25,9},{2,18},{10... | collective-permute-start | bytes 2359304 | tf_op jit(solution)/shard_map/ppermute | solution.py:56
  102.8 52.3 %collective-permute-start.18 = (bf16[192,1536]{1,0:T(8,128)(2,1)}, bf16[192,1536]{1,0:T(8,128)(2,1)}, u32[]{:S(2)}, u32[]{:S(2)}) collective-permute-start(bf16[192,1536]{1,0:T(8,128)(2,1)} %param.13), channel_id=1, source_target_pairs={{0,2},{1,3},{2,0},{3,1},{4,6},{5,7},{6,4},{7,5},{8,10},{9,11},{10,... | collective-permute-start | bytes 1769480 | tf_op jit(solution)/shard_map/ppermute | solution.py:51
  103.3 53.2 %collective-permute-start.19 = (bf16[192,1536]{1,0:T(8,128)(2,1)}, bf16[192,1536]{1,0:T(8,128)(2,1)}, u32[]{:S(2)}, u32[]{:S(2)}) collective-permute-start(bf16[192,1536]{1,0:T(8,128)(2,1)} %param.13), channel_id=1, source_target_pairs={{0,4},{1,5},{2,6},{3,7},{4,0},{5,1},{6,2},{7,3},{8,12},{9,13},{10,... | collective-permute-start | bytes 1769480 | tf_op jit(solution)/shard_map/ppermute | solution.py:51
  126.2 78.4 %collective-permute-start.22 = (bf16[192,1536]{1,0:T(8,128)(2,1)}, bf16[192,1536]{1,0:T(8,128)(2,1)}, u32[]{:S(2)}, u32[]{:S(2)}) collective-permute-start(bf16[192,1536]{1,0:T(8,128)(2,1)} %param.13), channel_id=1, source_target_pairs={{0,1},{1,0},{2,3},{3,2},{4,5},{5,4},{6,7},{7,6},{8,9},{9,8},{10,11... | collective-permute-start | bytes 1769480 | tf_op jit(solution)/shard_map/ppermute | solution.py:51
  155.0 81.1 %collective-permute-start.29 = (bf16[192,4608]{1,0:T(8,128)(2,1)S(1)}, bf16[192,4608]{1,0:T(8,128)(2,1)S(1)}, u32[]{:S(2)}, u32[]{:S(2)}) collective-permute-start(bf16[192,4608]{1,0:T(8,128)(2,1)S(1)} %copy-done.15), channel_id=1, source_target_pairs={{0,2},{1,3},{2,0},{3,1},{4,6},{5,7},{6,4},{7,5},{8,10},{9,11},{10,... | collective-permute-start | bytes 5308424 | tf_op jit(solution)/shard_map/ppermute | solution.py:51
  156.6 79.9 %collective-permute-start.30 = (bf16[192,4608]{1,0:T(8,128)(2,1)S(1)}, bf16[192,4608]{1,0:T(8,128)(2,1)S(1)}, u32[]{:S(2)}, u32[]{:S(2)}) collective-permute-start(bf16[192,4608]{1,0:T(8,128)(2,1)S(1)} %copy-done.15), channel_id=1, source_target_pairs={{0,4},{1,5},{2,6},{3,7},{4,0},{5,1},{6,2},{7,3},{8,12},{9,13},{10,... | collective-permute-start | bytes 5308424 | tf_op jit(solution)/shard_map/ppermute | solution.py:51
  219.2 75.6 %collective-permute-start.33 = (bf16[192,4608]{1,0:T(8,128)(2,1)S(1)}, bf16[192,4608]{1,0:T(8,128)(2,1)}, u32[]{:S(2)}, u32[]{:S(2)}) collective-permute-start(bf16[192,4608]{1,0:T(8,128)(2,1)S(1)} %copy-done.15), channel_id=1, source_target_pairs={{0,1},{1,0},{2,3},{3,2},{4,5},{5,4},{6,7},{7,6},{8,9},{9,8},{10,11... | collective-permute-start | bytes 5308424 | tf_op jit(solution)/shard_map/ppermute | solution.py:51
  236.1 52.4 %collective-permute-start.27 = (bf16[256,1536]{1,0:T(8,128)(2,1)}, bf16[256,1536]{1,0:T(8,128)(2,1)}, u32[]{:S(2)}, u32[]{:S(2)}) collective-permute-start(bf16[256,1536]{1,0:T(8,128)(2,1)} %get-tuple-element.32), channel_id=1, source_target_pairs={{0,16},{8,24},{16,0},{24,8},{1,17},{9,25},{17,1},{25,9},{2,18},{10... | collective-permute-start | bytes 2359304 | tf_op jit(solution)/shard_map/ppermute | solution.py:56
  236.5 54.1 %collective-permute-start.28 = (bf16[256,1536]{1,0:T(8,128)(2,1)}, bf16[256,1536]{1,0:T(8,128)(2,1)}, u32[]{:S(2)}, u32[]{:S(2)}) collective-permute-start(bf16[256,1536]{1,0:T(8,128)(2,1)} %get-tuple-element.32), channel_id=1, source_target_pairs={{0,24},{8,0},{16,8},{24,16},{1,25},{9,1},{17,9},{25,17},{2,26},{10... | collective-permute-start | bytes 2359304 | tf_op jit(solution)/shard_map/ppermute | solution.py:56
  239.3 54.0 %collective-permute-start.31 = (bf16[96,4608]{1,0:T(8,128)(2,1)S(1)}, bf16[96,4608]{1,0:T(8,128)(2,1)}, u32[]{:S(2)}, u32[]{:S(2)}) collective-permute-start(bf16[96,4608]{1,0:T(8,128)(2,1)S(1)} %slice.337), channel_id=1, source_target_pairs={{0,4},{1,5},{2,6},{3,7},{4,0},{5,1},{6,2},{7,3},{8,12},{9,13},{10,... | collective-permute-start | bytes 2654216 | tf_op jit(solution)/shard_map/ppermute | solution.py:51
  373.8 45.3 %collective-permute-start.53 = (bf16[256,1536]{1,0:T(8,128)(2,1)S(1)}, bf16[256,1536]{1,0:T(8,128)(2,1)S(1)}, u32[]{:S(2)}, u32[]{:S(2)}) collective-permute-start(bf16[256,1536]{1,0:T(8,128)(2,1)S(1)} %get-tuple-element.61), channel_id=1, source_target_pairs={{0,24},{8,0},{16,8},{24,16},{1,25},{9,1},{17,9},{25,17},{2,26},{10... | collective-permute-start | bytes 2359304 | tf_op jit(solution)/shard_map/ppermute | solution.py:56
  412.6 54.0 %collective-permute-start.52 = (bf16[256,1536]{1,0:T(8,128)(2,1)}, bf16[256,1536]{1,0:T(8,128)(2,1)S(1)}, u32[]{:S(2)}, u32[]{:S(2)}) collective-permute-start(bf16[256,1536]{1,0:T(8,128)(2,1)} %get-tuple-element.62), channel_id=1, source_target_pairs={{0,16},{8,24},{16,0},{24,8},{1,17},{9,25},{17,1},{25,9},{2,18},{10... | collective-permute-start | bytes 2359304 | tf_op jit(solution)/shard_map/ppermute | solution.py:56
  412.7 53.9 %collective-permute-start.51 = (bf16[256,1536]{1,0:T(8,128)(2,1)S(1)}, bf16[256,1536]{1,0:T(8,128)(2,1)S(1)}, u32[]{:S(2)}, u32[]{:S(2)}) collective-permute-start(bf16[256,1536]{1,0:T(8,128)(2,1)S(1)} %get-tuple-element.60), channel_id=1, source_target_pairs={{0,8},{8,16},{16,24},{24,0},{1,9},{9,17},{17,25},{25,1},{2,10},{10... | collective-permute-start | bytes 2359304 | tf_op jit(solution)/shard_map/ppermute | solution.py:56
  416.4 53.1 %collective-permute-start.47 = (bf16[256,1536]{1,0:T(8,128)(2,1)}, bf16[256,1536]{1,0:T(8,128)(2,1)S(1)}, u32[]{:S(2)}, u32[]{:S(2)}) collective-permute-start(bf16[256,1536]{1,0:T(8,128)(2,1)} %get-tuple-element.64), channel_id=1, source_target_pairs={{0,24},{8,0},{16,8},{24,16},{1,25},{9,1},{17,9},{25,17},{2,26},{10... | collective-permute-start | bytes 2359304 | tf_op jit(solution)/shard_map/ppermute | solution.py:56
  418.0 115.4 %collective-permute-start.46 = (bf16[256,1536]{1,0:T(8,128)(2,1)S(1)}, bf16[256,1536]{1,0:T(8,128)(2,1)S(1)}, u32[]{:S(2)}, u32[]{:S(2)}) collective-permute-start(bf16[256,1536]{1,0:T(8,128)(2,1)S(1)} %get-tuple-element.65), channel_id=1, source_target_pairs={{0,16},{8,24},{16,0},{24,8},{1,17},{9,25},{17,1},{25,9},{2,18},{10... | collective-permute-start | bytes 2359304 | tf_op jit(solution)/shard_map/ppermute | solution.py:56
  419.1 114.3 %collective-permute-start.45 = (bf16[256,1536]{1,0:T(8,128)(2,1)S(1)}, bf16[256,1536]{1,0:T(8,128)(2,1)}, u32[]{:S(2)}, u32[]{:S(2)}) collective-permute-start(bf16[256,1536]{1,0:T(8,128)(2,1)S(1)} %get-tuple-element.63), channel_id=1, source_target_pairs={{0,8},{8,16},{16,24},{24,0},{1,9},{9,17},{17,25},{25,1},{2,10},{10... | collective-permute-start | bytes 2359304 | tf_op jit(solution)/shard_map/ppermute | solution.py:56
  466.6 228.2 %collective-permute-start.93 = (bf16[4,192,4608]{2,1,0:T(8,128)(2,1)}, bf16[4,192,4608]{2,1,0:T(8,128)(2,1)}, u32[]{:S(2)}, u32[]{:S(2)}) collective-permute-start(bf16[4,192,4608]{2,1,0:T(8,128)(2,1)} %dynamic-slice_bitcast_fusion), channel_id=1, source_target_pairs={{0,1},{1,0},{2,3},{3,2},{4,5},{5,4},{6,7},{7,6},{8,9},{9,8},{10,11... | collective-permute-start | bytes 21233672 | tf_op jit(solution)/shard_map/ppermute | solution.py:51
  605.9 53.8 %collective-permute-start.80 = (bf16[4,192,1536]{2,1,0:T(8,128)(2,1)}, bf16[4,192,1536]{2,1,0:T(8,128)(2,1)}, u32[]{:S(2)}, u32[]{:S(2)}) collective-permute-start(bf16[4,192,1536]{2,1,0:T(8,128)(2,1)} %dynamic-slice_bitcast_fusion.3), channel_id=1, source_target_pairs={{0,1},{1,0},{2,3},{3,2},{4,5},{5,4},{6,7},{7,6},{8,9},{9,8},{10,11... | collective-permute-start | bytes 7077896 | tf_op jit(solution)/shard_map/ppermute | solution.py:51
  687.6 42.6 %collective-permute-start.89 = (bf16[48,1536]{1,0:T(8,128)(2,1)}, bf16[48,1536]{1,0:T(8,128)(2,1)}, u32[]{:S(2)}, u32[]{:S(2)}) collective-permute-start(bf16[48,1536]{1,0:T(8,128)(2,1)} %get-tuple-element.93), channel_id=1, source_target_pairs={{0,24},{8,0},{16,8},{24,16},{1,25},{9,1},{17,9},{25,17},{2,26},{10... | collective-permute-start | bytes 442376 | tf_op jit(solution)/shard_map/ppermute | solution.py:56
  732.2 46.0 %collective-permute-start.96 = (bf16[96,4608]{1,0:T(8,128)(2,1)S(1)}, bf16[96,4608]{1,0:T(8,128)(2,1)S(1)}, u32[]{:S(2)}, u32[]{:S(2)}) collective-permute-start(bf16[96,4608]{1,0:T(8,128)(2,1)S(1)} %get-tuple-element.39), channel_id=1, source_target_pairs={{0,2},{1,3},{2,0},{3,1},{4,6},{5,7},{6,4},{7,5},{8,10},{9,11},{10,... | collective-permute-start | bytes 2654216 | tf_op jit(solution)/shard_map/ppermute | solution.py:51
  741.4 45.6 %collective-permute-start.107 = (bf16[144,1536]{1,0:T(8,128)(2,1)S(1)}, bf16[144,1536]{1,0:T(8,128)(2,1)S(1)}, u32[]{:S(2)}, u32[]{:S(2)}) collective-permute-start(bf16[144,1536]{1,0:T(8,128)(2,1)S(1)} %copy-done.43), channel_id=1, source_target_pairs={{0,2},{1,3},{2,0},{3,1},{4,6},{5,7},{6,4},{7,5},{8,10},{9,11},{10,... | collective-permute-start | bytes 1327112 | tf_op jit(solution)/shard_map/ppermute | solution.py:51
  787.0 77.5 %collective-permute-start.103 = (bf16[192,4608]{1,0:T(8,128)(2,1)S(1)}, bf16[192,4608]{1,0:T(8,128)(2,1)S(1)}, u32[]{:S(2)}, u32[]{:S(2)}) collective-permute-start(bf16[192,4608]{1,0:T(8,128)(2,1)S(1)} %fusion.26), channel_id=1, source_target_pairs={{8,0},{16,8},{24,16},{9,1},{17,9},{25,17},{10,2},{18,10},{26,18},{... | collective-permute-start | bytes 5308424 | tf_op jit(solution)/shard_map/ppermute | solution.py:135
  791.1 74.7 %collective-permute-start.100 = (bf16[192,4608]{1,0:T(8,128)(2,1)S(1)}, bf16[192,4608]{1,0:T(8,128)(2,1)S(1)}, u32[]{:S(2)}, u32[]{:S(2)}) collective-permute-start(bf16[192,4608]{1,0:T(8,128)(2,1)S(1)} %fusion.26), channel_id=1, source_target_pairs={{0,8},{8,16},{16,24},{1,9},{9,17},{17,25},{2,10},{10,18},{18,26},{... | collective-permute-start | bytes 5308424 | tf_op jit(solution)/shard_map/ppermute | solution.py:134
  809.3 59.5 %collective-permute-start.113 = (bf16[280,1536]{1,0:T(8,128)(2,1)S(1)}, bf16[280,1536]{1,0:T(8,128)(2,1)S(1)}, u32[]{:S(2)}, u32[]{:S(2)}) collective-permute-start(bf16[280,1536]{1,0:T(8,128)(2,1)S(1)} %fusion.30), channel_id=1, source_target_pairs={{0,8},{8,16},{16,24},{1,9},{9,17},{17,25},{2,10},{10,18},{18,26},{... | collective-permute-start | bytes 2580488 | tf_op jit(solution)/shard_map/ppermute | solution.py:134
  811.6 57.9 %collective-permute-start.116 = (bf16[280,1536]{1,0:T(8,128)(2,1)S(1)}, bf16[280,1536]{1,0:T(8,128)(2,1)S(1)}, u32[]{:S(2)}, u32[]{:S(2)}) collective-permute-start(bf16[280,1536]{1,0:T(8,128)(2,1)S(1)} %fusion.30), channel_id=1, source_target_pairs={{8,0},{16,8},{24,16},{9,1},{17,9},{25,17},{10,2},{18,10},{26,18},{... | collective-permute-start | bytes 2580488 | tf_op jit(solution)/shard_map/ppermute | solution.py:135
  864.6 94.0 %collective-permute-start.104 = (bf16[192,4608]{1,0:T(8,128)(2,1)S(1)}, bf16[192,4608]{1,0:T(8,128)(2,1)S(1)}, u32[]{:S(2)}, u32[]{:S(2)}) collective-permute-start(bf16[192,4608]{1,0:T(8,128)(2,1)S(1)} %collective-permute-done.103), channel_id=1, source_target_pairs={{8,0},{16,8},{9,1},{17,9},{10,2},{18,10},{11,3},{19,11},{12,4},{20... | collective-permute-start | bytes 5308424 | tf_op jit(solution)/shard_map/ppermute | solution.py:135
  865.9 94.0 %collective-permute-start.101 = (bf16[192,4608]{1,0:T(8,128)(2,1)S(1)}, bf16[192,4608]{1,0:T(8,128)(2,1)S(1)}, u32[]{:S(2)}, u32[]{:S(2)}) collective-permute-start(bf16[192,4608]{1,0:T(8,128)(2,1)S(1)} %collective-permute-done.100), channel_id=1, source_target_pairs={{8,16},{16,24},{9,17},{17,25},{10,18},{18,26},{11,19},{19,27},{12,... | collective-permute-start | bytes 5308424 | tf_op jit(solution)/shard_map/ppermute | solution.py:134
  867.8 44.1 %collective-permute-start.65 = (bf16[48,2048]{1,0:T(8,128)(2,1)S(1)}, bf16[48,2048]{1,0:T(8,128)(2,1)S(1)}, u32[]{:S(2)}, u32[]{:S(2)}) collective-permute-start(bf16[48,2048]{1,0:T(8,128)(2,1)S(1)} %get-tuple-element.91), channel_id=1, source_target_pairs={{0,16},{8,24},{16,0},{24,8},{1,17},{9,25},{17,1},{25,9},{2,18},{10... | collective-permute-start | bytes 589832 | tf_op jit(solution)/shard_map/ppermute | solution.py:56
  868.8 74.3 %collective-permute-start.114 = (bf16[280,1536]{1,0:T(8,128)(2,1)S(1)}, bf16[280,1536]{1,0:T(8,128)(2,1)S(1)}, u32[]{:S(2)}, u32[]{:S(2)}) collective-permute-start(bf16[280,1536]{1,0:T(8,128)(2,1)S(1)} %collective-permute-done.113), channel_id=1, source_target_pairs={{8,16},{16,24},{9,17},{17,25},{10,18},{18,26},{11,19},{19,27},{12,... | collective-permute-start | bytes 2580488 | tf_op jit(solution)/shard_map/ppermute | solution.py:134
  869.5 74.3 %collective-permute-start.117 = (bf16[280,1536]{1,0:T(8,128)(2,1)S(1)}, bf16[280,1536]{1,0:T(8,128)(2,1)S(1)}, u32[]{:S(2)}, u32[]{:S(2)}) collective-permute-start(bf16[280,1536]{1,0:T(8,128)(2,1)S(1)} %collective-permute-done.116), channel_id=1, source_target_pairs={{8,0},{16,8},{9,1},{17,9},{10,2},{18,10},{11,3},{19,11},{12,4},{20... | collective-permute-start | bytes 2580488 | tf_op jit(solution)/shard_map/ppermute | solution.py:135
  958.5 41.9 %collective-permute-start.105 = (bf16[192,4608]{1,0:T(8,128)(2,1)S(1)}, bf16[192,4608]{1,0:T(8,128)(2,1)S(1)}, u32[]{:S(2)}, u32[]{:S(2)}) collective-permute-start(bf16[192,4608]{1,0:T(8,128)(2,1)S(1)} %collective-permute-done.104), channel_id=1, source_target_pairs={{8,0},{9,1},{10,2},{11,3},{12,4},{13,5},{14,6},{15,7}} | collective-permute-start | bytes 5308424 | tf_op jit(solution)/shard_map/ppermute | solution.py:135
  (154 other events, 2953.3 us)

commit v2 on v1

--- a/solution.py
+++ b/solution.py
@@ -161,13 +161,7 @@
     return ctx_gather(part.astype(BF)).astype(F32)
 
 
-def lane_pad(n):
-    return -(-n // 128) * 128
-
-
-def pack_kernel(nz, nf, ff, wide, z_ref, w_ref, out_ref):
-    unit = ff // (nf * nz)
-    pad = wide - nf * unit
+def pack_kernel(nz, nf, ff, unit, upad, z_ref, w_ref, out_ref):
     for k in range(nz):
 
         @pl.when(z_ref[0] == k)
@@ -175,20 +169,21 @@
             for h in range(2):
                 for f in range(nf):
                     src = h * ff + f * (ff // nf) + k * unit
-                    dst = h * wide + f * unit
+                    dst = (h * nf + f) * upad
                     out_ref[:, dst : dst + unit] = w_ref[:, src : src + unit]
-                if pad:
-                    out_ref[:, (h + 1) * wide - pad : (h + 1) * wide] = jnp.zeros(
-                        (out_ref.shape[0], pad), out_ref.dtype
+                    out_ref[:, dst + unit : dst + upad] = jnp.zeros(
+                        (out_ref.shape[0], upad - unit), out_ref.dtype
                     )
 
 
 def pack(w, nz, nf, z):
     rows, ff = w.shape[0], w.shape[1] // 2
-    wide = lane_pad(ff // nz)
+    unit = ff // (nf * nz)
+    upad = -(-unit // 16) * 16
+    wide = nf * upad
     step = 32
     return pl.pallas_call(
-        functools.partial(pack_kernel, nz, nf, ff, wide),
+        functools.partial(pack_kernel, nz, nf, ff, unit, upad),
         grid=(rows // step,),
         in_specs=[
             pl.BlockSpec(memory_space=pltpu.SMEM),
@@ -199,27 +194,572 @@
     )(z.reshape(1).astype(jnp.int32), w)
 
 
-def unpack_kernel(nz, nf, ff, wide, *refs):
-    unit = ff // (nf * nz)
+def unpack_kernel(nz, nf, ff, unit, upad, *refs):
     out_ref = refs[-1]
     for k in range(nz):
         for h in range(2):
             for f in range(nf):
-                src = h * wide + f * unit
+                src = (h * nf + f) * upad
                 dst = h * ff + f * (ff // nf) + k * unit
                 out_ref[:, dst : dst + unit] = refs[k][:, src : src + unit].astype(F32)
 
 
 def unpack(parts, nz, nf, ff):
     rows, wide = parts[0].shape[0], parts[0].shape[1] // 2
+    unit, upad = ff // (nf * nz), wide // nf
     step = 32
     return pl.pallas_call(
-        functools.partial(unpack_kernel, nz, nf, ff, wide),
+        functools.partial(unpack_kernel, nz, nf, ff, unit, upad),
         grid=(rows // step,),
         in_specs=[pl.BlockSpec((step, 2 * wide), lambda i: (i, 0))] * nz,
         out_specs=pl.BlockSpec((step, 2 * ff), lambda i: (i, 0)),
         out_shape=jax.ShapeDtypeStruct((rows, 2 * ff), F32),
     )(*parts)
+
+
+MESH = pl.DeviceIdType.MESH
+VMEM_LIMIT = 63 * 2**20
+
+
+def remote(src, dst, send, recv, z, f):
+    return pltpu.make_async_remote_copy(
+        src_ref=src, dst_ref=dst, send_sem=send, recv_sem=recv, device_id=(z, f), device_id_type=MESH
+    )
+
+
+def rows_at(ref, index, count):
+    return ref.at[pl.ds(pl.multiple_of(index * count, count), count)]
+
+
+class PlaneGather:
+    def __init__(self, src, dst, rows, nf, z, me, send, recv, local, base):
+        self.src, self.dst, self.rows, self.nf, self.z, self.me = src, dst, rows, nf, z, me
+        self.send, self.recv, self.base = send, recv, base
+        self.local = pltpu.make_async_copy(src, rows_at(dst, me, rows), local)
+        self.sent = []
+        self.cut = half_rows(rows)
+        self.swaps = {}
+
+    @staticmethod
+    def sems(nf):
+        return 2 * nf
+
+    def slot(self, k, lo=0, hi=None):
+        hi = self.rows if hi is None else hi
+        start = pl.multiple_of((self.me ^ k) * self.rows, 16) + lo
+        return self.dst.at[pl.ds(pl.multiple_of(start, 16), hi - lo)]
+
+    def push(self, index, src, dst, flip_by):
+        copy = remote(
+            src, dst, self.send.at[self.base + index], self.recv.at[self.base + index],
+            self.z, self.me ^ flip_by,
+        )
+        copy.start()
+        self.sent.append(copy)
+        return copy
+
+    def begin(self):
+        self.local.start()
+        self.direct = {}
+        for k in (2, 4) if self.nf == 8 else range(2, self.nf, 2):
+            self.direct[k] = self.push(k, self.src, self.slot(0), k)
+        self.swaps[0] = self.push(1, self.src, self.slot(0), 1)
+
+    def swap(self, k):
+        self.swaps[k] = self.push(k + 1, self.slot(k), self.slot(k), 1)
+
+    def middle(self):
+        for k, copy in self.direct.items():
+            copy.wait_recv()
+            if self.nf == 8:
+                if k == 2:
+                    self.far_a = self.push(6, self.slot(2, 0, self.cut), self.slot(2, 0, self.cut), 4)
+                elif self.cut < self.rows:
+                    self.far_b = self.push(
+                        8, self.slot(4, self.cut), self.slot(4, self.cut), 2
+                    )
+            self.swap(k)
+
+    def late(self):
+        if self.nf == 8:
+            self.far_a.wait_recv()
+            if self.cut < self.rows:
+                self.far_b.wait_recv()
+            self.swap(6)
+
+    def finish(self):
+        self.local.wait()
+        for copy in self.swaps.values():
+            copy.wait_recv()
+
+    def drain(self):
+        for copy in self.sent:
+            copy.wait_send()
+
+
+class Chain:
+    def __init__(self, buf, rows, nz, z, me, send, recv, base):
+        self.buf, self.rows, self.nz, self.z, self.me = buf, rows, nz, z, me
+        self.send, self.recv, self.base = send, recv, base
+
+    @staticmethod
+    def sems(nz):
+        return nz + 2
+
+    def copy(self, j, sem, step):
+        slot = rows_at(self.buf, j, self.rows)
+        return remote(
+            slot, slot, self.send.at[self.base + sem], self.recv.at[self.base + j], self.z + step, self.me
+        )
+
+    def order(self, k):
+        z, nz = self.z, self.nz
+        below, above = z, nz - 1 - z
+        m = jnp.minimum(below, above)
+        near = jnp.where(k % 2 == 1, z - (k + 1) // 2, z + k // 2)
+        far = jnp.where(above > below, z + (k - m), z - (k - m))
+        return jnp.where(k <= 2 * m, near, far)
+
+    def begin(self):
+        z, nz = self.z, self.nz
+
+        @pl.when(z < nz - 1)
+        def _():
+            self.copy(z, nz, 1).start()
+
+        @pl.when(z > 0)
+        def _():
+            self.copy(z, nz + 1, -1).start()
+
+    def passing(self, j):
+        z, nz = self.z, self.nz
+        return jnp.logical_and(j < z, z < nz - 1), jnp.logical_and(j > z, z > 0)
+
+    def forward(self, k):
+        j = self.order(k)
+        up, down = self.passing(j)
+
+        @pl.when(up)
+        def _():
+            self.copy(j, j, 1).wait_recv()
+            self.copy(j, j, 1).start()
+
+        @pl.when(down)
+        def _():
+            self.copy(j, j, -1).wait_recv()
+            self.copy(j, j, -1).start()
+
+    def arrive(self, k):
+        j = self.order(k)
+        up, down = self.passing(j)
+
+        @pl.when(jnp.logical_not(jnp.logical_or(up, down)))
+        def _():
+            self.copy(j, j, 0).wait_recv()
+
+    def drain(self):
+        z, nz = self.z, self.nz
+
+        @pl.when(z < nz - 1)
+        def _():
+            self.copy(z, nz, 1).wait_send()
+
+        @pl.when(z > 0)
+        def _():
+            self.copy(z, nz + 1, -1).wait_send()
+
+        def one(k, carry):
+            j = self.order(k)
+            up, down = self.passing(j)
+
+            @pl.when(jnp.logical_or(up, down))
+            def _():
+                self.copy(j, j, 0).wait_send()
+
+            return carry
+
+        lax.fori_loop(1, nz, one, 0)
+
+
+def greet_ctx_and_plane(nz, nf, z, me):
+    barrier = pltpu.get_barrier_semaphore()
+    flips = (1, 2, 4) if nf == 8 else (1,) + tuple(range(2, nf, 2))
+    for k in flips:
+        pl.semaphore_signal(barrier, inc=1, device_id=(z, me ^ k), device_id_type=MESH)
+
+    @pl.when(z < nz - 1)
+    def _():
+        pl.semaphore_signal(barrier, inc=1, device_id=(z + 1, me), device_id_type=MESH)
+
+    @pl.when(z > 0)
+    def _():
+        pl.semaphore_signal(barrier, inc=1, device_id=(z - 1, me), device_id_type=MESH)
+
+    inner = jnp.logical_and(z > 0, z < nz - 1)
+
+    @pl.when(inner)
+    def _():
+        pl.semaphore_wait(barrier, len(flips) + 2)
+
+    @pl.when(jnp.logical_not(inner))
+    def _():
+        pl.semaphore_wait(barrier, len(flips) + 1)
+
+
+def loop(n, body):
+    def step(i, carry):
+        body(i)
+        return carry
+
+    lax.fori_loop(0, n, step, 0)
+
+
+def at128(i, n):
+    return i * n if isinstance(i, int) else pl.multiple_of(i * n, n)
+
+
+def turn(t, cos2, sin2):
+    return t * cos2 + pltpu.roll(t, HEAD_DIM // 2, 1) * sin2
+
+
+def front_kernel(
+    dims,
+    wq, sm, wo, wp, dn, x_ref, g_ref, cos_ref, sin_ref, qpos_ref, kpos_ref,
+    wq_all, wo_all, q_ref, kv_out, o_ref, lse_ref, mid_ref, dx_ref, gain_ref, dwgu, dwd, dpart,
+    stage, gu, dnb, g_all, x_all, act, dgu, smb, kv, bias, mask, send, recv, local,
+):
+    nz, nf, rows, d, wide, upad, nb, ng = dims
+    z, me = lax.axis_index("ctx"), lax.axis_index("fsdp")
+    q_width, k_width = HEADS * HEAD_DIM, KV_HEADS * HEAD_DIM
+    qkv = q_width + 2 * k_width
+    scale = HEAD_DIM ** (-0.5)
+    wr = d // nf
+    per = PlaneGather.sems(nf)
+    plane = [
+        PlaneGather(src, dst, r, nf, z, me, send, recv, local.at[i], i * per)
+        for i, (src, dst, r) in enumerate(
+            [(wq, wq_all, wr), (sm, smb, 16), (wo, wo_all, wr), (wp, gu, wr), (dn, dnb, upad)]
+        )
+    ]
+    p_q, p_s, p_o, p_gu, p_d = plane
+    base = len(plane) * per
+    chain = [
+        Chain(buf, rows, nz, z, me, send, recv, base + i * Chain.sems(nz))
+        for i, buf in enumerate([g_all, kv, x_all])
+    ]
+    c_g, c_kv, c_x = chain
+    base += len(chain) * Chain.sems(nz)
+    spare = len(plane)
+
+    g_copy = pltpu.make_async_copy(g_ref, rows_at(g_all, z, rows), local.at[spare])
+    g_copy.start()
+    greet_ctx_and_plane(nz, nf, z, me)
+    p_s.begin()
+    p_q.begin()
+    g_copy.wait()
+    c_g.begin()
+
+    x = x_ref[...].astype(F32)
+    inverse = lax.rsqrt(jnp.mean(x * x, -1, keepdims=True) + EPSILON)
+    mask[...] = jnp.where(kpos_ref[...] <= qpos_ref[...], 0.0, MASKED)
+
+    p_s.middle()
+    p_q.middle()
+    p_s.late()
+    p_q.late()
+    p_o.begin()
+    p_s.finish()
+    for f in range(nf):
+        row = smb[f * 16 : (f + 1) * 16, :].astype(F32)[0:1]
+        bias[0:1, f * nb : (f + 1) * nb] = row[:, :nb]
+        gain_ref[0:1, f * ng : (f + 1) * ng] = row[:, nb : nb + ng]
+        gain_ref[1:2, f * ng : (f + 1) * ng] = row[:, nb + ng : nb + 2 * ng]
+    normed = (x * inverse * gain_ref[0:1, :]).astype(BF)
+    x_all[pl.ds(at128(z, rows), rows), :] = normed
+    p_q.finish()
+    fetch = pltpu.make_async_copy(wq_all, stage.at[pl.ds(0, d)], local.at[spare])
+    fetch.start()
+    for k in range(1, nz - 1):
+        c_g.forward(k)
+    fetch.wait()
+
+    def project(t):
+        c0 = at128(t, 2 * HEAD_DIM)
+        y = dot(
+            x_all[pl.ds(at128(z, rows), rows), :], stage[pl.ds(0, d), pl.ds(c0, 2 * HEAD_DIM)]
+        ) + bias[0:1, pl.ds(c0, 2 * HEAD_DIM)]
+        return y, c0
+
+    def project_v(t):
+        y, c0 = project(t)
+        kv[pl.ds(at128(z, rows), rows), pl.ds(pl.multiple_of(c0 - q_width, 256), 256)] = y.astype(BF)
+
+    def turned(y):
+        halves = [
+            turn(y[:, h * HEAD_DIM : (h + 1) * HEAD_DIM], cos_ref[...], sin_ref[...]).astype(BF)
+            for h in range(2)
+        ]
+        return jnp.concatenate(halves, 1)
+
+    project_v((q_width + k_width) // 256)
+    y, _ = project(q_width // 256)
+    kv[pl.ds(at128(z, rows), rows), 0:k_width] = turned(y)
+    c_kv.begin()
+    p_gu.begin()
+
+    def project_q(t):
+        y, c0 = project(t)
+        q_ref[:, pl.ds(c0, 256)] = turned(y)
+
+    loop(q_width // 256, project_q)
+    for k in range(1, nz):
+        c_kv.forward(k)
+        c_kv.arrive(k)
+    c_g.forward(nz - 1)
+    p_o.middle()
+
+    lanes = lax.broadcasted_iota(jnp.int32, (rows, HEAD_DIM), 1)
+    lse_ref[...] = jnp.zeros_like(lse_ref)
+
+    def head(h):
+        c0 = at128(h, HEAD_DIM)
+        kc = at128(h // (HEADS // KV_HEADS), HEAD_DIM)
+        vc = pl.multiple_of(kc + k_width, HEAD_DIM)
+        s = dot_bt(q_ref[:, pl.ds(c0, HEAD_DIM)], kv[:, pl.ds(kc, HEAD_DIM)]) * scale + mask[...]
+        top = jnp.max(s, -1, keepdims=True)
+        p = jnp.exp(s - top)
+        total = jnp.sum(p, -1, keepdims=True)
+        o = dot(p.astype(BF), kv[:, pl.ds(vc, HEAD_DIM)]) / total
+        o_ref[:, pl.ds(c0, HEAD_DIM)] = o.astype(BF)
+        lse_ref[...] = jnp.where(lanes == h, top + jnp.log(total), lse_ref[...])
+
+    half = HEADS // 2
+    loop(half, head)
+    p_o.late()
+    loop(HEADS - half, lambda h: head(h + half))
+    p_o.finish()
+    fetch = pltpu.make_async_copy(wo_all, stage.at[pl.ds(0, q_width), pl.ds(0, d)], local.at[spare])
+    fetch.start()
+    p_gu.middle()
+    fetch.wait()
+
+    def out_proj(t):
+        c0 = at128(t, 512)
+        mid_ref[:, pl.ds(c0, 512)] = (
+            dot(o_ref[...], stage[pl.ds(0, q_width), pl.ds(c0, 512)]) + x_ref[:, pl.ds(c0, 512)].astype(F32)
+        )
+
+    loop(d // 512, out_proj)
+    mid = mid_ref[...]
+    inverse_two = lax.rsqrt(jnp.mean(mid * mid, -1, keepdims=True) + EPSILON)
+    x_all[pl.ds(at128(z, rows), rows), :] = (mid * inverse_two * gain_ref[1:2, :]).astype(BF)
+    c_x.begin()
+    for k in range(1, nz - 1):
+        c_x.forward(k)
+    p_gu.late()
+    p_d.begin()
+    p_gu.finish()
+
+    cols = 768 if wide % 768 == 0 else 256
+
+    def hidden(j):
+        r0 = at128(j, rows)
+
+        def one(t):
+            c0 = at128(t, cols)
+            xb = x_all[pl.ds(r0, rows), :]
+            gate = dot(xb, gu[:, pl.ds(c0, cols)])
+            up = dot(xb, gu[:, pl.ds(pl.multiple_of(wide + c0, 128), cols)])
+            act[pl.ds(r0, rows), pl.ds(c0, cols)] = (gate * jax.nn.sigmoid(gate) * up).astype(BF)
+            dgu[pl.ds(r0, rows), pl.ds(c0, cols)] = gate.astype(BF)
+            dgu[pl.ds(r0, rows), pl.ds(pl.multiple_of(wide + c0, 128), cols)] = up.astype(BF)
+
+        loop(wide // cols, one)
+
+    hidden(z)
+
+    def nearest(k):
+        c_x.arrive(k)
+        hidden(c_x.order(k))
+
+    loop(nz - 2, lambda i: nearest(i + 1))
+    c_x.forward(nz - 1)
+    p_d.middle()
+    nearest(nz - 1)
+    for k in range(1, nz):
+        c_g.arrive(k)
+    p_d.late()
+    p_d.finish()
+
+    def back(j):
+        r0 = at128(j, rows)
+
+        def one(t):
+            c0 = at128(t, cols)
+            c1 = pl.multiple_of(wide + c0, 128)
+            da = dot_bt(g_all[pl.ds(r0, rows), :], dnb[pl.ds(c0, cols), :])
+            gate = dgu[pl.ds(r0, rows), pl.ds(c0, cols)].astype(F32)
+            up = dgu[pl.ds(r0, rows), pl.ds(c1, cols)].astype(F32)
+            sig = jax.nn.sigmoid(gate)
+            dgu[pl.ds(r0, rows), pl.ds(c0, cols)] = (
+                da * up * (sig * (1.0 + gate * (1.0 - sig)))
+            ).astype(BF)
+            dgu[pl.ds(r0, rows), pl.ds(c1, cols)] = (da * gate * sig).astype(BF)
+
+        loop(wide // cols, one)
+
+    rs = base
+
+    slots = stage.at[:, pl.ds(0, d)]
+
+    def slot_copy(src, dst, step):
+        return remote(
+            rows_at(slots, src, rows), rows_at(slots, dst, rows),
+            send.at[rs + src], recv.at[rs + dst], z + step, me,
+        )
+
+    def give(j):
+        r0 = at128(j, rows)
+        back(j)
+        below, above = j > z, j < z
+        got = jnp.logical_or(
+            jnp.logical_and(below, z > 0), jnp.logical_and(above, z < nz - 1)
+        )
+
+        @pl.when(got)
+        def _():
+            slot_copy(j, j, 0).wait_recv()
+
+        def one(t):
+            c0 = at128(t, 512)
+            y = dot_bt(dgu[pl.ds(r0, rows), :], gu[pl.ds(c0, 512), :])
+            where = (pl.ds(at128(j, rows), rows), pl.ds(c0, 512))
+            y = y + jnp.where(got, stage[where].astype(F32), 0.0)
+            stage[where] = y.astype(BF)
+
+        loop(d // 512, one)
+
+        @pl.when(below)
+        def _():
+            slot_copy(j, j, 1).start()
+
+        @pl.when(above)
+        def _():
+            slot_copy(j, jnp.where(z - 1 == j, nz, j), -1).start()
+
+    loop(nz - 1, lambda i: give(c_x.order(nz - 1 - i)))
+    back(z)
+
+    def own(t):
+        c0 = at128(t, 512)
+        dx_ref[:, pl.ds(c0, 512)] = dot_bt(
+            dgu[pl.ds(at128(z, rows), rows), :], gu[pl.ds(c0, 512), :]
+        )
+
+    loop(d // 512, own)
+
+    p_gu.drain()
+
+    def w_gu_grad(t):
+        c0 = at128(t, 256)
+        gu[:, pl.ds(c0, 256)] = dot_at(x_all[...], dgu[:, pl.ds(c0, 256)]).astype(BF)
+
+    loop(2 * wide // 256, w_gu_grad)
+    out_gu = pltpu.make_async_copy(gu, dwgu, local.at[spare + 1])
+    out_gu.start()
+
+    c_x.drain()
+
+    def down_part(t):
+        c0 = at128(t, 256)
+        x_all[:, pl.ds(c0, 256)] = dot(act[...], dnb[:, pl.ds(c0, 256)]).astype(BF)
+
+    loop(d // 256, down_part)
+    out_p = pltpu.make_async_copy(x_all, dpart, local.at[spare + 3])
+    out_p.start()
+
+    p_d.drain()
+
+    def w_down_grad(t):
+        c0 = at128(t, 512)
+        dnb[:, pl.ds(c0, 512)] = dot_at(act[...], g_all[:, pl.ds(c0, 512)]).astype(BF)
+
+    loop(d // 512, w_down_grad)
+    out_d = pltpu.make_async_copy(dnb, dwd, local.at[spare])
+    out_d.start()
+    out_kv = pltpu.make_async_copy(kv, kv_out, local.at[spare + 2])
+    out_kv.start()
+
+    @pl.when(z > 0)
+    def _():
+        slot_copy(z, z, 0).wait_recv()
+        dx_ref[...] += rows_at(slots, z, rows)[...].astype(F32)
+
+    @pl.when(z < nz - 1)
+    def _():
+        slot_copy(z, nz, 0).wait_recv()
+        dx_ref[...] += rows_at(slots, nz, rows)[...].astype(F32)
+
+    for part in (p_q, p_s, p_o, c_g, c_kv):
+        part.drain()
+
+    def gave(i):
+        j = c_x.order(i + 1)
+        slot_copy(j, j, 0).wait_send()
+
+    loop(nz - 1, gave)
+    out_d.wait()
+    out_gu.wait()
+    out_kv.wait()
+    out_p.wait()
+
+
+def front(dims, wq, sm, wo, wp, dn, x, g, cos2, sin2, qpos, kpos):
+    nz, nf, rows, d, wide, upad, nb, ng = dims
+    q_width, k_width = HEADS * HEAD_DIM, KV_HEADS * HEAD_DIM
+    qkv = q_width + 2 * k_width
+    tokens = nz * rows
+    any_, vm = pl.BlockSpec(memory_space=pl.ANY), pl.BlockSpec(memory_space=pltpu.VMEM)
+    sems = 5 * PlaneGather.sems(nf) + 3 * Chain.sems(nz) + nz + 1
+    out = jax.ShapeDtypeStruct
+    return pl.pallas_call(
+        functools.partial(front_kernel, dims),
+        in_specs=[any_] * 5 + [vm, any_] + [vm] * 4,
+        out_specs=[any_, any_, vm, any_] + [vm] * 5 + [any_] * 3,
+        out_shape=[
+            out((d, qkv), BF),
+            out((q_width, d), BF),
+            out((rows, q_width), BF),
+            out((tokens, 2 * k_width), BF),
+            out((rows, q_width), BF),
+            out((rows, HEAD_DIM), F32),
+            out((rows, d), F32),
+            out((rows, d), F32),
+            out((8, d), F32),
+            out((d, 2 * wide), BF),
+            out((wide, d), BF),
+            out((tokens, d), BF),
+        ],
+        scratch_shapes=[
+            pltpu.VMEM((max(d, (nz + 1) * rows), qkv), BF),
+            pltpu.VMEM((d, 2 * wide), BF),
+            pltpu.VMEM((wide, d), BF),
+            pltpu.VMEM((tokens, d), BF),
+            pltpu.VMEM((tokens, d), BF),
+            pltpu.VMEM((tokens, wide), BF),
+            pltpu.VMEM((tokens, 2 * wide), BF),
+            pltpu.VMEM((nf * 16, sm.shape[1]), BF),
+            pltpu.VMEM((tokens, 2 * k_width), BF),
+            pltpu.VMEM((8, qkv), F32),
+            pltpu.VMEM((rows, tokens), F32),
+            pltpu.SemaphoreType.DMA((sems,)),
+            pltpu.SemaphoreType.DMA((sems,)),
+            pltpu.SemaphoreType.DMA((9,)),
+        ],
+        compiler_params=pltpu.CompilerParams(
+            collective_id=0, has_side_effects=True, vmem_limit_bytes=VMEM_LIMIT
+        ),
+    )(wq, sm, wo, wp, dn, x, g, cos2, sin2, qpos, kpos)
 
 
 def shards(
@@ -233,8 +773,6 @@
     piece_len = rows // 2
     ff = w_gate_up.shape[1] // 2
     unit = ff // (nf * nz)
-    quarter = ff // nz
-    wide = lane_pad(quarter)
     scale = HEAD_DIM ** (-0.5)
     order_row = block_order[0]
     all_places = (
@@ -243,76 +781,42 @@
     my_places = lax.dynamic_slice_in_dim(all_places, z * rows, rows)
     visible = all_places[None, :] <= my_places[:, None]
     cosine, sine_table = angle_tables(my_places)
-
-    whole_qkv = plane_gather(w_qkv)
-    small = jnp.concatenate([b_qkv, gain_attn, gain_mlp]).reshape(1, -1)
-    smalls = plane_gather(small)
+    cos2 = jnp.concatenate([cosine, cosine], 1)
+    sin2 = jnp.concatenate([-sine_table, sine_table], 1)
+
+    packed = pack(w_gate_up, nz, nf, z)
+    wide = packed.shape[1] // 2
+    upad = wide // nf
+    down_mine = jnp.pad(
+        lax.dynamic_slice_in_dim(w_down, z * unit, unit), ((0, upad - unit), (0, 0))
+    )
     nb, ng = b_qkv.shape[0], gain_attn.shape[0]
-    bias = smalls[:, :nb].reshape(-1).astype(F32)
-    gain_first = smalls[:, nb : nb + ng].reshape(-1).astype(F32)
-    gain_second = smalls[:, nb + ng :].reshape(-1).astype(F32)
-
-    packed = pack(w_gate_up, nz, nf, z)
-    down_mine = lax.dynamic_slice_in_dim(w_down, z * unit, unit)
-    packed, down_mine, w_out, whole_qkv = lax.optimization_barrier(
-        (packed, down_mine, w_out, whole_qkv)
-    )
-    whole_out = plane_gather(w_out)
-    gu = plane_gather(packed)
-    down = jnp.pad(plane_gather(down_mine), ((0, wide - quarter), (0, 0)))
+    d = hidden_in.shape[2]
+    small = jnp.concatenate([b_qkv, gain_attn, gain_mlp])
+    small = jnp.pad(small[None], ((0, 15), (0, -small.shape[0] % 128)))
     grad_low = cotangent[0]
-    grad_all = ctx_gather(grad_low)
-
+    (whole_qkv, whole_out, q_low, kv_all, attn_low, lse, middle, grad_normed_two, gains, gate_up_local, down_local,
+     down_part) = front(
+        (nz, nf, rows, d, wide, upad, nb, ng),
+        w_qkv, small, w_out, packed, down_mine, hidden_in[0], grad_low, cos2, sin2,
+        my_places[:, None], all_places[None, :],
+    )
+    gain_first, gain_second = gains[0], gains[1]
     inputs = hidden_in[0].astype(F32)
     inverse_one = lax.rsqrt(jnp.mean(inputs * inputs, -1, keepdims=True) + EPSILON)
     normed = (inputs * inverse_one * gain_first).astype(BF)
-    projected = dot(normed, whole_qkv) + bias
-    queries = rotate(
-        projected[:, :q_width].reshape(rows, KV_HEADS, groups, HEAD_DIM), cosine, sine_table
-    ).astype(BF)
-    keys = rotate(
-        projected[:, q_width : q_width + k_width].reshape(rows, KV_HEADS, HEAD_DIM),
-        cosine,
-        sine_table,
-    ).astype(BF)
-    kv = jnp.concatenate(
-        [keys.reshape(rows, k_width), projected[:, q_width + k_width :].astype(BF)], 1
-    )
-    kv_all = ctx_gather(kv)
+    inverse_two = lax.rsqrt(jnp.mean(middle * middle, -1, keepdims=True) + EPSILON)
+    queries = q_low.reshape(rows, KV_HEADS, groups, HEAD_DIM)
     keys_all = kv_all[:, :k_width].reshape(-1, KV_HEADS, HEAD_DIM)
     values_all = kv_all[:, k_width:].reshape(-1, KV_HEADS, HEAD_DIM)
-    scores = jnp.einsum("qkgd,tkd->kgqt", queries, keys_all, preferred_element_type=F32) * scale
-    scores = jnp.where(visible, scores, MASKED)
-    row_top = jnp.max(scores, -1, keepdims=True)
-    weights = jnp.exp(scores - row_top)
-    row_total = jnp.sum(weights, -1, keepdims=True)
-    attn_heads = (
-        jnp.einsum("kgqt,tkd->kgqd", weights.astype(BF), values_all, preferred_element_type=F32)
-        / row_total
-    )
-    log_total = row_top + jnp.log(row_total)
-    attn_low = attn_heads.transpose(2, 0, 1, 3).reshape(rows, q_width).astype(BF)
-    middle = inputs + dot(attn_low, whole_out)
-    inverse_two = lax.rsqrt(jnp.mean(middle * middle, -1, keepdims=True) + EPSILON)
-    normed_two = (middle * inverse_two * gain_second).astype(BF)
-
-    x_all = ctx_gather(normed_two)
-    gate = dot(x_all, gu[:, :wide])
-    up = dot(x_all, gu[:, wide:])
-    sigmoid_gate = jax.nn.sigmoid(gate)
-    act = (gate * sigmoid_gate * up).astype(BF)
-    grad_act = dot_bt(grad_all, down)
-    grad_gate = grad_act * up * (sigmoid_gate * (1.0 + gate * (1.0 - sigmoid_gate)))
-    grad_up = grad_act * gate * sigmoid_gate
-    grad_mixed = jnp.concatenate([grad_gate, grad_up], 1).astype(BF)
-    grad_normed_two = ctx_scatter(dot_bt(grad_mixed, gu).reshape(nz, rows, -1))
-    down_sum = ctx_scatter(dot(act, down).reshape(nz, rows, -1))
+    attn_heads = attn_low.astype(F32).reshape(rows, KV_HEADS, groups, HEAD_DIM).transpose(1, 2, 0, 3)
+    log_total = lse[:, :HEADS].reshape(rows, KV_HEADS, groups).transpose(1, 2, 0)[..., None]
+    down_sum = ctx_scatter(down_part.reshape(nz, rows, -1))
     hidden_out = (middle + down_sum).astype(BF)[None]
-
-    down_local = dot_at(act, grad_all)[:quarter].reshape(nf, unit, -1)
-    gate_up_local = dot_at(x_all, grad_mixed).reshape(nf, -1, 2 * wide)
-    grad_down = jnp.concatenate(ctx_chain(plane_scatter(down_local).astype(BF)), 0).astype(F32)
-    grad_gate_up = unpack(ctx_chain(plane_scatter(gate_up_local).astype(BF)), nz, nf, ff)
+    down_sums = plane_scatter(down_local.reshape(nf, upad, -1))[:unit]
+    grad_down = jnp.concatenate(ctx_chain(down_sums.astype(BF)), 0).astype(F32)
+    gate_up_sums = plane_scatter(gate_up_local.reshape(nf, -1, 2 * wide))
+    grad_gate_up = unpack(ctx_chain(gate_up_sums.astype(BF)), nz, nf, ff)
 
     grad_full = grad_low.astype(F32)
     scaled_two = gain_second * grad_normed_two

time: 1020 us -> 853 us (0.84)
  Pallas kernels: 15.8 us -> 253 us
  waiting for transfers between devices: 439 us -> 258 us
  matrix products: 157 us -> 39.7 us
  local copies, waits for them, and re-layouts: 168 us -> 71.8 us
  other arithmetic: 68.2 us -> 57.1 us
    pallas_call x2 -> x3, Pallas kernels: 15.8 us -> 253 us  [the longest x1 238 us: front(): pl.pallas_call(functools.partial(front_kernel, dims), in_specs=[any_] * 5...]
    ppermute x36 -> x24, waiting for transfers between devices: 287 us -> 149 us  [shift(): return lax.ppermute(x, 'ctx', [(i, (i + distance) % n) for i in range(n)])]
    dynamic_update_slice x61 -> x10, local copies, waits for them, and re-layouts: 55.6 us -> 0.25 us  [place(): out = lax.dynamic_update_slice(out, piece, start)]
    dot_general x6 -> x0, matrix products: 51.4 us -> none  [the longest x5 46.9 us: dot(): return jnp.dot(a, b, preferred_element_type=F32)]
    ppermute x71 -> x32, waiting for transfers between devices: 131 us -> 84.7 us  [flip(): return lax.ppermute(x, 'fsdp', [(i, i ^ bit) for i in range(n)])]
    dot_general x4 -> x2, matrix products: 42.6 us -> 7 us  [dot_bt(): lax.dot_general(a, b, (((1,), (1,)), ((), ())), preferred_element_type=F32)]
    dot_general x4 -> x2, matrix products: 35.9 us -> 5.35 us  [dot_at(): lax.dot_general(a, b, (((0,), (0,)), ((), ())), preferred_element_type=F32)]
    ppermute x71 -> x32, starting transfers between devices: 60.2 us -> 36.8 us  [flip(): return lax.ppermute(x, 'fsdp', [(i, i ^ bit) for i in range(n)])]
  transfers between devices with their start and end apart: 119 -> 68, of which waited for: 45 -> 28; matrix products, arithmetic and copies ran while one was open for 29% -> 18% of each run, Pallas kernels for 1% -> 0%
where the time goes in v2:
time: 853 us; the launch traced here: 842 us
  waiting for transfers between devices  258 us (30%)
  Pallas kernels  253 us (30%)
  starting transfers between devices  161 us (19%)
  local copies, waits for them, and re-layouts  71.8 us (8%)
  other arithmetic  57.1 us (7%)
  matrix products  39.7 us (5%)
    pallas_call x1, Pallas kernels, front(): pl.pallas_call(functools.partial(front_kernel, dims), in_specs=[any_] * 5...  238 us
    ppermute x24, waiting for transfers between devices, shift(): return lax.ppermute(x, 'ctx', [(i, (i + distance) % n) for i in range(n)])  149 us
    ppermute x24, starting transfers between devices, shift(): return lax.ppermute(x, 'ctx', [(i, (i + distance) % n) for i in range(n)])  109 us
    ppermute x32, waiting for transfers between devices, flip(): return lax.ppermute(x, 'fsdp', [(i, i ^ bit) for i in range(n)])  84.7 us
    ppermute x32, starting transfers between devices, flip(): return lax.ppermute(x, 'fsdp', [(i, i ^ bit) for i in range(n)])  36.8 us
    ppermute x6, waiting for transfers between devices, ctx_chain(): lax.ppermute(down[-1], 'ctx', [(i, i - 1) for i in range(1, n - t + 1)])  24.1 us
    convert_element_type x5, other arithmetic, plane_scatter(): acc = (kept.astype(F32) + flip(given, 1).astype(F32)).astype(BF)  20.6 us
  transfers between devices with their start and end apart: 68, of which 28 were waited for; matrix products, arithmetic and copies ran while one was open for 18% of the time, Pallas kernels for 0%

profile of v2, /device:TPU:0, one launch (start us, length us, event | category | flops | bytes accessed | tf_op | source)
XLA Modules:
  0.0 842.1 jit_solution(1204679421812681600)
XLA Ops:
  7.0 6.0 shard_map.177.wp
  13.9 237.7 %shard_map.178 = (bf16[1536,2048]{1,0:T(8,128)(2,1)}, bf16[1536,1536]{1,0:T(8,128)(2,1)}, bf16[256,1536]{1,0:T(8,128)(2,1)}, bf16[1024,512]{1,0:T(8,128)(2,1)}, ...) custom-call(bf16[192,2048]{1,0:T(8,128)(2,1)} %wq.1, ...), custom_call_target="tpu_custom_call" | custom-call | tf_op jit(solution)/shard_map/pallas_call | solution.py:725
  254.7 28.2 %collective-permute-start = (bf16[256,1536]{1,0:T(8,128)(2,1)}, bf16[256,1536]{1,0:T(8,128)(2,1)}, u32[]{:S(2)}, u32[]{:S(2)}) collective-permute-start(bf16[256,1536]{1,0:T(8,128)(2,1)} %get-tuple-element.72), channel_id=1, source_target_pairs={{0,8},{8,16},{16,24},{24,0},{1,9},{9,17},{17,25},{25,1},{2,10},{10... | collective-permute-start | bytes 2359304 | tf_op jit(solution)/shard_map/ppermute | solution.py:56
  282.9 8.1 collective-permute-start.1
  291.0 6.5 dynamic-slice_bitcast_fusion
  317.8 7.8 fusion.90
  325.6 15.5 %collective-permute-done.1 = bf16[256,1536]{1,0:T(8,128)(2,1)} collective-permute-done((bf16[256,1536]{1,0:T(8,128)(2,1)}, bf16[256,1536]{1,0:T(8,128)(2,1)}, u32[]{:S(2)}, u32[]{:S(2)}) %collective-permute-start.1) | collective-permute-done | bytes 786464 | tf_op jit(solution)/shard_map/ppermute | solution.py:56
  354.6 8.3 fusion.29
  362.9 7.1 multiply_convert_fusion
  396.4 15.6 %collective-permute-start.5 = (bf16[256,512]{1,0:T(8,128)(2,1)}, bf16[256,512]{1,0:T(8,128)(2,1)}, u32[]{:S(2)}, u32[]{:S(2)}) collective-permute-start(bf16[256,512]{1,0:T(8,128)(2,1)} %bitcast.342), channel_id=1, source_target_pairs={{0,24},{8,0},{16,8},{24,16},{1,25},{9,1},{17,9},{25,17},{2,26},{10... | collective-permute-start | bytes 786440 | tf_op jit(solution)/shard_map/ppermute | solution.py:56
  419.6 11.0 %collective-permute-done.3 = bf16[256,512]{1,0:T(8,128)(2,1)} collective-permute-done((bf16[256,512]{1,0:T(8,128)(2,1)}, bf16[256,512]{1,0:T(8,128)(2,1)}, u32[]{:S(2)}, u32[]{:S(2)}) %collective-permute-start.3) | collective-permute-done | bytes 262176 | tf_op jit(solution)/shard_map/ppermute | solution.py:56
  432.9 4.7 fusion.82
  498.4 9.8 %fusion = bf16[4,192,4608]{2,1,0:T(8,128)(2,1)} fusion(bf16[4,192,4608]{2,1,0:T(8,128)(2,1)} %collective-permute-done.42, bf16[4,2,192,4608]{3,2,1,0:T(8,128)(2,1)} %bitcast.314, s32[]{:T(128)S(6)} %select_n.335), kind=kLoop, calls=%fused_computation.1 | loop fusion | flops 14155776 | bytes 21233668 | tf_op jit(solution)/shard_map/convert_element_type | solution.py:96
  520.7 20.5 %collective-permute-done.46 = bf16[96,4608]{1,0:T(8,128)(2,1)S(1)} collective-permute-done((bf16[96,4608]{1,0:T(8,128)(2,1)S(1)}, bf16[96,4608]{1,0:T(8,128)(2,1)S(1)}, u32[]{:S(2)}, u32[]{:S(2)}) %collective-permute-start.46) | collective-permute-done | bytes 884768 | tf_op jit(solution)/shard_map/ppermute | solution.py:51
  548.8 4.5 collective-permute-done.10
  555.2 17.0 %collective-permute-done.43 = bf16[96,4608]{1,0:T(8,128)(2,1)S(1)} collective-permute-done((bf16[96,4608]{1,0:T(8,128)(2,1)S(1)}, bf16[96,4608]{1,0:T(8,128)(2,1)S(1)}, u32[]{:S(2)}, u32[]{:S(2)}) %collective-permute-start.43) | collective-permute-done | bytes 884768 | tf_op jit(solution)/shard_map/ppermute | solution.py:51
  574.2 11.0 %collective-permute-done.47 = bf16[96,4608]{1,0:T(8,128)(2,1)S(1)} collective-permute-done((bf16[96,4608]{1,0:T(8,128)(2,1)S(1)}, bf16[96,4608]{1,0:T(8,128)(2,1)S(1)}, u32[]{:S(2)}, u32[]{:S(2)}) %collective-permute-start.47) | collective-permute-done | bytes 884768 | tf_op jit(solution)/shard_map/ppermute | solution.py:51
  593.5 7.1 collective-permute-done.56
  602.7 7.5 collective-permute-done.58
  613.2 5.4 collective-permute-done.7
  630.5 32.4 %collective-permute-done.40 = bf16[48,1536]{1,0:T(8,128)(2,1)S(1)} collective-permute-done((bf16[48,1536]{1,0:T(8,128)(2,1)S(1)}, bf16[48,1536]{1,0:T(8,128)(2,1)S(1)}, u32[]{:S(2)}, u32[]{:S(2)}) %collective-permute-start.40) | collective-permute-done | bytes 147488 | tf_op jit(solution)/shard_map/ppermute | solution.py:56
  662.9 5.7 collective-permute-start.39
  668.7 10.6 %collective-permute-done.39 = bf16[48,1536]{1,0:T(8,128)(2,1)S(1)} collective-permute-done((bf16[48,1536]{1,0:T(8,128)(2,1)S(1)}, bf16[48,1536]{1,0:T(8,128)(2,1)S(1)}, u32[]{:S(2)}, u32[]{:S(2)}) %collective-permute-start.39) | collective-permute-done | bytes 147488 | tf_op jit(solution)/shard_map/ppermute | solution.py:56
  679.3 6.9 collective-permute-start.13
  689.4 8.2 collective-permute-start.15
  699.7 36.1 %collective-permute-done.15 = bf16[48,2048]{1,0:T(8,128)(2,1)S(1)} collective-permute-done((bf16[48,2048]{1,0:T(8,128)(2,1)S(1)}, bf16[48,2048]{1,0:T(8,128)(2,1)S(1)}, u32[]{:S(2)}, u32[]{:S(2)}) %collective-permute-start.15) | collective-permute-done | bytes 196640 | tf_op jit(solution)/shard_map/ppermute | solution.py:56
  739.6 16.5 %collective-permute-done.14 = bf16[48,2048]{1,0:T(8,128)(2,1)S(1)} collective-permute-done((bf16[48,2048]{1,0:T(8,128)(2,1)S(1)}, bf16[48,2048]{1,0:T(8,128)(2,1)S(1)}, u32[]{:S(2)}, u32[]{:S(2)}) %collective-permute-start.14) | collective-permute-done | bytes 196640 | tf_op jit(solution)/shard_map/ppermute | solution.py:56
  756.1 7.4 collective-permute-start.41
  778.9 5.9 collective-permute-done.17
  790.7 9.3 %collective-permute-done.18 = bf16[48,2048]{1,0:T(8,128)(2,1)S(1)} collective-permute-done((bf16[48,2048]{1,0:T(8,128)(2,1)S(1)}, bf16[48,2048]{1,0:T(8,128)(2,1)S(1)}, u32[]{:S(2)}, u32[]{:S(2)}) %collective-permute-start.18) | collective-permute-done | bytes 196640 | tf_op jit(solution)/shard_map/ppermute | solution.py:56
  804.9 24.1 %collective-permute-done.54 = bf16[192,4608]{1,0:T(8,128)(2,1)S(1)} collective-permute-done((bf16[192,4608]{1,0:T(8,128)(2,1)S(1)}, bf16[192,4608]{1,0:T(8,128)(2,1)S(1)}, u32[]{:S(2)}, u32[]{:S(2)}) %collective-permute-start.54) | collective-permute-done | bytes 1769504 | tf_op jit(solution)/shard_map/ppermute | solution.py:135
  832.4 9.3 %shard_map.179 = f32[192,17920]{1,0:T(8,128)} custom-call(bf16[192,4608]{1,0:T(8,128)(2,1)} %get-tuple-element.59.refs_0_, bf16[192,4608]{1,0:T(8,128)(2,1)} %get-tuple-element.58.refs_1_, bf16[192,4608]{1,0:T(8,128)(2,1)} %get-tuple-element.57.refs_2_, bf16[192,4608]{1,0:T(8,128)(2,1)} %get-tuple-element.56.refs_3_), custom_call_target="tpu_custom_call" | custom-call | tf_op jit(solution)/shard_map/pallas_call | solution.py:211
  (321 shorter events, 228.2 us)
Async XLA Ops:
  254.7 71.0 %collective-permute-start = (bf16[256,1536]{1,0:T(8,128)(2,1)}, bf16[256,1536]{1,0:T(8,128)(2,1)}, u32[]{:S(2)}, u32[]{:S(2)}) collective-permute-start(bf16[256,1536]{1,0:T(8,128)(2,1)} %get-tuple-element.72), channel_id=1, source_target_pairs={{0,8},{8,16},{16,24},{24,0},{1,9},{9,17},{17,25},{25,1},{2,10},{10... | collective-permute-start | bytes 2359304 | tf_op jit(solution)/shard_map/ppermute | solution.py:56
  282.9 42.8 %collective-permute-start.2 = (bf16[256,1536]{1,0:T(8,128)(2,1)}, bf16[256,1536]{1,0:T(8,128)(2,1)}, u32[]{:S(2)}, u32[]{:S(2)}) collective-permute-start(bf16[256,1536]{1,0:T(8,128)(2,1)} %get-tuple-element.73), channel_id=1, source_target_pairs={{0,24},{8,0},{16,8},{24,16},{1,25},{9,1},{17,9},{25,17},{2,26},{10... | collective-permute-start | bytes 2359304 | tf_op jit(solution)/shard_map/ppermute | solution.py:56
  282.9 58.2 %collective-permute-start.1 = (bf16[256,1536]{1,0:T(8,128)(2,1)}, bf16[256,1536]{1,0:T(8,128)(2,1)}, u32[]{:S(2)}, u32[]{:S(2)}) collective-permute-start(bf16[256,1536]{1,0:T(8,128)(2,1)} %get-tuple-element.74), channel_id=1, source_target_pairs={{0,16},{8,24},{16,0},{24,8},{1,17},{9,25},{17,1},{25,9},{2,18},{10... | collective-permute-start | bytes 2359304 | tf_op jit(solution)/shard_map/ppermute | solution.py:56
  297.5 200.7 %collective-permute-start.42 = (bf16[4,192,4608]{2,1,0:T(8,128)(2,1)}, bf16[4,192,4608]{2,1,0:T(8,128)(2,1)}, u32[]{:S(2)}, u32[]{:S(2)}) collective-permute-start(bf16[4,192,4608]{2,1,0:T(8,128)(2,1)} %dynamic-slice_bitcast_fusion), channel_id=1, source_target_pairs={{0,1},{1,0},{2,3},{3,2},{4,5},{5,4},{6,7},{7,6},{8,9},{9,8},{10,11... | collective-permute-start | bytes 21233672 | tf_op jit(solution)/shard_map/ppermute | solution.py:51
  376.9 88.9 %collective-permute-start.29 = (bf16[4,192,1536]{2,1,0:T(8,128)(2,1)}, bf16[4,192,1536]{2,1,0:T(8,128)(2,1)}, u32[]{:S(2)}, u32[]{:S(2)}) collective-permute-start(bf16[4,192,1536]{2,1,0:T(8,128)(2,1)} %dynamic-slice_bitcast_fusion.3), channel_id=1, source_target_pairs={{0,1},{1,0},{2,3},{3,2},{4,5},{5,4},{6,7},{7,6},{8,9},{9,8},{10,11... | collective-permute-start | bytes 7077896 | tf_op jit(solution)/shard_map/ppermute | solution.py:51
  443.8 39.5 %collective-permute-start.55 = (bf16[4,288,1536]{2,1,0:T(8,128)(2,1)}, bf16[4,288,1536]{2,1,0:T(8,128)(2,1)}, u32[]{:S(2)}, u32[]{:S(2)}) collective-permute-start(bf16[4,288,1536]{2,1,0:T(8,128)(2,1)} %dynamic-slice_bitcast_fusion.1), channel_id=1, source_target_pairs={{0,1},{1,0},{2,3},{3,2},{4,5},{5,4},{6,7},{7,6},{8,9},{9,8},{10,11... | collective-permute-start | bytes 10616840 | tf_op jit(solution)/shard_map/ppermute | solution.py:51
  491.1 52.5 %collective-permute-start.57 = (bf16[144,1536]{1,0:T(8,128)(2,1)}, bf16[144,1536]{1,0:T(8,128)(2,1)}, u32[]{:S(2)}, u32[]{:S(2)}) collective-permute-start(bf16[144,1536]{1,0:T(8,128)(2,1)} %get-tuple-element.61), channel_id=1, source_target_pairs={{0,4},{1,5},{2,6},{3,7},{4,0},{5,1},{6,2},{7,3},{8,12},{9,13},{10,... | collective-permute-start | bytes 1327112 | tf_op jit(solution)/shard_map/ppermute | solution.py:51
  510.5 34.9 %collective-permute-start.59 = (bf16[144,1536]{1,0:T(8,128)(2,1)S(1)}, bf16[144,1536]{1,0:T(8,128)(2,1)S(1)}, u32[]{:S(2)}, u32[]{:S(2)}) collective-permute-start(bf16[144,1536]{1,0:T(8,128)(2,1)S(1)} %copy-done.21), channel_id=1, source_target_pairs={{0,2},{1,3},{2,0},{3,1},{4,6},{5,7},{6,4},{7,5},{8,10},{9,11},{10,... | collective-permute-start | bytes 1327112 | tf_op jit(solution)/shard_map/ppermute | solution.py:51
  512.5 28.7 %collective-permute-start.46 = (bf16[96,4608]{1,0:T(8,128)(2,1)S(1)}, bf16[96,4608]{1,0:T(8,128)(2,1)S(1)}, u32[]{:S(2)}, u32[]{:S(2)}) collective-permute-start(bf16[96,4608]{1,0:T(8,128)(2,1)S(1)} %get-tuple-element.52), channel_id=1, source_target_pairs={{0,2},{1,3},{2,0},{3,1},{4,6},{5,7},{6,4},{7,5},{8,10},{9,11},{10,... | collective-permute-start | bytes 2654216 | tf_op jit(solution)/shard_map/ppermute | solution.py:51
  512.6 30.3 %collective-permute-start.44 = (bf16[96,4608]{1,0:T(8,128)(2,1)S(1)}, bf16[96,4608]{1,0:T(8,128)(2,1)S(1)}, u32[]{:S(2)}, u32[]{:S(2)}) collective-permute-start(bf16[96,4608]{1,0:T(8,128)(2,1)S(1)} %get-tuple-element.53), channel_id=1, source_target_pairs={{0,4},{1,5},{2,6},{3,7},{4,0},{5,1},{6,2},{7,3},{8,12},{9,13},{10,... | collective-permute-start | bytes 2654216 | tf_op jit(solution)/shard_map/ppermute | solution.py:51
  542.9 29.3 %collective-permute-start.43 = (bf16[96,4608]{1,0:T(8,128)(2,1)S(1)}, bf16[96,4608]{1,0:T(8,128)(2,1)S(1)}, u32[]{:S(2)}, u32[]{:S(2)}) collective-permute-start(bf16[96,4608]{1,0:T(8,128)(2,1)S(1)} %get-tuple-element.54), channel_id=1, source_target_pairs={{0,2},{1,3},{2,0},{3,1},{4,6},{5,7},{6,4},{7,5},{8,10},{9,11},{10,... | collective-permute-start | bytes 2654216 | tf_op jit(solution)/shard_map/ppermute | solution.py:51
  543.7 30.3 %collective-permute-start.48 = (bf16[96,4608]{1,0:T(8,128)(2,1)S(1)}, bf16[96,4608]{1,0:T(8,128)(2,1)S(1)}, u32[]{:S(2)}, u32[]{:S(2)}) collective-permute-start(bf16[96,4608]{1,0:T(8,128)(2,1)S(1)} %get-tuple-element.55), channel_id=1, source_target_pairs={{0,4},{1,5},{2,6},{3,7},{4,0},{5,1},{6,2},{7,3},{8,12},{9,13},{10,... | collective-permute-start | bytes 2654216 | tf_op jit(solution)/shard_map/ppermute | solution.py:51
  545.5 39.8 %collective-permute-start.47 = (bf16[96,4608]{1,0:T(8,128)(2,1)S(1)}, bf16[96,4608]{1,0:T(8,128)(2,1)S(1)}, u32[]{:S(2)}, u32[]{:S(2)}) collective-permute-start(bf16[96,4608]{1,0:T(8,128)(2,1)S(1)} %get-tuple-element.50), channel_id=1, source_target_pairs={{0,4},{1,5},{2,6},{3,7},{4,0},{5,1},{6,2},{7,3},{8,12},{9,13},{10,... | collective-permute-start | bytes 2654216 | tf_op jit(solution)/shard_map/ppermute | solution.py:51
  545.8 45.4 %collective-permute-start.45 = (bf16[96,4608]{1,0:T(8,128)(2,1)S(1)}, bf16[96,4608]{1,0:T(8,128)(2,1)S(1)}, u32[]{:S(2)}, u32[]{:S(2)}) collective-permute-start(bf16[96,4608]{1,0:T(8,128)(2,1)S(1)} %get-tuple-element.51), channel_id=1, source_target_pairs={{0,2},{1,3},{2,0},{3,1},{4,6},{5,7},{6,4},{7,5},{8,10},{9,11},{10,... | collective-permute-start | bytes 2654216 | tf_op jit(solution)/shard_map/ppermute | solution.py:51
  553.3 47.4 %collective-permute-start.56 = (bf16[144,1536]{1,0:T(8,128)(2,1)S(1)}, bf16[144,1536]{1,0:T(8,128)(2,1)S(1)}, u32[]{:S(2)}, u32[]{:S(2)}) collective-permute-start(bf16[144,1536]{1,0:T(8,128)(2,1)S(1)} %copy-done.20), channel_id=1, source_target_pairs={{0,2},{1,3},{2,0},{3,1},{4,6},{5,7},{6,4},{7,5},{8,10},{9,11},{10,... | collective-permute-start | bytes 1327112 | tf_op jit(solution)/shard_map/ppermute | solution.py:51
  572.2 30.2 %collective-permute-start.61 = (bf16[144,1536]{1,0:T(8,128)(2,1)S(1)}, bf16[144,1536]{1,0:T(8,128)(2,1)S(1)}, u32[]{:S(2)}, u32[]{:S(2)}) collective-permute-start(bf16[144,1536]{1,0:T(8,128)(2,1)S(1)} %copy-done.19), channel_id=1, source_target_pairs={{0,4},{1,5},{2,6},{3,7},{4,0},{5,1},{6,2},{7,3},{8,12},{9,13},{10,... | collective-permute-start | bytes 1327112 | tf_op jit(solution)/shard_map/ppermute | solution.py:51
  574.0 36.2 %collective-permute-start.58 = (bf16[144,1536]{1,0:T(8,128)(2,1)S(1)}, bf16[144,1536]{1,0:T(8,128)(2,1)S(1)}, u32[]{:S(2)}, u32[]{:S(2)}) collective-permute-start(bf16[144,1536]{1,0:T(8,128)(2,1)S(1)} %get-tuple-element.64), channel_id=1, source_target_pairs={{0,2},{1,3},{2,0},{3,1},{4,6},{5,7},{6,4},{7,5},{8,10},{9,11},{10,... | collective-permute-start | bytes 1327112 | tf_op jit(solution)/shard_map/ppermute | solution.py:51
  591.2 27.4 %collective-permute-start.7 = (bf16[96,2048]{1,0:T(8,128)(2,1)S(1)}, bf16[96,2048]{1,0:T(8,128)(2,1)S(1)}, u32[]{:S(2)}, u32[]{:S(2)}) collective-permute-start(bf16[96,2048]{1,0:T(8,128)(2,1)S(1)} %get-tuple-element.66), channel_id=1, source_target_pairs={{0,2},{1,3},{2,0},{3,1},{4,6},{5,7},{6,4},{7,5},{8,10},{9,11},{10,... | collective-permute-start | bytes 1179656 | tf_op jit(solution)/shard_map/ppermute | solution.py:51
  611.9 74.3 %collective-permute-start.52 = (bf16[192,4608]{1,0:T(8,128)(2,1)S(1)}, bf16[192,4608]{1,0:T(8,128)(2,1)S(1)}, u32[]{:S(2)}, u32[]{:S(2)}) collective-permute-start(bf16[192,4608]{1,0:T(8,128)(2,1)S(1)} %fusion.11), channel_id=1, source_target_pairs={{8,0},{16,8},{24,16},{9,1},{17,9},{25,17},{10,2},{18,10},{26,18},{... | collective-permute-start | bytes 5308424 | tf_op jit(solution)/shard_map/ppermute | solution.py:135
  618.6 68.9 %collective-permute-start.49 = (bf16[192,4608]{1,0:T(8,128)(2,1)S(1)}, bf16[192,4608]{1,0:T(8,128)(2,1)S(1)}, u32[]{:S(2)}, u32[]{:S(2)}) collective-permute-start(bf16[192,4608]{1,0:T(8,128)(2,1)S(1)} %fusion.11), channel_id=1, source_target_pairs={{0,8},{8,16},{16,24},{1,9},{9,17},{17,25},{2,10},{10,18},{18,26},{... | collective-permute-start | bytes 5308424 | tf_op jit(solution)/shard_map/ppermute | solution.py:134
  624.6 38.3 %collective-permute-start.40 = (bf16[48,1536]{1,0:T(8,128)(2,1)S(1)}, bf16[48,1536]{1,0:T(8,128)(2,1)S(1)}, u32[]{:S(2)}, u32[]{:S(2)}) collective-permute-start(bf16[48,1536]{1,0:T(8,128)(2,1)S(1)} %get-tuple-element.41), channel_id=1, source_target_pairs={{0,16},{8,24},{16,0},{24,8},{1,17},{9,25},{17,1},{25,9},{2,18},{10... | collective-permute-start | bytes 442376 | tf_op jit(solution)/shard_map/ppermute | solution.py:56
  626.5 71.1 %collective-permute-start.62 = (bf16[280,1536]{1,0:T(8,128)(2,1)S(1)}, bf16[280,1536]{1,0:T(8,128)(2,1)S(1)}, u32[]{:S(2)}, u32[]{:S(2)}) collective-permute-start(bf16[280,1536]{1,0:T(8,128)(2,1)S(1)} %fusion.15), channel_id=1, source_target_pairs={{0,8},{8,16},{16,24},{1,9},{9,17},{17,25},{2,10},{10,18},{18,26},{... | collective-permute-start | bytes 2580488 | tf_op jit(solution)/shard_map/ppermute | solution.py:134
  628.7 69.6 %collective-permute-start.65 = (bf16[280,1536]{1,0:T(8,128)(2,1)S(1)}, bf16[280,1536]{1,0:T(8,128)(2,1)S(1)}, u32[]{:S(2)}, u32[]{:S(2)}) collective-permute-start(bf16[280,1536]{1,0:T(8,128)(2,1)S(1)} %fusion.15), channel_id=1, source_target_pairs={{8,0},{16,8},{24,16},{9,1},{17,9},{25,17},{10,2},{18,10},{26,18},{... | collective-permute-start | bytes 2580488 | tf_op jit(solution)/shard_map/ppermute | solution.py:135
  686.2 102.4 %collective-permute-start.53 = (bf16[192,4608]{1,0:T(8,128)(2,1)S(1)}, bf16[192,4608]{1,0:T(8,128)(2,1)S(1)}, u32[]{:S(2)}, u32[]{:S(2)}) collective-permute-start(bf16[192,4608]{1,0:T(8,128)(2,1)S(1)} %collective-permute-done.52), channel_id=1, source_target_pairs={{8,0},{16,8},{9,1},{17,9},{10,2},{18,10},{11,3},{19,11},{12,4},{20... | collective-permute-start | bytes 5308424 | tf_op jit(solution)/shard_map/ppermute | solution.py:135
  687.5 102.4 %collective-permute-start.50 = (bf16[192,4608]{1,0:T(8,128)(2,1)S(1)}, bf16[192,4608]{1,0:T(8,128)(2,1)S(1)}, u32[]{:S(2)}, u32[]{:S(2)}) collective-permute-start(bf16[192,4608]{1,0:T(8,128)(2,1)S(1)} %collective-permute-done.49), channel_id=1, source_target_pairs={{8,16},{16,24},{9,17},{17,25},{10,18},{18,26},{11,19},{19,27},{12,... | collective-permute-start | bytes 5308424 | tf_op jit(solution)/shard_map/ppermute | solution.py:134
  689.4 46.4 %collective-permute-start.15 = (bf16[48,2048]{1,0:T(8,128)(2,1)S(1)}, bf16[48,2048]{1,0:T(8,128)(2,1)S(1)}, u32[]{:S(2)}, u32[]{:S(2)}) collective-permute-start(bf16[48,2048]{1,0:T(8,128)(2,1)S(1)} %get-tuple-element.96), channel_id=1, source_target_pairs={{0,24},{8,0},{16,8},{24,16},{1,25},{9,1},{17,9},{25,17},{2,26},{10... | collective-permute-start | bytes 589832 | tf_op jit(solution)/shard_map/ppermute | solution.py:56
  697.6 71.0 %collective-permute-start.63 = (bf16[280,1536]{1,0:T(8,128)(2,1)S(1)}, bf16[280,1536]{1,0:T(8,128)(2,1)S(1)}, u32[]{:S(2)}, u32[]{:S(2)}) collective-permute-start(bf16[280,1536]{1,0:T(8,128)(2,1)S(1)} %collective-permute-done.62), channel_id=1, source_target_pairs={{8,16},{16,24},{9,17},{17,25},{10,18},{18,26},{11,19},{19,27},{12,... | collective-permute-start | bytes 2580488 | tf_op jit(solution)/shard_map/ppermute | solution.py:134
  698.3 71.0 %collective-permute-start.66 = (bf16[280,1536]{1,0:T(8,128)(2,1)S(1)}, bf16[280,1536]{1,0:T(8,128)(2,1)S(1)}, u32[]{:S(2)}, u32[]{:S(2)}) collective-permute-start(bf16[280,1536]{1,0:T(8,128)(2,1)S(1)} %collective-permute-done.65), channel_id=1, source_target_pairs={{8,0},{16,8},{9,1},{17,9},{10,2},{18,10},{11,3},{19,11},{12,4},{20... | collective-permute-start | bytes 2580488 | tf_op jit(solution)/shard_map/ppermute | solution.py:135
  768.6 32.7 %collective-permute-start.64 = (bf16[280,1536]{1,0:T(8,128)(2,1)S(1)}, bf16[280,1536]{1,0:T(8,128)(2,1)S(1)}, u32[]{:S(2)}, u32[]{:S(2)}) collective-permute-start(bf16[280,1536]{1,0:T(8,128)(2,1)S(1)} %collective-permute-done.63), channel_id=1, source_target_pairs={{16,24},{17,25},{18,26},{19,27},{20,28},{21,29},{22,30},{23,31}} | collective-permute-start | bytes 2580488 | tf_op jit(solution)/shard_map/ppermute | solution.py:134
  769.3 32.0 %collective-permute-start.67 = (bf16[280,1536]{1,0:T(8,128)(2,1)S(1)}, bf16[280,1536]{1,0:T(8,128)(2,1)S(1)}, u32[]{:S(2)}, u32[]{:S(2)}) collective-permute-start(bf16[280,1536]{1,0:T(8,128)(2,1)S(1)} %collective-permute-done.66), channel_id=1, source_target_pairs={{8,0},{9,1},{10,2},{11,3},{12,4},{13,5},{14,6},{15,7}} | collective-permute-start | bytes 2580488 | tf_op jit(solution)/shard_map/ppermute | solution.py:135
  788.6 40.4 %collective-permute-start.54 = (bf16[192,4608]{1,0:T(8,128)(2,1)S(1)}, bf16[192,4608]{1,0:T(8,128)(2,1)S(1)}, u32[]{:S(2)}, u32[]{:S(2)}) collective-permute-start(bf16[192,4608]{1,0:T(8,128)(2,1)S(1)} %collective-permute-done.53), channel_id=1, source_target_pairs={{8,0},{9,1},{10,2},{11,3},{12,4},{13,5},{14,6},{15,7}} | collective-permute-start | bytes 5308424 | tf_op jit(solution)/shard_map/ppermute | solution.py:135
  789.9 39.1 %collective-permute-start.51 = (bf16[192,4608]{1,0:T(8,128)(2,1)S(1)}, bf16[192,4608]{1,0:T(8,128)(2,1)S(1)}, u32[]{:S(2)}, u32[]{:S(2)}) collective-permute-start(bf16[192,4608]{1,0:T(8,128)(2,1)S(1)} %collective-permute-done.50), channel_id=1, source_target_pairs={{16,24},{17,25},{18,26},{19,27},{20,28},{21,29},{22,30},{23,31}} | collective-permute-start | bytes 5308424 | tf_op jit(solution)/shard_map/ppermute | solution.py:134
  (73 other events, 832.3 us)

commit v3 on v2

--- a/solution.py
+++ b/solution.py
@@ -36,129 +36,8 @@
     return (jnp.cos(angles), jnp.sin(angles))
 
 
-def rotate(values_in, cosine, sine_table):
-    half_dim = HEAD_DIM // 2
-    shape = (cosine.shape[0],) + (1,) * (values_in.ndim - 2) + (half_dim,)
-    cos_b = cosine.reshape(shape)
-    sin_b = sine_table.reshape(shape)
-    first = values_in[..., :half_dim]
-    second = values_in[..., half_dim:]
-    return jnp.concatenate([first * cos_b - second * sin_b, second * cos_b + first * sin_b], -1)
-
-
-def flip(x, bit):
-    n = lax.axis_size("fsdp")
-    return lax.ppermute(x, "fsdp", [(i, i ^ bit) for i in range(n)])
-
-
-def shift(x, distance):
-    n = lax.axis_size("ctx")
-    return lax.ppermute(x, "ctx", [(i, (i + distance) % n) for i in range(n)])
-
-
-def place(pieces, index, total):
-    rows = pieces[0][1].shape[0]
-    out = jnp.zeros((total * rows,) + pieces[0][1].shape[1:], pieces[0][1].dtype)
-    for block, piece in pieces:
-        start = (block * rows,) + (0,) * (piece.ndim - 1)
-        out = lax.dynamic_update_slice(out, piece, start)
-    return out
-
-
 def half_rows(rows):
     return -(-rows // 32) * 16
-
-
-def plane_gather(shard):
-    n = lax.axis_size("fsdp")
-    me = lax.axis_index("fsdp")
-    pieces = {0: shard}
-    if n == 8:
-        cut = half_rows(shard.shape[0])
-        along_x, along_y = flip(shard, 2), flip(shard, 4)
-        pieces[2], pieces[4] = along_x, along_y
-        pieces[6] = jnp.concatenate([flip(along_x[:cut], 4), flip(along_y[cut:], 2)], 0)
-    else:
-        for k in range(2, n, 2):
-            pieces[k] = flip(shard, k)
-    for k in range(0, n, 2):
-        pieces[k + 1] = flip(pieces[k], 1)
-    return place([(me ^ k, piece) for k, piece in pieces.items()], me, n)
-
-
-def plane_scatter(blocks):
-    n = lax.axis_size("fsdp")
-    me = lax.axis_index("fsdp")
-    chip, core = me // 2, me % 2
-    low = blocks.astype(BF).reshape((n // 2, 2) + blocks.shape[1:])
-    kept = lax.dynamic_index_in_dim(low, core, 1, keepdims=False)
-    given = lax.dynamic_index_in_dim(low, 1 - core, 1, keepdims=False)
-    acc = (kept.astype(F32) + flip(given, 1).astype(F32)).astype(BF)
-
-    def pick(k):
-        return lax.dynamic_index_in_dim(acc, chip ^ k, 0, keepdims=False)
-
-    if n == 8:
-        rows = blocks.shape[1]
-        cut = half_rows(rows) if rows > 1 else 0
-        to_x, to_y, to_far = pick(1), pick(2), pick(3)
-        if cut:
-            first = flip(to_far[:cut], 2)
-            from_x = [flip(to_x[:cut], 2)]
-            second = flip(to_far[cut:], 4)
-            from_y = [flip(to_y[cut:], 4)]
-            from_x.append(flip((to_x[cut:].astype(F32) + second.astype(F32)).astype(BF), 2))
-            from_y.insert(0, flip((to_y[:cut].astype(F32) + first.astype(F32)).astype(BF), 4))
-            from_x, from_y = jnp.concatenate(from_x, 0), jnp.concatenate(from_y, 0)
-            return pick(0).astype(F32) + from_x.astype(F32) + from_y.astype(F32)
-    total = pick(0).astype(F32)
-    for k in range(1, n // 2):
-        total = total + flip(pick(k), 2 * k).astype(F32)
-    return total
-
-
-def ctx_gather(block):
-    n = lax.axis_size("ctx")
-    me = lax.axis_index("ctx")
-    pieces = [(me, block)]
-    for d in range(1, n):
-        pieces.append(((me - d) % n, shift(block, d)))
-    return place(pieces, me, n)
-
-
-def ctx_chain(block):
-    n = lax.axis_size("ctx")
-    me = lax.axis_index("ctx")
-    up, down = [block], [block]
-    for t in range(1, n):
-        up.append(lax.ppermute(up[-1], "ctx", [(i, i + 1) for i in range(t - 1, n - 1)]))
-        down.append(lax.ppermute(down[-1], "ctx", [(i, i - 1) for i in range(1, n - t + 1)]))
-    parts = []
-    for j in range(n):
-        part = block
-        for i in range(n):
-            if i != j:
-                held = up[i - j] if i > j else down[j - i]
-                part = jnp.where(me == i, held, part)
-        parts.append(part)
-    return parts
-
-
-def ctx_scatter(blocks):
-    n = lax.axis_size("ctx")
-    me = lax.axis_index("ctx")
-    total = lax.dynamic_index_in_dim(blocks, me, 0, keepdims=False).astype(F32)
-    low = blocks.astype(BF)
-    for d in range(1, n):
-        part = lax.dynamic_index_in_dim(low, (me + d) % n, 0, keepdims=False)
-        total = total + shift(part, d).astype(F32)
-    return total
-
-
-def ctx_sum(block):
-    n = lax.axis_size("ctx")
-    part = ctx_scatter(block.reshape((n, block.shape[0] // n) + block.shape[1:]))
-    return ctx_gather(part.astype(BF)).astype(F32)
 
 
 def pack_kernel(nz, nf, ff, unit, upad, z_ref, w_ref, out_ref):
@@ -199,22 +78,25 @@
     for k in range(nz):
         for h in range(2):
             for f in range(nf):
-                src = (h * nf + f) * upad
+                src = f * upad
                 dst = h * ff + f * (ff // nf) + k * unit
-                out_ref[:, dst : dst + unit] = refs[k][:, src : src + unit].astype(F32)
-
-
-def unpack(parts, nz, nf, ff):
-    rows, wide = parts[0].shape[0], parts[0].shape[1] // 2
-    unit, upad = ff // (nf * nz), wide // nf
+                part = refs[h * nz + k]
+                out_ref[:, dst : dst + unit] = part[:, src : src + unit].astype(F32)
+
+
+def unpack(gate, up, nz, nf, ff):
+    rows, wide = gate.shape[0] // nz, gate.shape[1]
     step = 32
+    specs = [
+        pl.BlockSpec((step, wide), lambda i, k=k: (k * (rows // step) + i, 0)) for k in range(nz)
+    ]
     return pl.pallas_call(
-        functools.partial(unpack_kernel, nz, nf, ff, unit, upad),
+        functools.partial(unpack_kernel, nz, nf, ff, ff // (nf * nz), wide // nf),
         grid=(rows // step,),
-        in_specs=[pl.BlockSpec((step, 2 * wide), lambda i: (i, 0))] * nz,
+        in_specs=specs * 2,
         out_specs=pl.BlockSpec((step, 2 * ff), lambda i: (i, 0)),
         out_shape=jax.ShapeDtypeStruct((rows, 2 * ff), F32),
-    )(*parts)
+    )(*[gate] * nz, *[up] * nz)
 
 
 MESH = pl.DeviceIdType.MESH
@@ -762,24 +644,524 @@
     )(wq, sm, wo, wp, dn, x, g, cos2, sin2, qpos, kpos)
 
 
+class Scatter:
+    def __init__(self, src, c0, rows, cols, recv4, land, inside, nf, z, me, send, recv, base):
+        self.src, self.c0, self.rows, self.cols = src, c0, rows, cols
+        self.recv4, self.land, self.inside = recv4, land, inside
+        self.nf, self.z, self.me, self.send, self.recv, self.base = nf, z, me, send, recv, base
+        self.chips, self.chip, self.core = nf // 2, me // 2, me % 2
+        self.cut = half_rows(rows)
+        self.sent = []
+        self.got = {}
+
+    @staticmethod
+    def sems(nf):
+        return nf
+
+    def push(self, index, src, dst, flip_by):
+        copy = remote(
+            src, dst, self.send.at[self.base + index], self.recv.at[self.base + index],
+            self.z, self.me ^ flip_by,
+        )
+        copy.start()
+        self.sent.append(copy)
+        self.got[index] = copy
+
+    def mine(self, ref, start, n):
+        return ref.at[pl.ds(pl.multiple_of(start, 16), n)]
+
+    def block(self, k, lo=0, hi=None):
+        hi = self.rows if hi is None else hi
+        return self.mine(self.recv4, (self.chip ^ k) * self.rows + lo, hi - lo)
+
+    def swap(self):
+        for p in range(self.chips):
+            start = pl.multiple_of((2 * p + 1 - self.core) * self.rows, 16)
+            src = self.src.at[pl.ds(start, self.rows), pl.ds(self.c0, self.cols)]
+            self.push(p, src, self.mine(self.recv4, p * self.rows, self.rows), 1)
+
+    def merge(self):
+        rows, cols = self.rows, self.cols
+        for p in range(self.chips):
+            self.got[p].wait_recv()
+        if self.inside:
+            for p in range(self.chips):
+                start = pl.multiple_of((2 * p + self.core) * rows, 16)
+                own = self.src[pl.ds(start, rows), pl.ds(self.c0, cols)]
+                where = pl.ds(p * rows, rows)
+                self.recv4[where, :] = (self.recv4[where, :].astype(F32) + own.astype(F32)).astype(BF)
+            return
+        step = rows if rows <= 96 else rows // 2
+        n = rows // step
+        core, col = self.core, self.c0 // cols
+        own = pl.BlockSpec((step, cols), lambda p, i: ((2 * p + core) * n + i, col))
+        held = pl.BlockSpec((step, cols), lambda p, i: (p * n + i, 0))
+        pltpu.emit_pipeline(
+            add_two, grid=(self.chips, n), in_specs=[own, held], out_specs=[held]
+        )(self.src, self.recv4, self.recv4)
+
+    def add(self, out, parts, n):
+        if self.inside:
+            total = parts[0][...].astype(F32)
+            for part in parts[1:]:
+                total = total + part[...].astype(F32)
+            out[...] = total.astype(BF)
+            return
+        step = n if n <= 96 else n // 2
+        spec = pl.BlockSpec((step, self.cols), lambda i: (i, 0))
+        body = add_two if len(parts) == 2 else add_all
+        pltpu.emit_pipeline(
+            body, grid=(n // step,), in_specs=[spec] * len(parts), out_specs=[spec]
+        )(*parts, out)
+
+    def first(self):
+        base, rows, cut = self.chips, self.rows, self.cut
+        if self.nf == 8:
+            self.push(base, self.block(3, 0, cut), self.land.at[pl.ds(0, cut)], 2)
+            self.push(base + 1, self.block(3, cut), self.land.at[pl.ds(cut, rows - cut)], 4)
+        else:
+            for k in range(1, self.chips):
+                self.push(base + k - 1, self.block(k), self.land.at[pl.ds((k - 1) * rows, rows)], 2 * k)
+
+    def second(self):
+        if self.nf != 8:
+            return
+        base, rows, cut = self.chips, self.rows, self.cut
+        self.got[base].wait_recv()
+        to_y = self.block(2, 0, cut)
+        self.add(to_y, [to_y, self.land.at[pl.ds(0, cut)]], cut)
+        self.push(base + 3, self.block(2), self.land.at[pl.ds(2 * rows, rows)], 4)
+        self.got[base + 1].wait_recv()
+        to_x = self.block(1, cut)
+        self.add(to_x, [to_x, self.land.at[pl.ds(cut, rows - cut)]], rows - cut)
+        self.push(base + 2, self.block(1), self.land.at[pl.ds(rows, rows)], 2)
+
+    def last(self, out):
+        base, rows = self.chips, self.rows
+        if self.nf == 8:
+            incoming = [(base + 2, rows), (base + 3, 2 * rows)]
+        else:
+            incoming = [(base + k - 1, (k - 1) * rows) for k in range(1, self.chips)]
+        for index, _ in incoming:
+            self.got[index].wait_recv()
+        parts = [self.block(0)] + [self.land.at[pl.ds(at, rows)] for _, at in incoming]
+        self.add(out, parts, rows)
+
+    def drain(self):
+        for copy in self.sent:
+            copy.wait_send()
+
+
+def add_two(a, b, out):
+    out[...] = (a[...].astype(F32) + b[...].astype(F32)).astype(BF)
+
+
+def add_all(*refs):
+    total = refs[0][...].astype(F32)
+    for ref in refs[1:-1]:
+        total = total + ref[...].astype(F32)
+    refs[-1][...] = total.astype(BF)
+
+
+class Reduce:
+    def __init__(self, slots, rows, nz, z, me, send, recv, base, order):
+        self.slots, self.rows, self.nz, self.z, self.me = slots, rows, nz, z, me
+        self.send, self.recv, self.base, self.order = send, recv, base, order
+
+    @staticmethod
+    def sems(nz):
+        return nz + 1
+
+    def copy(self, src, dst, step):
+        return remote(
+            rows_at(self.slots, src, self.rows), rows_at(self.slots, dst, self.rows),
+            self.send.at[self.base + src], self.recv.at[self.base + dst], self.z + step, self.me,
+        )
+
+    def give(self, i, part):
+        z, nz, rows = self.z, self.nz, self.rows
+        j = self.order(nz - 1 - i)
+        below, above = j > z, j < z
+        got = jnp.logical_or(jnp.logical_and(below, z > 0), jnp.logical_and(above, z < nz - 1))
+        where = pl.ds(at128(j, rows) if rows % 128 == 0 else pl.multiple_of(j * rows, 16), rows)
+        own = part(j)
+
+        @pl.when(got)
+        def _():
+            self.copy(j, j, 0).wait_recv()
+            self.slots[where, :] = (self.slots[where, :].astype(F32) + own.astype(F32)).astype(BF)
+
+        @pl.when(jnp.logical_not(got))
+        def _():
+            self.slots[where, :] = own.astype(BF)
+
+        @pl.when(below)
+        def _():
+            self.copy(j, j, 1).start()
+
+        @pl.when(above)
+        def _():
+            self.copy(j, jnp.where(z - 1 == j, nz, j), -1).start()
+
+    def take(self, total):
+        z, nz = self.z, self.nz
+
+        @pl.when(z > 0)
+        def _():
+            self.copy(z, z, 0).wait_recv()
+            total[...] += rows_at(self.slots, z, self.rows)[...].astype(F32)
+
+        @pl.when(z < nz - 1)
+        def _():
+            self.copy(z, nz, 0).wait_recv()
+            total[...] += rows_at(self.slots, nz, self.rows)[...].astype(F32)
+
+    def drain(self):
+        def gave(i):
+            j = self.order(i + 1)
+            self.copy(j, j, 0).wait_send()
+
+        loop(self.nz - 1, gave)
+
+
+def back_kernel(
+    dims,
+    dwgu, dwd, dpart, wq_all, wo_all, kv_hbm, mid_hbm, dx_hbm,
+    x_ref, g_ref, q_ref, o_ref, lse_ref, gain_ref, cos_ref, sin_ref, qpos_ref, kpos_ref,
+    hid_ref, gh_ref, all_d, all_g, all_u, z_out, tiny_out,
+    r0, r1, r2, l0, l1, l2,
+    stage, full, dslots, part, do_ref, kv, dkv, kslots, m32, dh, t32, dqkv, mask, normed,
+    r3, l3, r4, l4, zsrc, zslots, zfull, zown, tiny, tin, zin, send, recv, local,
+):
+    nz, nf, rows, d, wide, upad, nb, ng, ch = dims
+    z, me = lax.axis_index("ctx"), lax.axis_index("fsdp")
+    q_width, k_width = HEADS * HEAD_DIM, KV_HEADS * HEAD_DIM
+    qkv = q_width + 2 * k_width
+    scale = HEAD_DIM ** (-0.5)
+    wr = d // nf
+    place = {"nf": nf, "z": z, "me": me, "send": send, "recv": recv}
+    per = Scatter.sems(nf)
+    s_d = Scatter(dwd, 0, upad, d, r0, l0, False, base=0, **place)
+    s_g = Scatter(dwgu, 0, wr, wide, r1, l1, False, base=per, **place)
+    s_u = Scatter(dwgu, wide, wr, wide, r2, l2, False, base=2 * per, **place)
+    s_o = Scatter(full, 0, wr, d, r3, l3, True, base=3 * per, **place)
+    s_q = Scatter(full, 0, wr, qkv, r4, l4, True, base=4 * per, **place)
+    base = 5 * per
+    line = {"nz": nz, "z": z, "me": me, "send": send, "recv": recv}
+    per = Chain.sems(nz)
+    a_d = Chain(all_d, upad, base=base, **line)
+    a_g = Chain(all_g, wr, base=base + per, **line)
+    a_u = Chain(all_u, wr, base=base + 2 * per, **line)
+    a_z = Chain(zfull, ch, base=base + 3 * per, **line)
+    base += 4 * per
+    per = Reduce.sems(nz)
+    d_kv = Reduce(kslots, rows, base=base, order=a_d.order, **line)
+    d_h = Reduce(dslots, rows, base=base + per, order=a_d.order, **line)
+    d_z = Reduce(zslots, ch, base=base + 2 * per, order=a_d.order, **line)
+    base += 3 * per
+
+    def fetch(src, dst, i):
+        copy = pltpu.make_async_copy(src, dst, local.at[i])
+        copy.start()
+        return copy
+
+    wo_in = fetch(wo_all, stage.at[pl.ds(0, q_width), pl.ds(0, d)], 0)
+    mid_in = fetch(mid_hbm, m32, 1)
+    dx_in = fetch(dx_hbm, dh, 2)
+    kv_in = fetch(kv_hbm, kv, 3)
+
+    barrier = pltpu.get_barrier_semaphore()
+    for k in range(1, nf):
+        pl.semaphore_signal(barrier, inc=1, device_id=(z, me ^ k), device_id_type=MESH)
+    for k in range(1, nz):
+        pl.semaphore_signal(barrier, inc=1, device_id=((z + k) % nz, me), device_id_type=MESH)
+    pl.semaphore_wait(barrier, nf + nz - 2)
+
+    s_d.swap()
+    mask[...] = jnp.where(kpos_ref[...] <= qpos_ref[...], 0.0, MASKED)
+    dkv[...] = jnp.zeros_like(dkv)
+    mid_in.wait()
+    dx_in.wait()
+
+    mid, dxn = m32[...], dh[...]
+    inverse_two = lax.rsqrt(jnp.mean(mid * mid, -1, keepdims=True) + EPSILON)
+    scaled = gain_ref[1:2, :] * dxn
+    gain_two = jnp.sum(dxn * mid * inverse_two, 0, keepdims=True)
+    dh[...] = (
+        g_ref[...].astype(F32)
+        + inverse_two * scaled
+        - mid
+        * (inverse_two * inverse_two * inverse_two)
+        * jnp.mean(scaled * mid, -1, keepdims=True)
+    )
+    da = dh[...].astype(BF)
+    normed[...] = da
+    wo_in.wait()
+
+    def do_tile(t):
+        c0 = at128(t, 512)
+        do_ref[:, pl.ds(c0, 512)] = dot_bt(
+            normed[...], stage[pl.ds(c0, 512), pl.ds(0, d)]
+        ).astype(BF)
+
+    loop(q_width // 512, do_tile)
+    kv_in.wait()
+    s_d.merge()
+    s_d.first()
+    s_g.swap()
+
+    def w_out_grad(t):
+        c0 = at128(t, 512)
+        full[pl.ds(0, q_width), pl.ds(c0, 512)] = dot_at(
+            o_ref[...], normed[:, pl.ds(c0, 512)]
+        ).astype(BF)
+
+    loop(d // 512, w_out_grad)
+    lanes = lax.broadcasted_iota(jnp.int32, (rows, HEAD_DIM), 1)
+
+    def head(h):
+        c0 = at128(h, HEAD_DIM)
+        kc = at128(h // (HEADS // KV_HEADS), HEAD_DIM)
+        vc = pl.multiple_of(kc + k_width, HEAD_DIM)
+        q, k, v = q_ref[:, pl.ds(c0, HEAD_DIM)], kv[:, pl.ds(kc, HEAD_DIM)], kv[:, pl.ds(vc, HEAD_DIM)]
+        do = do_ref[:, pl.ds(c0, HEAD_DIM)]
+        lse = jnp.sum(jnp.where(lanes == h, lse_ref[...], 0.0), -1, keepdims=True)
+        delta = jnp.sum(
+            do.astype(F32) * o_ref[:, pl.ds(c0, HEAD_DIM)].astype(F32), -1, keepdims=True
+        )
+        p = jnp.exp(dot_bt(q, k) * scale + mask[...] - lse)
+        dkv[:, pl.ds(vc, HEAD_DIM)] += dot_at(p.astype(BF), do)
+        ds = (p * (dot_bt(do, v) - delta)).astype(BF)
+        dq = dot(ds, k) * scale
+        dkv[:, pl.ds(kc, HEAD_DIM)] += dot_at(ds, q) * scale
+        dqkv[:, pl.ds(c0, HEAD_DIM)] = turn(dq, cos_ref[...], -sin_ref[...]).astype(BF)
+
+    third = HEADS // 3
+    loop(third, head)
+    s_d.second()
+    s_g.merge()
+    s_g.first()
+    s_u.swap()
+    loop(third, lambda h: head(h + third))
+    s_d.last(rows_at(all_d, z, upad))
+    a_d.begin()
+    s_g.second()
+    s_u.merge()
+    s_u.first()
+    s_o.swap()
+    loop(third, lambda h: head(h + 2 * third))
+
+    def kv_part(j):
+        return dkv[pl.ds(at128(j, rows), rows), :]
+
+    for i in range(nz - 1):
+        d_kv.give(i, kv_part)
+        if i == 0:
+            s_o.merge()
+            s_o.first()
+            s_g.last(rows_at(all_g, z, wr))
+            a_g.begin()
+            s_u.second()
+            a_d.forward(1)
+    mine = dkv.at[pl.ds(at128(z, rows), rows)]
+    d_kv.take(mine)
+    for h in range(KV_HEADS):
+        c0 = h * HEAD_DIM
+        dqkv[:, q_width + c0 : q_width + c0 + HEAD_DIM] = turn(
+            mine[:, c0 : c0 + HEAD_DIM], cos_ref[...], -sin_ref[...]
+        ).astype(BF)
+    dqkv[:, q_width + k_width :] = mine[:, k_width:].astype(BF)
+    for k in range(2, nz - 1):
+        a_d.forward(k)
+    s_o.second()
+    s_u.last(rows_at(all_u, z, wr))
+    a_u.begin()
+    wq_in = fetch(wq_all, stage.at[pl.ds(0, d)], 0)
+    x = x_ref[...].astype(F32)
+    inverse = lax.rsqrt(jnp.mean(x * x, -1, keepdims=True) + EPSILON)
+    normed[...] = (x * inverse * gain_ref[0:1, :]).astype(BF)
+    s_o.last(zsrc.at[pl.ds(0, wr), pl.ds(0, d)])
+    s_o.drain()
+
+    def w_qkv_grad(t):
+        c0 = at128(t, 512)
+        full[pl.ds(0, d), pl.ds(c0, 512)] = dot_at(normed[...], dqkv[:, pl.ds(c0, 512)]).astype(BF)
+
+    loop(qkv // 512, w_qkv_grad)
+    s_q.swap()
+    wq_in.wait()
+    for k in range(1, nz - 1):
+        a_g.forward(k)
+    a_d.forward(nz - 1)
+
+    def dxn_tile(t):
+        c0 = at128(t, 512)
+        t32[:, pl.ds(c0, 512)] = dot_bt(dqkv[...], stage[pl.ds(c0, 512), :])
+
+    loop(d // 512, dxn_tile)
+    dxn = t32[...]
+    scaled = gain_ref[0:1, :] * dxn
+    gain_one = jnp.sum(dxn * x * inverse, 0, keepdims=True)
+    bias = jnp.sum(dqkv[...].astype(F32), 0, keepdims=True)
+    gh_ref[...] = (
+        dh[...]
+        + inverse * scaled
+        - x * (inverse * inverse * inverse) * jnp.mean(scaled * x, -1, keepdims=True)
+    ).astype(BF)
+
+    cut = q_width + k_width
+    qk, vb = cut // nf, k_width // nf
+    tiny[...] = jnp.zeros_like(tiny)
+    for f in range(nf):
+        r = slice(8 * f, 8 * f + 1)
+        tiny[r, 0:qk] = bias[:, f * qk : (f + 1) * qk]
+        tiny[r, qk : qk + vb] = bias[:, cut + f * vb : cut + (f + 1) * vb]
+        tiny[r, qk + vb : qk + vb + ng] = gain_one[:, f * ng : (f + 1) * ng]
+        tiny[r, qk + vb + ng : qk + vb + 2 * ng] = gain_two[:, f * ng : (f + 1) * ng]
+    tin[pl.ds(pl.multiple_of(me * 8, 8), 8), :] = tiny[pl.ds(pl.multiple_of(me * 8, 8), 8), :]
+    tiny_copies = []
+    for k in range(1, nf):
+        copy = remote(
+            rows_at(tiny, me ^ k, 8), rows_at(tin, me, 8), send.at[base + k], recv.at[base + k], z, me ^ k
+        )
+        copy.start()
+        tiny_copies.append(copy)
+    base += nf
+
+    s_q.merge()
+    s_q.first()
+    for copy in tiny_copies:
+        copy.wait_recv()
+    total = tin[0:8, :]
+    for f in range(1, nf):
+        total = total + tin[8 * f : 8 * f + 8, :]
+    zin[pl.ds(pl.multiple_of(z * 8, 8), 8), :] = total
+    for k in range(1, nz):
+        copy = remote(
+            rows_at(zin, z, 8), rows_at(zin, z, 8), send.at[base + k], recv.at[base + k], (z + k) % nz, me
+        )
+        copy.start()
+        tiny_copies.append(copy)
+
+    def down_part(j):
+        copy = pltpu.make_async_copy(rows_at(dpart, j, rows), part, local.at[1])
+        copy.start()
+        copy.wait()
+        return part[...]
+
+    for i in range(nz - 1):
+        d_h.give(i, down_part)
+        if i == 0:
+            s_q.second()
+        if i == 1:
+            for k in range(1, nz - 1):
+                a_u.forward(k)
+    s_q.last(zsrc.at[pl.ds(0, wr), pl.ds(d, qkv)])
+
+    def z_part(j):
+        return zsrc[pl.ds(pl.multiple_of(j * ch, 16), ch), :]
+
+    for i in range(nz - 1):
+        d_z.give(i, z_part)
+    zown[...] = z_part(z).astype(F32)
+    d_z.take(zown)
+    zfull[pl.ds(pl.multiple_of(z * ch, 16), ch), :] = zown[...].astype(BF)
+    a_z.begin()
+    for k in range(1, nz):
+        a_z.forward(k)
+        a_z.arrive(k)
+    z_put = fetch(zfull, z_out, 2)
+    m32[...] += down_part(z).astype(F32)
+    d_h.take(m32)
+    hid_ref[...] = m32[...].astype(BF)
+    for copy in tiny_copies[nf - 1 :]:
+        copy.wait_recv()
+    total = zin[0:8, :]
+    for j in range(1, nz):
+        total = total + zin[8 * j : 8 * j + 8, :]
+    tiny_out[...] = total
+    a_g.forward(nz - 1)
+    a_u.forward(nz - 1)
+    for chain in (a_d, a_g, a_u):
+        for k in range(1, nz):
+            chain.arrive(k)
+    for item in (s_d, s_g, s_u, s_q, a_d, a_g, a_u, a_z, d_kv, d_h, d_z):
+        item.drain()
+    for copy in tiny_copies:
+        copy.wait_send()
+    z_put.wait()
+
+
+def back(dims, *args):
+    nz, nf, rows, d, wide, upad, nb, ng, ch = dims
+    q_width, k_width = HEADS * HEAD_DIM, KV_HEADS * HEAD_DIM
+    qkv = q_width + 2 * k_width
+    tokens, chips, wr = nz * rows, nf // 2, d // nf
+    tiny = -(-((qkv + 2 * d) // nf) // 128) * 128
+    any_, vm = pl.BlockSpec(memory_space=pl.ANY), pl.BlockSpec(memory_space=pltpu.VMEM)
+    out = jax.ShapeDtypeStruct
+    sems = 5 * Scatter.sems(nf) + 4 * Chain.sems(nz) + 3 * Reduce.sems(nz) + nf + nz
+    pieces = [(upad, d), (wr, wide), (wr, wide)]
+    return pl.pallas_call(
+        functools.partial(back_kernel, dims),
+        in_specs=[any_] * 8 + [vm] * 10,
+        out_specs=[vm, vm] + [any_] * 4 + [vm] + [any_] * 6,
+        out_shape=[out((rows, d), BF), out((rows, d), BF)]
+        + [out((nz * r, c), BF) for r, c in pieces]
+        + [out((nz * ch, d + qkv), BF), out((8, tiny), F32)]
+        + [out((chips * r, c), BF) for r, c in pieces]
+        + [out(((chips - 1) * r, c), BF) for r, c in pieces],
+        scratch_shapes=[
+            pltpu.VMEM((d, qkv), BF),
+            pltpu.VMEM((d, qkv), BF),
+            pltpu.VMEM(((nz + 1) * rows, d), BF),
+            pltpu.VMEM((rows, d), BF),
+            pltpu.VMEM((rows, q_width), BF),
+            pltpu.VMEM((tokens, 2 * k_width), BF),
+            pltpu.VMEM((tokens, 2 * k_width), F32),
+            pltpu.VMEM(((nz + 1) * rows, 2 * k_width), BF),
+            pltpu.VMEM((rows, d), F32),
+            pltpu.VMEM((rows, d), F32),
+            pltpu.VMEM((rows, d), F32),
+            pltpu.VMEM((rows, qkv), BF),
+            pltpu.VMEM((rows, tokens), F32),
+            pltpu.VMEM((rows, d), BF),
+            pltpu.VMEM((chips * wr, d), BF),
+            pltpu.VMEM(((chips - 1) * wr, d), BF),
+            pltpu.VMEM((chips * wr, qkv), BF),
+            pltpu.VMEM(((chips - 1) * wr, qkv), BF),
+            pltpu.VMEM((nz * ch, d + qkv), BF),
+            pltpu.VMEM(((nz + 1) * ch, d + qkv), BF),
+            pltpu.VMEM((nz * ch, d + qkv), BF),
+            pltpu.VMEM((ch, d + qkv), F32),
+            pltpu.VMEM((nf * 8, tiny), F32),
+            pltpu.VMEM((nf * 8, tiny), F32),
+            pltpu.VMEM((nz * 8, tiny), F32),
+            pltpu.SemaphoreType.DMA((sems,)),
+            pltpu.SemaphoreType.DMA((sems,)),
+            pltpu.SemaphoreType.DMA((4,)),
+        ],
+        compiler_params=pltpu.CompilerParams(
+            collective_id=1, has_side_effects=True, vmem_limit_bytes=VMEM_LIMIT
+        ),
+    )(*args)
+
+
 def shards(
     hidden_in, w_qkv, b_qkv, w_out, w_gate_up, w_down, gain_attn, gain_mlp, block_order, cotangent
 ):
     nz, nf = lax.axis_size("ctx"), lax.axis_size("fsdp")
     z, me = lax.axis_index("ctx"), lax.axis_index("fsdp")
-    groups = HEADS // KV_HEADS
     q_width, k_width = HEADS * HEAD_DIM, KV_HEADS * HEAD_DIM
     rows = hidden_in.shape[1]
     piece_len = rows // 2
     ff = w_gate_up.shape[1] // 2
     unit = ff // (nf * nz)
-    scale = HEAD_DIM ** (-0.5)
     order_row = block_order[0]
     all_places = (
         order_row[:, None] * piece_len + jnp.arange(piece_len, dtype=jnp.int32)[None, :]
     ).reshape(-1)
     my_places = lax.dynamic_slice_in_dim(all_places, z * rows, rows)
-    visible = all_places[None, :] <= my_places[:, None]
     cosine, sine_table = angle_tables(my_places)
     cos2 = jnp.concatenate([cosine, cosine], 1)
     sin2 = jnp.concatenate([-sine_table, sine_table], 1)
@@ -801,102 +1183,27 @@
         w_qkv, small, w_out, packed, down_mine, hidden_in[0], grad_low, cos2, sin2,
         my_places[:, None], all_places[None, :],
     )
-    gain_first, gain_second = gains[0], gains[1]
-    inputs = hidden_in[0].astype(F32)
-    inverse_one = lax.rsqrt(jnp.mean(inputs * inputs, -1, keepdims=True) + EPSILON)
-    normed = (inputs * inverse_one * gain_first).astype(BF)
-    inverse_two = lax.rsqrt(jnp.mean(middle * middle, -1, keepdims=True) + EPSILON)
-    queries = q_low.reshape(rows, KV_HEADS, groups, HEAD_DIM)
-    keys_all = kv_all[:, :k_width].reshape(-1, KV_HEADS, HEAD_DIM)
-    values_all = kv_all[:, k_width:].reshape(-1, KV_HEADS, HEAD_DIM)
-    attn_heads = attn_low.astype(F32).reshape(rows, KV_HEADS, groups, HEAD_DIM).transpose(1, 2, 0, 3)
-    log_total = lse[:, :HEADS].reshape(rows, KV_HEADS, groups).transpose(1, 2, 0)[..., None]
-    down_sum = ctx_scatter(down_part.reshape(nz, rows, -1))
-    hidden_out = (middle + down_sum).astype(BF)[None]
-    down_sums = plane_scatter(down_local.reshape(nf, upad, -1))[:unit]
-    grad_down = jnp.concatenate(ctx_chain(down_sums.astype(BF)), 0).astype(F32)
-    gate_up_sums = plane_scatter(gate_up_local.reshape(nf, -1, 2 * wide))
-    grad_gate_up = unpack(ctx_chain(gate_up_sums.astype(BF)), nz, nf, ff)
-
-    grad_full = grad_low.astype(F32)
-    scaled_two = gain_second * grad_normed_two
-    gain_two_local = jnp.sum(grad_normed_two * middle * inverse_two, 0)
-    grad_middle = (
-        grad_full
-        + inverse_two * scaled_two
-        - middle
-        * (inverse_two * inverse_two * inverse_two)
-        * jnp.mean(scaled_two * middle, -1, keepdims=True)
-    )
-    grad_branch = grad_middle.astype(BF)
-    out_local = dot_at(attn_low, grad_branch)
-    grad_out = ctx_sum(plane_scatter(out_local.reshape(nf, -1, out_local.shape[1])))
-    grad_attn = dot_bt(grad_branch, whole_out).astype(BF)
-    grad_heads = grad_attn.reshape(rows, KV_HEADS, groups, HEAD_DIM).transpose(1, 2, 0, 3)
-    row_delta = jnp.sum(grad_heads.astype(F32) * attn_heads, -1, keepdims=True)
-    scores = jnp.einsum("qkgd,tkd->kgqt", queries, keys_all, preferred_element_type=F32) * scale
-    probs = jnp.where(visible, jnp.exp(scores - log_total), 0.0)
-    grad_values = jnp.einsum(
-        "kgqt,kgqd->tkd", probs.astype(BF), grad_heads, preferred_element_type=F32
-    )
-    grad_probs = jnp.einsum("kgqd,tkd->kgqt", grad_heads, values_all, preferred_element_type=F32)
-    grad_scores = (probs * (grad_probs - row_delta)).astype(BF)
-    grad_queries = (
-        jnp.einsum("kgqt,tkd->kgqd", grad_scores, keys_all, preferred_element_type=F32) * scale
-    )
-    grad_keys = (
-        jnp.einsum("kgqt,qkgd->tkd", grad_scores, queries, preferred_element_type=F32) * scale
-    )
-    kv_grads = jnp.concatenate(
-        [grad_keys.reshape(nz, rows, k_width), grad_values.reshape(nz, rows, k_width)], -1
-    )
-    kv_grad = ctx_scatter(kv_grads)
-    query_back = rotate(grad_queries.transpose(2, 0, 1, 3), cosine, -sine_table).reshape(
-        rows, q_width
-    )
-    key_back = rotate(
-        kv_grad[:, :k_width].reshape(rows, KV_HEADS, HEAD_DIM), cosine, -sine_table
-    ).reshape(rows, k_width)
-    grad_projected = jnp.concatenate([query_back, key_back, kv_grad[:, k_width:]], 1).astype(BF)
-    bias_local = jnp.sum(grad_projected.astype(F32), 0)
-    qkv_local = dot_at(normed, grad_projected)
-    grad_qkv = ctx_sum(plane_scatter(qkv_local.reshape(nf, -1, qkv_local.shape[1])))
-    grad_normed = dot_bt(grad_projected, whole_qkv)
-    scaled_one = gain_first * grad_normed
-    gain_one_local = jnp.sum(grad_normed * inputs * inverse_one, 0)
-    grad_inputs = (
-        grad_middle
-        + inverse_one * scaled_one
-        - inputs
-        * (inverse_one * inverse_one * inverse_one)
-        * jnp.mean(scaled_one * inputs, -1, keepdims=True)
-    )
-    cut = q_width + k_width
-    tiny = jnp.concatenate(
-        [
-            bias_local[:cut].reshape(nf, -1),
-            bias_local[cut:].reshape(nf, -1),
-            gain_one_local.reshape(nf, -1),
-            gain_two_local.reshape(nf, -1),
-        ],
-        1,
-    ).reshape(nf, 1, -1)
-    tiny = plane_scatter(tiny).reshape(nz, -1)
-    tiny = ctx_sum(tiny).reshape(-1)
-    e1 = cut // nf
+    ch = -(-(d // (nf * nz)) // 16) * 16
+    hidden, grad_hidden, down_all, gate_all, up_all, attn_all, tiny = back(
+        (nz, nf, rows, d, wide, upad, nb, ng, ch),
+        gate_up_local, down_local, down_part, whole_qkv, whole_out, kv_all, middle, grad_normed_two,
+        hidden_in[0], grad_low, q_low, attn_low, lse, gains, cos2, sin2, my_places[:, None], all_places[None, :],
+    )[:7]
+    e1 = (q_width + k_width) // nf
     e2 = e1 + k_width // nf
     e3 = e2 + ng
+    shard = d // nf
     return (
-        hidden_out,
-        grad_inputs.astype(BF)[None],
-        grad_qkv,
-        tiny[:e1],
-        tiny[e1:e2],
-        grad_out,
-        grad_gate_up,
-        grad_down,
-        tiny[e2:e3],
-        tiny[e3:],
+        hidden[None],
+        grad_hidden[None],
+        attn_all[:shard, d:].astype(F32),
+        tiny[0, :e1],
+        tiny[0, e1:e2],
+        attn_all[:shard, :d].astype(F32),
+        unpack(gate_all, up_all, nz, nf, ff),
+        down_all.reshape(nz, upad, d)[:, :unit].reshape(nz * unit, d).astype(F32),
+        tiny[0, e2:e3],
+        tiny[0, e3 : e3 + ng],
     )
 
 

time: 853 us -> 642 us (0.75); the launches traced: 842 us -> 641 us
  Pallas kernels: 253 us -> 618 us
  waiting for transfers between devices: 258 us -> 0 us
  starting transfers between devices: 161 us -> 0 us
  local copies, waits for them, and re-layouts: 71.8 us -> 9.78 us
  other arithmetic: 57.1 us -> 12.3 us
  matrix products: 39.7 us -> 0 us
    pallas_call x1 -> x2, Pallas kernels: 9.32 us -> 374 us  [the longest x1 364 us: back(): pl.pallas_call(functools.partial(back_kernel, dims), in_specs=[any_] * 8...]
    ppermute x68 -> x0, waiting for transfers between devices: 258 us -> none  [the longest x24 149 us: shift(): return lax.ppermute(x, 'ctx', [(i, (i + distance) % n) for i in range(n)])]
    ppermute x68 -> x0, starting transfers between devices: 161 us -> none  [the longest x24 109 us: shift(): return lax.ppermute(x, 'ctx', [(i, (i + distance) % n) for i in range(n)])]
    dot_general x9 -> x0, matrix products: 39.7 us -> none  [the longest x1 8.33 us: shards(): jnp.einsum('kgqt,kgqd->tkd', probs.astype(BF), grad_heads, preferred_elem...]
    convert_element_type x18 -> x3, other arithmetic: 31 us -> 8.74 us  [the longest x1 4.08 us: shards(): down_all.reshape(nz, upad, d)[:, :unit].reshape(nz * unit, d).astype(F32)]
    squeeze x10 -> x1, local copies, waits for them, and re-layouts: 18 us -> 1.41 us  [shards(): tiny[0, e1:e2]]
    dynamic_slice x8 -> x0, local copies, waits for them, and re-layouts: 12.6 us -> none  [the longest x4 8.23 us: ctx_scatter(): part = lax.dynamic_index_in_dim(low, (me + d) % n, 0, keepdims=False)]
    reshape x9 -> x0, local copies, waits for them, and re-layouts: 12.5 us -> none  [the longest x2 3.97 us: shards(): keys_all = kv_all[:, :k_width].reshape(-1, KV_HEADS, HEAD_DIM)]
  transfers between devices with their start and end apart: 68 -> 0, of which waited for: 28 -> 0; matrix products, arithmetic and copies ran while one was open for 18% -> 0% of each run, Pallas kernels for 0% -> 0%
where the time goes in v3:
time: 642 us; the launch traced here: 641 us
  Pallas kernels  618 us (96%)
  other arithmetic  12.3 us (2%)
  local copies, waits for them, and re-layouts  9.78 us (2%)
    pallas_call x1, Pallas kernels, back(): pl.pallas_call(functools.partial(back_kernel, dims), in_specs=[any_] * 8...  364 us
    pallas_call x1, Pallas kernels, front(): pl.pallas_call(functools.partial(front_kernel, dims), in_specs=[any_] * 5...  238 us

profile of v3, /device:TPU:0, one launch (start us, length us, event | category | flops | bytes accessed | tf_op | source)
XLA Modules:
  0.0 640.5 jit_solution(4010135527116327488)
XLA Ops:
  0.6 0.7 multiply_bitcast_fusion
  1.3 0.8 pad_maximum_fusion.2
  2.1 0.7 iota_add_fusion
  2.7 0.1 fusion.2
  2.8 0.6 pad.8.sm
  3.4 0.8 copy.20.qpos_ref
  4.2 0.5 fusion
  4.8 0.8 pad_maximum_fusion
  5.6 1.2 constant_dynamic-slice_fusion
  6.8 1.0 pad.9.dn
  7.8 6.0 shard_map.177.wp
  13.8 237.7 %shard_map.178 = (bf16[1536,2048]{1,0:T(8,128)(2,1)}, bf16[1536,1536]{1,0:T(8,128)(2,1)}, bf16[256,1536]{1,0:T(8,128)(2,1)}, bf16[1024,512]{1,0:T(8,128)(2,1)}, ...) custom-call(bf16[192,2048]{1,0:T(8,128)(2,1)} %wq.1, ...), custom_call_target="tpu_custom_call" | custom-call | tf_op jit(solution)/shard_map/pallas_call | solution.py:607
  251.6 364.1 %shard_map.179 = (bf16[256,1536]{1,0:T(8,128)(2,1)}, bf16[256,1536]{1,0:T(8,128)(2,1)}, bf16[1152,1536]{1,0:T(8,128)(2,1)}, bf16[768,2304]{1,0:T(8,128)(2,1)}, b...) custom-call(bf16[1536,4608]{1,0:T(8,128)(2,1)} %get-tuple-element.29, ...), custom_call_target="tpu_custom_call" | custom-call | tf_op jit(solution)/shard_map/pallas_call | solution.py:1105
  615.7 0.0 copy-start
  615.7 1.4 slice_bitcast_fusion
  617.1 1.3 slice.22
  618.4 1.4 fusion.3
  619.8 2.2 slice_convert_fusion.1
  622.0 2.5 slice_convert_fusion
  624.4 0.0 copy-done
  624.4 0.3 slice.28
  624.8 4.1 bitcast_convert_fusion
  628.8 0.0 copy-start.2
  628.9 0.0 copy-start.1
  628.9 9.9 %shard_map.180 = f32[192,17920]{1,0:T(8,128)} custom-call(bf16[768,2304]{1,0:T(8,128)(2,1)} %get-tuple-element.45.refs_0_.refs_1_.refs_2_.refs_3_, bf16[768,2304]{1,0:T(8,128)(2,1)} %get-tuple-element.45.refs_0_.refs_1_.refs_2_.refs_3_, bf16[768,2304]{1,0:T(8,128)(2,1)} %get-tuple-element.45.refs_0_.refs_1_.refs_2_.refs_3_, ...), custom_call_target="tpu_custom_call" | custom-call | tf_op jit(solution)/shard_map/pallas_call | solution.py:93
  638.8 0.0 copy-done.2
  638.8 0.9 copy.24
  639.7 0.0 copy-done.1
  639.7 0.9 copy.25
  (2 shorter events, 0.0 us)
Async XLA Ops:
  615.7 8.8 %copy-start = (bf16[1152,1536]{1,0:T(8,128)(2,1)S(1)}, bf16[1152,1536]{1,0:T(8,128)(2,1)}, u32[]{:S(2)}) copy-start(bf16[1152,1536]{1,0:T(8,128)(2,1)} %get-tuple-element.47) | copy-start | bytes 10616836
  628.8 9.9 %copy-start.2 = (bf16[256,1536]{1,0:T(8,128)(2,1)S(1)}, bf16[256,1536]{1,0:T(8,128)(2,1)}, u32[]{:S(2)}) copy-start(bf16[256,1536]{1,0:T(8,128)(2,1)} %get-tuple-element.41) | copy-start | bytes 2359300
  628.9 10.8 %copy-start.1 = (bf16[256,1536]{1,0:T(8,128)(2,1)S(1)}, bf16[256,1536]{1,0:T(8,128)(2,1)}, u32[]{:S(2)}) copy-start(bf16[256,1536]{1,0:T(8,128)(2,1)} %get-tuple-element.42) | copy-start | bytes 2359300

commit v4 on v2

v4 whole, which is shorter than its diff:
```python
import functools

import jax
import jax.numpy as jnp
from jax import lax
from jax.experimental import pallas as pl
from jax.experimental.pallas import tpu as pltpu
from jax.sharding import PartitionSpec as P

HEADS = 12
KV_HEADS = 2
HEAD_DIM = 128
EPSILON = 1e-06
THETA = 1000000.0
MASKED = -1e30
BF = jnp.bfloat16
F32 = jnp.float32


def dot(a, b):
    return jnp.dot(a, b, preferred_element_type=F32)


def dot_bt(a, b):
    return lax.dot_general(a, b, (((1,), (1,)), ((), ())), preferred_element_type=F32)


def dot_at(a, b):
    return lax.dot_general(a, b, (((0,), (0,)), ((), ())), preferred_element_type=F32)


def angle_tables(places):
    half_dim = HEAD_DIM // 2
    freqs = THETA ** (-(jnp.arange(half_dim).astype(F32) * 2.0 / HEAD_DIM))
    angles = places.astype(F32)[:, None] * freqs[None, :]
    return (jnp.cos(angles), jnp.sin(angles))


def half_rows(rows):
    return -(-rows // 32) * 16


def pack_kernel(nz, nf, ff, unit, upad, z_ref, w_ref, out_ref):
    for k in range(nz):

        @pl.when(z_ref[0] == k)
        def _():
            for h in range(2):
                for f in range(nf):
                    src = h * ff + f * (ff // nf) + k * unit
                    dst = (h * nf + f) * upad
                    out_ref[:, dst : dst + unit] = w_ref[:, src : src + unit]
                    out_ref[:, dst + unit : dst + upad] = jnp.zeros(
                        (out_ref.shape[0], upad - unit), out_ref.dtype
                    )


def pack(w, nz, nf, z):
    rows, ff = w.shape[0], w.shape[1] // 2
    unit = ff // (nf * nz)
    upad = -(-unit // 16) * 16
    wide = nf * upad
    step = 32
    return pl.pallas_call(
        functools.partial(pack_kernel, nz, nf, ff, unit, upad),
        grid=(rows // step,),
        in_specs=[
            pl.BlockSpec(memory_space=pltpu.SMEM),
            pl.BlockSpec((step, 2 * ff), lambda i: (i, 0)),
        ],
        out_specs=pl.BlockSpec((step, 2 * wide), lambda i: (i, 0)),
        out_shape=jax.ShapeDtypeStruct((rows, 2 * wide), w.dtype),
    )(z.reshape(1).astype(jnp.int32), w)


def unpack_kernel(nz, nf, ff, unit, upad, *refs):
    out_ref = refs[-1]
    for k in range(nz):
        for h in range(2):
            for f in range(nf):
                src = f * upad
                dst = h * ff + f * (ff // nf) + k * unit
                part = refs[h * nz + k]
                out_ref[:, dst : dst + unit] = part[:, src : src + unit].astype(F32)


def unpack(gate, up, nz, nf, ff):
    rows, wide = gate.shape[0] // nz, gate.shape[1]
    step = 32
    specs = [
        pl.BlockSpec((step, wide), lambda i, k=k: (k * (rows // step) + i, 0)) for k in range(nz)
    ]
    return pl.pallas_call(
        functools.partial(unpack_kernel, nz, nf, ff, ff // (nf * nz), wide // nf),
        grid=(rows // step,),
        in_specs=specs * 2,
        out_specs=pl.BlockSpec((step, 2 * ff), lambda i: (i, 0)),
        out_shape=jax.ShapeDtypeStruct((rows, 2 * ff), F32),
    )(*[gate] * nz, *[up] * nz)


MESH = pl.DeviceIdType.MESH
VMEM_LIMIT = 63 * 2**20


def remote(src, dst, send, recv, z, f):
    return pltpu.make_async_remote_copy(
        src_ref=src, dst_ref=dst, send_sem=send, recv_sem=recv, device_id=(z, f), device_id_type=MESH
    )


def rows_at(ref, index, count):
    return ref.at[pl.ds(pl.multiple_of(index * count, count), count)]


class PlaneGather:
    def __init__(self, src, dst, rows, nf, z, me, send, recv, local, base):
        self.src, self.dst, self.rows, self.nf, self.z, self.me = src, dst, rows, nf, z, me
        self.send, self.recv, self.base = send, recv, base
        self.local = pltpu.make_async_copy(src, rows_at(dst, me, rows), local)
        self.sent = []
        self.cut = half_rows(rows)
        self.swaps = {}

    @staticmethod
    def sems(nf):
        return 2 * nf

    def slot(self, k, lo=0, hi=None):
        hi = self.rows if hi is None else hi
        start = pl.multiple_of((self.me ^ k) * self.rows, 16) + lo
        return self.dst.at[pl.ds(pl.multiple_of(start, 16), hi - lo)]

    def push(self, index, src, dst, flip_by):
        copy = remote(
            src, dst, self.send.at[self.base + index], self.recv.at[self.base + index],
            self.z, self.me ^ flip_by,
        )
        copy.start()
        self.sent.append(copy)
        return copy

    def begin(self):
        self.local.start()
        self.direct = {}
        for k in (2, 4) if self.nf == 8 else range(2, self.nf, 2):
            self.direct[k] = self.push(k, self.src, self.slot(0), k)
        self.swaps[0] = self.push(1, self.src, self.slot(0), 1)

    def swap(self, k):
        self.swaps[k] = self.push(k + 1, self.slot(k), self.slot(k), 1)

    def middle(self):
        for k, copy in self.direct.items():
            copy.wait_recv()
            if self.nf == 8:
                if k == 2:
                    self.far_a = self.push(6, self.slot(2, 0, self.cut), self.slot(2, 0, self.cut), 4)
                elif self.cut < self.rows:
                    self.far_b = self.push(
                        8, self.slot(4, self.cut), self.slot(4, self.cut), 2
                    )
            self.swap(k)

    def late(self):
        if self.nf == 8:
            self.far_a.wait_recv()
            if self.cut < self.rows:
                self.far_b.wait_recv()
            self.swap(6)

    def finish(self):
        self.local.wait()
        for copy in self.swaps.values():
            copy.wait_recv()

    def drain(self):
        for copy in self.sent:
            copy.wait_send()


class Chain:
    def __init__(self, buf, rows, nz, z, me, send, recv, base):
        self.buf, self.rows, self.nz, self.z, self.me = buf, rows, nz, z, me
        self.send, self.recv, self.base = send, recv, base

    @staticmethod
    def sems(nz):
        return nz + 2

    def copy(self, j, sem, step):
        slot = rows_at(self.buf, j, self.rows)
        return remote(
            slot, slot, self.send.at[self.base + sem], self.recv.at[self.base + j], self.z + step, self.me
        )

    def order(self, k):
        z, nz = self.z, self.nz
        below, above = z, nz - 1 - z
        m = jnp.minimum(below, above)
        near = jnp.where(k % 2 == 1, z - (k + 1) // 2, z + k // 2)
        far = jnp.where(above > below, z + (k - m), z - (k - m))
        return jnp.where(k <= 2 * m, near, far)

    def begin(self):
        z, nz = self.z, self.nz

        @pl.when(z < nz - 1)
        def _():
            self.copy(z, nz, 1).start()

        @pl.when(z > 0)
        def _():
            self.copy(z, nz + 1, -1).start()

    def passing(self, j):
        z, nz = self.z, self.nz
        return jnp.logical_and(j < z, z < nz - 1), jnp.logical_and(j > z, z > 0)

    def forward(self, k):
        j = self.order(k)
        up, down = self.passing(j)

        @pl.when(up)
        def _():
            self.copy(j, j, 1).wait_recv()
            self.copy(j, j, 1).start()

        @pl.when(down)
        def _():
            self.copy(j, j, -1).wait_recv()
            self.copy(j, j, -1).start()

    def arrive(self, k):
        j = self.order(k)
        up, down = self.passing(j)

        @pl.when(jnp.logical_not(jnp.logical_or(up, down)))
        def _():
            self.copy(j, j, 0).wait_recv()

    def drain(self):
        z, nz = self.z, self.nz

        @pl.when(z < nz - 1)
        def _():
            self.copy(z, nz, 1).wait_send()

        @pl.when(z > 0)
        def _():
            self.copy(z, nz + 1, -1).wait_send()

        def one(k, carry):
            j = self.order(k)
            up, down = self.passing(j)

            @pl.when(jnp.logical_or(up, down))
            def _():
                self.copy(j, j, 0).wait_send()

            return carry

        lax.fori_loop(1, nz, one, 0)


class Scatter:
    def __init__(self, src, c0, rows, cols, recv4, land, inside, nf, z, me, send, recv, base, own=None, sems=None):
        self.src, self.c0, self.rows, self.cols = src, c0, rows, cols
        self.recv4, self.land, self.inside = recv4, land, inside
        self.nf, self.z, self.me, self.send, self.recv, self.base = nf, z, me, send, recv, base
        self.chips, self.chip, self.core = nf // 2, me // 2, me % 2
        self.cut = half_rows(rows)
        self.sent = []
        self.got = {}
        self.own, self.own_sems = own, sems

    @staticmethod
    def sems(nf):
        return nf

    def push(self, index, src, dst, flip_by):
        copy = remote(
            src, dst, self.send.at[self.base + index], self.recv.at[self.base + index],
            self.z, self.me ^ flip_by,
        )
        copy.start()
        self.sent.append(copy)
        self.got[index] = copy

    def mine(self, ref, start, n):
        return ref.at[pl.ds(pl.multiple_of(start, 16), n)]

    def block(self, k, lo=0, hi=None):
        hi = self.rows if hi is None else hi
        return self.mine(self.recv4, (self.chip ^ k) * self.rows + lo, hi - lo)

    def swap(self):
        for p in range(self.chips):
            start = pl.multiple_of((2 * p + 1 - self.core) * self.rows, 16)
            src = self.src.at[pl.ds(start, self.rows), pl.ds(self.c0, self.cols)]
            self.push(p, src, self.mine(self.recv4, p * self.rows, self.rows), 1)

    def merge(self):
        rows, cols = self.rows, self.cols
        if self.own is not None:
            for p in range(min(2, self.chips)):
                self.fetch(p).start()
        for p in range(self.chips):
            self.got[p].wait_recv()
        if self.inside:
            for p in range(self.chips):
                start = pl.multiple_of((2 * p + self.core) * rows, 16)
                if self.own is None:
                    own, first = self.src, start
                else:
                    self.fetch(p).wait()
                    own, first = self.own, p % 2 * rows
                step = rows if rows <= 96 else rows // 2
                for i in range(0, rows, step):
                    where = pl.ds(p * rows + i, step)
                    part = own[pl.ds(pl.multiple_of(first + i, 16), step), pl.ds(0, cols)]
                    self.recv4[where, :] = (
                        self.recv4[where, :].astype(F32) + part.astype(F32)
                    ).astype(BF)
                if self.own is not None and p + 2 < self.chips:
                    self.fetch(p + 2).start()
            return
        step = rows if rows <= 96 else rows // 2
        n = rows // step
        core, col = self.core, self.c0 // cols
        own = pl.BlockSpec((step, cols), lambda p, i: ((2 * p + core) * n + i, col))
        held = pl.BlockSpec((step, cols), lambda p, i: (p * n + i, 0))
        pltpu.emit_pipeline(
            add_two, grid=(self.chips, n), in_specs=[own, held], out_specs=[held]
        )(self.src, self.recv4, self.recv4)

    def fetch(self, p):
        start = pl.multiple_of((2 * p + self.core) * self.rows, 16)
        return pltpu.make_async_copy(
            self.src.at[pl.ds(start, self.rows), pl.ds(self.c0, self.cols)],
            self.own.at[pl.ds(p % 2 * self.rows, self.rows)],
            self.own_sems.at[p % 2],
        )

    def add(self, out, parts, n):
        if self.inside:
            total = parts[0][...].astype(F32)
            for part in parts[1:]:
                total = total + part[...].astype(F32)
            out[...] = total.astype(BF)
            return
        step = n if n <= 96 else n // 2
        spec = pl.BlockSpec((step, self.cols), lambda i: (i, 0))
        body = add_two if len(parts) == 2 else add_all
        pltpu.emit_pipeline(
            body, grid=(n // step,), in_specs=[spec] * len(parts), out_specs=[spec]
        )(*parts, out)

    def first(self):
        base, rows, cut = self.chips, self.rows, self.cut
        if self.nf == 8:
            self.push(base, self.block(3, 0, cut), self.land.at[pl.ds(0, cut)], 2)
            self.push(base + 1, self.block(3, cut), self.land.at[pl.ds(cut, rows - cut)], 4)
        else:
            for k in range(1, self.chips):
                self.push(base + k - 1, self.block(k), self.land.at[pl.ds((k - 1) * rows, rows)], 2 * k)

    def second(self):
        if self.nf != 8:
            return
        base, rows, cut = self.chips, self.rows, self.cut
        self.got[base].wait_recv()
        to_y = self.block(2, 0, cut)
        self.add(to_y, [to_y, self.land.at[pl.ds(0, cut)]], cut)
        self.push(base + 3, self.block(2), self.land.at[pl.ds(2 * rows, rows)], 4)
        self.got[base + 1].wait_recv()
        to_x = self.block(1, cut)
        self.add(to_x, [to_x, self.land.at[pl.ds(cut, rows - cut)]], rows - cut)
        self.push(base + 2, self.block(1), self.land.at[pl.ds(rows, rows)], 2)

    def last(self, out):
        base, rows = self.chips, self.rows
        if self.nf == 8:
            incoming = [(base + 2, rows), (base + 3, 2 * rows)]
        else:
            incoming = [(base + k - 1, (k - 1) * rows) for k in range(1, self.chips)]
        for index, _ in incoming:
            self.got[index].wait_recv()
        parts = [self.block(0)] + [self.land.at[pl.ds(at, rows)] for _, at in incoming]
        self.add(out, parts, rows)

    def drain(self):
        for copy in self.sent:
            copy.wait_send()
        self.sent = []


def add_two(a, b, out):
    out[...] = (a[...].astype(F32) + b[...].astype(F32)).astype(BF)


def add_all(*refs):
    total = refs[0][...].astype(F32)
    for ref in refs[1:-1]:
        total = total + ref[...].astype(F32)
    refs[-1][...] = total.astype(BF)


def greet_ctx_and_plane(nz, nf, z, me):
    barrier = pltpu.get_barrier_semaphore()
    flips = (1, 2, 4) if nf == 8 else (1,) + tuple(range(2, nf, 2))
    for k in flips:
        pl.semaphore_signal(barrier, inc=1, device_id=(z, me ^ k), device_id_type=MESH)

    @pl.when(z < nz - 1)
    def _():
        pl.semaphore_signal(barrier, inc=1, device_id=(z + 1, me), device_id_type=MESH)

    @pl.when(z > 0)
    def _():
        pl.semaphore_signal(barrier, inc=1, device_id=(z - 1, me), device_id_type=MESH)

    inner = jnp.logical_and(z > 0, z < nz - 1)

    @pl.when(inner)
    def _():
        pl.semaphore_wait(barrier, len(flips) + 2)

    @pl.when(jnp.logical_not(inner))
    def _():
        pl.semaphore_wait(barrier, len(flips) + 1)


def loop(n, body):
    def step(i, carry):
        body(i)
        return carry

    lax.fori_loop(0, n, step, 0)


def at128(i, n):
    return i * n if isinstance(i, int) else pl.multiple_of(i * n, n)


def turn(t, cos2, sin2):
    return t * cos2 + pltpu.roll(t, HEAD_DIM // 2, 1) * sin2


def front_kernel(
    dims,
    wq, sm, wo, wp, dn, x_ref, g_ref, cos_ref, sin_ref, qpos_ref, kpos_ref,
    wq_all, wo_all, q_ref, kv_out, o_ref, lse_ref, mid_ref, dx_ref, gain_ref, dwgu, dpart, d_own, dwd, r0, l0,
    stage, gu, dnb, g_all, x_all, act, dgu, smb, kv, bias, mask, ybuf, send, recv, local,
):
    nz, nf, rows, d, wide, upad, nb, ng = dims
    z, me = lax.axis_index("ctx"), lax.axis_index("fsdp")
    q_width, k_width = HEADS * HEAD_DIM, KV_HEADS * HEAD_DIM
    qkv = q_width + 2 * k_width
    scale = HEAD_DIM ** (-0.5)
    wr = d // nf
    per = PlaneGather.sems(nf)
    plane = [
        PlaneGather(src, dst, r, nf, z, me, send, recv, local.at[i], i * per)
        for i, (src, dst, r) in enumerate(
            [
                (wq.at[:, pl.ds(0, q_width)], wq_all.at[:, pl.ds(0, q_width)], wr),
                (wq.at[:, pl.ds(q_width, 2 * k_width)], wq_all.at[:, pl.ds(q_width, 2 * k_width)], wr),
                (sm, smb, 16),
                (wo, wo_all, wr),
                (wp, gu, wr),
                (dn, dnb, upad),
            ]
        )
    ]
    p_q, p_kv, p_s, p_o, p_gu, p_d = plane
    base = len(plane) * per
    chain = [
        Chain(buf, rows, nz, z, me, send, recv, base + i * Chain.sems(nz))
        for i, buf in enumerate([g_all, kv, x_all])
    ]
    c_g, c_kv, c_x = chain
    base += len(chain) * Chain.sems(nz)
    s_d = Scatter(dwd, 0, upad, d, r0, l0, False, nf, z, me, send, recv, base)
    base += Scatter.sems(nf)
    spare = len(plane)

    g_copy = pltpu.make_async_copy(g_ref, rows_at(g_all, z, rows), local.at[spare])
    g_copy.start()
    greet_ctx_and_plane(nz, nf, z, me)
    p_s.begin()
    p_kv.begin()
    g_copy.wait()
    c_g.begin()

    x = x_ref[...].astype(F32)
    inverse = lax.rsqrt(jnp.mean(x * x, -1, keepdims=True) + EPSILON)
    mask[...] = jnp.where(kpos_ref[...] <= qpos_ref[...], 0.0, MASKED)

    p_s.middle()
    p_kv.middle()
    p_q.begin()
    p_s.late()
    p_kv.late()
    p_s.finish()
    for f in range(nf):
        row = smb[f * 16 : (f + 1) * 16, :].astype(F32)[0:1]
        bias[0:1, f * nb : (f + 1) * nb] = row[:, :nb]
        gain_ref[0:1, f * ng : (f + 1) * ng] = row[:, nb : nb + ng]
        gain_ref[1:2, f * ng : (f + 1) * ng] = row[:, nb + ng : nb + 2 * ng]
    normed = (x * inverse * gain_ref[0:1, :]).astype(BF)
    x_all[pl.ds(at128(z, rows), rows), :] = normed

    def fetch_qkv(c0, n):
        copy = pltpu.make_async_copy(
            wq_all.at[:, pl.ds(c0, n)], stage.at[pl.ds(0, d), pl.ds(c0, n)], local.at[spare]
        )
        copy.start()
        copy.wait()

    p_kv.finish()
    fetch_qkv(q_width, 2 * k_width)

    def project(t):
        c0 = at128(t, 2 * HEAD_DIM)
        y = dot(
            x_all[pl.ds(at128(z, rows), rows), :], stage[pl.ds(0, d), pl.ds(c0, 2 * HEAD_DIM)]
        ) + bias[0:1, pl.ds(c0, 2 * HEAD_DIM)]
        return y, c0

    def project_v(t):
        y, c0 = project(t)
        kv[pl.ds(at128(z, rows), rows), pl.ds(pl.multiple_of(c0 - q_width, 256), 256)] = y.astype(BF)

    def turned(y):
        halves = [
            turn(y[:, h * HEAD_DIM : (h + 1) * HEAD_DIM], cos_ref[...], sin_ref[...]).astype(BF)
            for h in range(2)
        ]
        return jnp.concatenate(halves, 1)

    project_v((q_width + k_width) // 256)
    y, _ = project(q_width // 256)
    kv[pl.ds(at128(z, rows), rows), 0:k_width] = turned(y)
    c_kv.begin()
    p_q.middle()
    p_o.begin()
    for k in range(1, nz - 1):
        c_kv.forward(k)
    p_q.late()
    p_q.finish()
    fetch_qkv(0, q_width)
    c_kv.forward(nz - 1)

    def project_q(t):
        y, c0 = project(t)
        q_ref[:, pl.ds(c0, 256)] = turned(y)

    loop(q_width // 256, project_q)
    p_o.middle()
    p_gu.begin()
    for k in range(1, nz):
        c_kv.arrive(k)
    for k in range(1, nz - 1):
        c_g.forward(k)

    lanes = lax.broadcasted_iota(jnp.int32, (rows, HEAD_DIM), 1)
    lse_ref[...] = jnp.zeros_like(lse_ref)

    def head(h):
        c0 = at128(h, HEAD_DIM)
        kc = at128(h // (HEADS // KV_HEADS), HEAD_DIM)
        vc = pl.multiple_of(kc + k_width, HEAD_DIM)
        s = dot_bt(q_ref[:, pl.ds(c0, HEAD_DIM)], kv[:, pl.ds(kc, HEAD_DIM)]) * scale + mask[...]
        top = jnp.max(s, -1, keepdims=True)
        p = jnp.exp(s - top)
        total = jnp.sum(p, -1, keepdims=True)
        o = dot(p.astype(BF), kv[:, pl.ds(vc, HEAD_DIM)]) / total
        o_ref[:, pl.ds(c0, HEAD_DIM)] = o.astype(BF)
        lse_ref[...] = jnp.where(lanes == h, top + jnp.log(total), lse_ref[...])

    loop(HEADS, head)
    p_o.late()
    p_o.finish()
    fetch = pltpu.make_async_copy(wo_all, stage.at[pl.ds(0, q_width), pl.ds(0, d)], local.at[spare])
    fetch.start()
    fetch.wait()

    def out_proj(t):
        c0 = at128(t, 512)
        mid_ref[:, pl.ds(c0, 512)] = (
            dot(o_ref[...], stage[pl.ds(0, q_width), pl.ds(c0, 512)]) + x_ref[:, pl.ds(c0, 512)].astype(F32)
        )

    loop(d // 512, out_proj)
    mid = mid_ref[...]
    inverse_two = lax.rsqrt(jnp.mean(mid * mid, -1, keepdims=True) + EPSILON)
    x_all[pl.ds(at128(z, rows), rows), :] = (mid * inverse_two * gain_ref[1:2, :]).astype(BF)
    c_x.begin()
    c_g.forward(nz - 1)
    for k in range(1, nz - 1):
        c_x.forward(k)
    p_gu.middle()
    if nz <= 4:
        c_x.forward(nz - 1)
    p_gu.late()
    p_d.begin()
    p_gu.finish()

    cols = 768 if wide % 768 == 0 else 256

    def hidden(j):
        r0 = at128(j, rows)

        def one(t):
            c0 = at128(t, cols)
            xb = x_all[pl.ds(r0, rows), :]
            gate = dot(xb, gu[:, pl.ds(c0, cols)])
            up = dot(xb, gu[:, pl.ds(pl.multiple_of(wide + c0, 128), cols)])
            act[pl.ds(r0, rows), pl.ds(c0, cols)] = (gate * jax.nn.sigmoid(gate) * up).astype(BF)
            dgu[pl.ds(r0, rows), pl.ds(c0, cols)] = gate.astype(BF)
            dgu[pl.ds(r0, rows), pl.ds(pl.multiple_of(wide + c0, 128), cols)] = up.astype(BF)

        loop(wide // cols, one)

    hidden(z)
    if nz > 4:
        c_x.forward(nz - 1)

    def nearest(k):
        c_x.arrive(k)
        hidden(c_x.order(k))

    loop(nz - 2, lambda i: nearest(i + 1))
    p_d.middle()
    nearest(nz - 1)
    for k in range(1, nz):
        c_g.arrive(k)
    part = wide // 2
    tiles = [stage.at[pl.ds(0, part), pl.ds(d + i * 256, 256)] for i in range(2)]

    def put(t, i):
        c0 = at128(t, 256)
        return pltpu.make_async_copy(
            tiles[i], dwd.at[pl.ds(i * part, part), pl.ds(c0, 256)], local.at[spare + i]
        )

    def w_down_grad(t):
        for i in range(2):

            @pl.when(t > 0)
            def _():
                put(t - 1, i).wait()

            tiles[i][...] = dot_at(
                act[:, i * part : (i + 1) * part], g_all[:, pl.ds(at128(t, 256), 256)]
            ).astype(BF)
            put(t, i).start()

    loop(d // 256, w_down_grad)
    for i in range(2):
        put(d // 256 - 1, i).wait()
    s_d.swap()
    p_d.late()
    p_d.finish()

    def back(j):
        r0 = at128(j, rows)

        def one(t):
            c0 = at128(t, cols)
            c1 = pl.multiple_of(wide + c0, 128)
            da = dot_bt(g_all[pl.ds(r0, rows), :], dnb[pl.ds(c0, cols), :])
            gate = dgu[pl.ds(r0, rows), pl.ds(c0, cols)].astype(F32)
            up = dgu[pl.ds(r0, rows), pl.ds(c1, cols)].astype(F32)
            sig = jax.nn.sigmoid(gate)
            dgu[pl.ds(r0, rows), pl.ds(c0, cols)] = (
                da * up * (sig * (1.0 + gate * (1.0 - sig)))
            ).astype(BF)
            dgu[pl.ds(r0, rows), pl.ds(c1, cols)] = (da * gate * sig).astype(BF)

        loop(wide // cols, one)

    rs = base

    slots = stage.at[:, pl.ds(0, d)]

    def slot_copy(src, dst, step):
        return remote(
            rows_at(slots, src, rows), rows_at(slots, dst, rows),
            send.at[rs + src], recv.at[rs + dst], z + step, me,
        )

    hold = nz <= 4

    def sides(i):
        j = c_x.order(nz - 1 - i)
        below, above = j > z, j < z
        got = jnp.logical_or(jnp.logical_and(below, z > 0), jnp.logical_and(above, z < nz - 1))
        return j, below, above, got, (pl.ds(at128(j, rows), rows), pl.ds(0, d))

    def terms(i, at):
        j = sides(i)[0]
        back(j)

        def one(t):
            c0 = at128(t, 512)
            ybuf[at : at + rows, pl.ds(c0, 512)] = dot_bt(
                dgu[pl.ds(at128(j, rows), rows), :], gu[pl.ds(c0, 512), :]
            ).astype(BF)

        loop(d // 512, one)

    def ship(j, below, above):
        @pl.when(below)
        def _():
            slot_copy(j, j, 1).start()

        @pl.when(above)
        def _():
            slot_copy(j, jnp.where(z - 1 == j, nz, j), -1).start()

    def early(i, at):
        j, below, above, got, where = sides(i)

        @pl.when(jnp.logical_not(got))
        def _():
            stage[where] = ybuf[at : at + rows, :]
            ship(j, below, above)

    def late(i, at):
        j, below, above, got, where = sides(i)

        @pl.when(got)
        def _():
            slot_copy(j, j, 0).wait_recv()
            stage[where] = (
                stage[where].astype(F32) + ybuf[at : at + rows, :].astype(F32)
            ).astype(BF)
            ship(j, below, above)

    if hold:
        between = {0: (s_d.merge, s_d.first), 1: (s_d.second,)}
        for i in range(nz - 1):
            terms(i, i * rows)
            early(i, i * rows)
            for step in between.get(i, ()):
                step()
        late(0, 0)
    else:

        def at_once(i):
            terms(i, 0)
            early(i, 0)
            late(i, 0)

        loop(nz - 1, at_once)
        for step in (s_d.merge, s_d.first, s_d.second):
            step()
    back(z)

    def own(t):
        c0 = at128(t, 512)
        dx_ref[:, pl.ds(c0, 512)] = dot_bt(
            dgu[pl.ds(at128(z, rows), rows), :], gu[pl.ds(c0, 512), :]
        )

    loop(d // 512, own)

    c_x.drain()

    def down_terms(t):
        c0 = at128(t, 256)
        g_all[:, pl.ds(c0, 256)] = dot(act[...], dnb[:, pl.ds(c0, 256)]).astype(BF)

    c_g.drain()
    loop(d // 256, down_terms)
    out_p = pltpu.make_async_copy(g_all, dpart, local.at[spare + 3])
    out_p.start()
    if hold:
        for i in range(1, nz - 1):
            late(i, i * rows)
            if i == 1:
                s_d.last(d_own)
    else:
        s_d.last(d_own)
    p_gu.drain()

    def w_gu_grad(t):
        c0 = at128(t, 256)
        gu[:, pl.ds(c0, 256)] = dot_at(x_all[...], dgu[:, pl.ds(c0, 256)]).astype(BF)

    outs = []
    for i in range(2):
        loop(wide // 256, lambda t: w_gu_grad(t + i * (wide // 256)))
        half = pl.ds(i * wide, wide)
        outs.append(pltpu.make_async_copy(gu.at[:, half], dwgu.at[:, half], local.at[spare + i]))
        outs[-1].start()
    out_kv = pltpu.make_async_copy(kv, kv_out, local.at[spare + 2])
    out_kv.start()

    @pl.when(z > 0)
    def _():
        slot_copy(z, z, 0).wait_recv()
        dx_ref[...] += rows_at(slots, z, rows)[...].astype(F32)

    @pl.when(z < nz - 1)
    def _():
        slot_copy(z, nz, 0).wait_recv()
        dx_ref[...] += rows_at(slots, nz, rows)[...].astype(F32)

    for item in (p_q, p_kv, p_s, p_o, p_d, c_kv, s_d):
        item.drain()

    def gave(i):
        j = c_x.order(i + 1)
        slot_copy(j, j, 0).wait_send()

    loop(nz - 1, gave)
    for copy in outs + [out_kv, out_p]:
        copy.wait()


def front(dims, wq, sm, wo, wp, dn, x, g, cos2, sin2, qpos, kpos):
    nz, nf, rows, d, wide, upad, nb, ng = dims
    q_width, k_width = HEADS * HEAD_DIM, KV_HEADS * HEAD_DIM
    qkv = q_width + 2 * k_width
    tokens = nz * rows
    any_, vm = pl.BlockSpec(memory_space=pl.ANY), pl.BlockSpec(memory_space=pltpu.VMEM)
    sems = 6 * PlaneGather.sems(nf) + 3 * Chain.sems(nz) + Scatter.sems(nf) + nz + 1
    chips = nf // 2
    out = jax.ShapeDtypeStruct
    return pl.pallas_call(
        functools.partial(front_kernel, dims),
        in_specs=[any_] * 5 + [vm, any_] + [vm] * 4,
        out_specs=[any_, any_, vm, any_] + [vm] * 5 + [any_] * 6,
        out_shape=[
            out((d, qkv), BF),
            out((q_width, d), BF),
            out((rows, q_width), BF),
            out((tokens, 2 * k_width), BF),
            out((rows, q_width), BF),
            out((rows, HEAD_DIM), F32),
            out((rows, d), F32),
            out((rows, d), F32),
            out((8, d), F32),
            out((d, 2 * wide), BF),
            out((tokens, d), BF),
            out((upad, d), BF),
            out((wide, d), BF),
            out((chips * upad, d), BF),
            out(((chips - 1) * upad, d), BF),
        ],
        scratch_shapes=[
            pltpu.VMEM((max(d, (nz + 1) * rows), qkv), BF),
            pltpu.VMEM((d, 2 * wide), BF),
            pltpu.VMEM((wide, d), BF),
            pltpu.VMEM((tokens, d), BF),
            pltpu.VMEM((tokens, d), BF),
            pltpu.VMEM((tokens, wide), BF),
            pltpu.VMEM((tokens, 2 * wide), BF),
            pltpu.VMEM((nf * 16, sm.shape[1]), BF),
            pltpu.VMEM((tokens, 2 * k_width), BF),
            pltpu.VMEM((8, qkv), F32),
            pltpu.VMEM((rows, tokens), F32),
            pltpu.VMEM(((nz - 1 if nz <= 4 else 1) * rows, d), BF),
            pltpu.SemaphoreType.DMA((sems,)),
            pltpu.SemaphoreType.DMA((sems,)),
            pltpu.SemaphoreType.DMA((10,)),
        ],
        compiler_params=pltpu.CompilerParams(
            collective_id=0, has_side_effects=True, vmem_limit_bytes=VMEM_LIMIT
        ),
    )(wq, sm, wo, wp, dn, x, g, cos2, sin2, qpos, kpos)


class Reduce:
    def __init__(self, slots, rows, nz, z, me, send, recv, base, order):
        self.slots, self.rows, self.nz, self.z, self.me = slots, rows, nz, z, me
        self.send, self.recv, self.base, self.order = send, recv, base, order

    @staticmethod
    def sems(nz):
        return nz + 1

    def copy(self, src, dst, step):
        return remote(
            rows_at(self.slots, src, self.rows), rows_at(self.slots, dst, self.rows),
            self.send.at[self.base + src], self.recv.at[self.base + dst], self.z + step, self.me,
        )

    def give(self, i, part):
        z, nz, rows = self.z, self.nz, self.rows
        j = self.order(nz - 1 - i)
        below, above = j > z, j < z
        got = jnp.logical_or(jnp.logical_and(below, z > 0), jnp.logical_and(above, z < nz - 1))
        where = pl.ds(at128(j, rows) if rows % 128 == 0 else pl.multiple_of(j * rows, 16), rows)
        own = part(j)

        @pl.when(got)
        def _():
            self.copy(j, j, 0).wait_recv()
            self.slots[where, :] = (self.slots[where, :].astype(F32) + own.astype(F32)).astype(BF)

        @pl.when(jnp.logical_not(got))
        def _():
            self.slots[where, :] = own.astype(BF)

        @pl.when(below)
        def _():
            self.copy(j, j, 1).start()

        @pl.when(above)
        def _():
            self.copy(j, jnp.where(z - 1 == j, nz, j), -1).start()

    def take(self, total):
        z, nz = self.z, self.nz

        @pl.when(z > 0)
        def _():
            self.copy(z, z, 0).wait_recv()
            total[...] += rows_at(self.slots, z, self.rows)[...].astype(F32)

        @pl.when(z < nz - 1)
        def _():
            self.copy(z, nz, 0).wait_recv()
            total[...] += rows_at(self.slots, nz, self.rows)[...].astype(F32)

    def drain(self):
        def gave(i):
            j = self.order(i + 1)
            self.copy(j, j, 0).wait_send()

        loop(self.nz - 1, gave)


def back_kernel(
    dims,
    dwgu, d_own, dpart, wq_all, wo_all, kv_hbm, mid_hbm, dx_hbm,
    x_ref, g_ref, q_ref, o_ref, lse_ref, gain_ref, cos_ref, sin_ref, qpos_ref, kpos_ref,
    hid_ref, gh_ref, all_d, all_g, all_u, z_out, tiny_out,
    stage, full, dslots, do_ref, kv, dkv, kslots, m32, dh, t32, dqkv, mask, normed,
    r3, l3, r4, l4, zsrc, zslots, zlow, zown, gain_sums, tiny, tin, zin,
    r1, r2, l1, l2, own2, own_sems, send, recv, local,
):
    nz, nf, rows, d, wide, upad, nb, ng, ch = dims
    z, me = lax.axis_index("ctx"), lax.axis_index("fsdp")
    q_width, k_width = HEADS * HEAD_DIM, KV_HEADS * HEAD_DIM
    qkv = q_width + 2 * k_width
    scale = HEAD_DIM ** (-0.5)
    wr = d // nf
    place = {"nf": nf, "z": z, "me": me, "send": send, "recv": recv}
    per = Scatter.sems(nf)
    own = {"own": own2, "sems": own_sems}
    s_g = Scatter(dwgu, 0, wr, wide, r1, l1, True, base=per, **own, **place)
    s_u = Scatter(dwgu, wide, wr, wide, r2, l2, True, base=2 * per, **own, **place)
    s_o = Scatter(full, 0, wr, d, r3, l3, True, base=3 * per, **place)
    s_q = Scatter(full, 0, wr, qkv, r4, l4, True, base=4 * per, **place)
    base = 5 * per
    line = {"nz": nz, "z": z, "me": me, "send": send, "recv": recv}
    per = Chain.sems(nz)
    a_d = Chain(all_d, upad, base=base, **line)
    a_g = Chain(all_g, wr, base=base + per, **line)
    a_u = Chain(all_u, wr, base=base + 2 * per, **line)
    a_z = Chain(z_out, ch, base=base + 3 * per, **line)
    base += 4 * per
    per = Reduce.sems(nz)
    d_kv = Reduce(kslots, rows, base=base, order=a_d.order, **line)
    d_h = Reduce(dslots, rows, base=base + per, order=a_d.order, **line)
    d_z = Reduce(zslots, ch, base=base + 2 * per, order=a_d.order, **line)
    base += 3 * per

    def fetch(src, dst, i):
        copy = pltpu.make_async_copy(src, dst, local.at[i])
        copy.start()
        return copy

    def stream(src, cols, use):
        copies = []
        for t in range(src.shape[0] // 512):
            slot = stage.at[pl.ds(t % 2 * 512, 512), pl.ds(0, cols)]
            copies.append(
                pltpu.make_async_copy(src.at[pl.ds(t * 512, 512)], slot, local.at[6 + t % 2])
            )
        for copy in copies[:2]:
            copy.start()
        for t, copy in enumerate(copies):
            copy.wait()
            use(t, t % 2 * 512)
            if t + 2 < len(copies):
                copies[t + 2].start()

    mid_in = fetch(mid_hbm, m32, 1)
    dx_in = fetch(dx_hbm, dh, 2)
    kv_in = fetch(kv_hbm, kv, 3)
    d_in = fetch(d_own, rows_at(all_d, z, upad), 4)

    barrier = pltpu.get_barrier_semaphore()
    for k in range(1, nf):
        pl.semaphore_signal(barrier, inc=1, device_id=(z, me ^ k), device_id_type=MESH)
    for k in range(1, nz):
        pl.semaphore_signal(barrier, inc=1, device_id=((z + k) % nz, me), device_id_type=MESH)
    pl.semaphore_wait(barrier, nf + nz - 2)

    mask[...] = jnp.where(kpos_ref[...] <= qpos_ref[...], 0.0, MASKED).astype(BF)
    dkv[...] = jnp.zeros_like(dkv)
    lanes = lax.broadcasted_iota(jnp.int32, (rows, HEAD_DIM), 1)
    mine = dkv.at[pl.ds(at128(z, rows), rows)]
    third = HEADS // 3

    def norm_back():
        mid_in.wait()
        dx_in.wait()
        mid, dxn = m32[...], dh[...]
        inverse_two = lax.rsqrt(jnp.mean(mid * mid, -1, keepdims=True) + EPSILON)
        scaled = gain_ref[1:2, :] * dxn
        gain_sums[1:2, :] = jnp.sum(dxn * mid * inverse_two, 0, keepdims=True)
        dh[...] = (
            g_ref[...].astype(F32)
            + inverse_two * scaled
            - mid
            * (inverse_two * inverse_two * inverse_two)
            * jnp.mean(scaled * mid, -1, keepdims=True)
        )
        normed[...] = dh[...].astype(BF)

    def out_back():
        def one(t, r):
            do_ref[:, t * 512 : t * 512 + 512] = dot_bt(
                normed[...], stage[r : r + 512, 0:d]
            ).astype(BF)

        stream(wo_all, d, one)
        kv_in.wait()

    def w_out_grad():
        def one(t):
            c0 = at128(t, 512)
            full[pl.ds(0, q_width), pl.ds(c0, 512)] = dot_at(
                o_ref[...], normed[:, pl.ds(c0, 512)]
            ).astype(BF)

        loop(d // 512, one)

    def head(h):
        c0 = at128(h, HEAD_DIM)
        kc = at128(h // (HEADS // KV_HEADS), HEAD_DIM)
        vc = pl.multiple_of(kc + k_width, HEAD_DIM)
        q, k, v = q_ref[:, pl.ds(c0, HEAD_DIM)], kv[:, pl.ds(kc, HEAD_DIM)], kv[:, pl.ds(vc, HEAD_DIM)]
        do = do_ref[:, pl.ds(c0, HEAD_DIM)]
        lse = jnp.sum(jnp.where(lanes == h, lse_ref[...], 0.0), -1, keepdims=True)
        delta = jnp.sum(
            do.astype(F32) * o_ref[:, pl.ds(c0, HEAD_DIM)].astype(F32), -1, keepdims=True
        )
        p = jnp.exp(dot_bt(q, k) * scale + mask[...].astype(F32) - lse)
        dkv[:, pl.ds(vc, HEAD_DIM)] += dot_at(p.astype(BF), do)
        ds = (p * (dot_bt(do, v) - delta)).astype(BF)
        dq = dot(ds, k) * scale
        dkv[:, pl.ds(kc, HEAD_DIM)] += dot_at(ds, q) * scale
        dqkv[:, pl.ds(c0, HEAD_DIM)] = turn(dq, cos_ref[...], -sin_ref[...]).astype(BF)

    def kv_part(j):
        return dkv[pl.ds(at128(j, rows), rows), :]

    def down_part(j):
        part = stage.at[pl.ds(0, rows), pl.ds(0, d)]
        fetch(rows_at(dpart, j, rows), part, 1).wait()
        return part[...]

    def z_part(j):
        return zsrc[pl.ds(pl.multiple_of(j * ch, 16), ch), :]

    def project_back():
        for h in range(KV_HEADS):
            c0 = h * HEAD_DIM
            dqkv[:, q_width + c0 : q_width + c0 + HEAD_DIM] = turn(
                mine[:, c0 : c0 + HEAD_DIM], cos_ref[...], -sin_ref[...]
            ).astype(BF)
        dqkv[:, q_width + k_width :] = mine[:, k_width:].astype(BF)

    def w_qkv_grad():
        x = x_ref[...].astype(F32)
        inverse = lax.rsqrt(jnp.mean(x * x, -1, keepdims=True) + EPSILON)
        normed[...] = (x * inverse * gain_ref[0:1, :]).astype(BF)
        s_o.drain()

        def one(t):
            c0 = at128(t, 512)
            full[pl.ds(0, d), pl.ds(c0, 512)] = dot_at(
                normed[...], dqkv[:, pl.ds(c0, 512)]
            ).astype(BF)

        loop(qkv // 512, one)

    tiny_copies = []

    def input_back():
        def one(t, r):
            t32[:, t * 512 : t * 512 + 512] = dot_bt(dqkv[...], stage[r : r + 512, :])

        stream(wq_all, qkv, one)
        x = x_ref[...].astype(F32)
        inverse = lax.rsqrt(jnp.mean(x * x, -1, keepdims=True) + EPSILON)
        dxn = t32[...]
        scaled = gain_ref[0:1, :] * dxn
        gain_one = jnp.sum(dxn * x * inverse, 0, keepdims=True)
        gain_two = gain_sums[1:2, :]
        bias = jnp.sum(dqkv[...].astype(F32), 0, keepdims=True)
        gh_ref[...] = (
            dh[...]
            + inverse * scaled
            - x * (inverse * inverse * inverse) * jnp.mean(scaled * x, -1, keepdims=True)
        ).astype(BF)

        cut = q_width + k_width
        qk, vb = cut // nf, k_width // nf
        tiny[...] = jnp.zeros_like(tiny)
        for f in range(nf):
            r = slice(8 * f, 8 * f + 1)
            tiny[r, 0:qk] = bias[:, f * qk : (f + 1) * qk]
            tiny[r, qk : qk + vb] = bias[:, cut + f * vb : cut + (f + 1) * vb]
            tiny[r, qk + vb : qk + vb + ng] = gain_one[:, f * ng : (f + 1) * ng]
            tiny[r, qk + vb + ng : qk + vb + 2 * ng] = gain_two[:, f * ng : (f + 1) * ng]
        own = pl.ds(pl.multiple_of(me * 8, 8), 8)
        tin[own, :] = tiny[own, :]
        for k in range(1, nf):
            copy = remote(
                rows_at(tiny, me ^ k, 8), rows_at(tin, me, 8),
                send.at[base + k], recv.at[base + k], z, me ^ k,
            )
            copy.start()
            tiny_copies.append(copy)

    def tiny_along():
        for copy in tiny_copies:
            copy.wait_recv()
        total = tin[0:8, :]
        for f in range(1, nf):
            total = total + tin[8 * f : 8 * f + 8, :]
        zin[pl.ds(pl.multiple_of(z * 8, 8), 8), :] = total
        for k in range(1, nz):
            copy = remote(
                rows_at(zin, z, 8), rows_at(zin, z, 8),
                send.at[base + nf + k], recv.at[base + nf + k], (z + k) % nz, me,
            )
            copy.start()
            tiny_copies.append(copy)

    def z_take():
        zown[...] = z_part(z).astype(F32)
        d_z.take(zown)
        zlow[...] = zown[...].astype(BF)
        fetch(zlow, rows_at(z_out, z, ch), 2).wait()

    def h_take():
        m32[...] += down_part(z).astype(F32)
        d_h.take(m32)
        hid_ref[...] = m32[...].astype(BF)

    d_in.wait()
    a_d.begin()
    s_g.swap()
    norm_back()
    out_back()
    w_out_grad()
    s_o.swap()
    s_g.merge()
    s_g.first()
    s_u.swap()
    a_d.forward(1)
    for k in range(2, nz - 1):
        a_d.forward(k)
    loop(third, head)
    loop(third, lambda h: head(h + third))
    loop(third, lambda h: head(h + 2 * third))
    s_u.merge()
    s_g.second()
    s_u.first()
    a_d.forward(nz - 1)
    d_kv.give(0, kv_part)
    for i in range(1, nz - 2):
        d_kv.give(i, kv_part)
    d_kv.give(nz - 2, kv_part)
    s_o.merge()
    s_o.first()
    s_g.last(s_g.block(0))
    fetch(s_g.block(0), rows_at(all_g, z, wr), 4).wait()
    a_g.begin()
    s_u.second()
    a_g.forward(1)
    for k in range(2, nz - 1):
        a_g.forward(k)
    s_o.second()
    d_kv.take(mine)
    d_h.give(0, down_part)
    project_back()
    a_g.forward(nz - 1)
    w_qkv_grad()
    s_q.swap()
    s_o.last(zsrc.at[pl.ds(0, wr), pl.ds(0, d)])
    s_u.last(s_u.block(0))
    fetch(s_u.block(0), rows_at(all_u, z, wr), 5).wait()
    s_q.merge()
    s_q.first()
    a_u.begin()
    a_u.forward(1)
    s_q.second()
    for k in range(2, nz - 1):
        a_u.forward(k)
    a_u.forward(nz - 1)
    input_back()
    s_q.last(zsrc.at[pl.ds(0, wr), pl.ds(d, qkv)])
    d_z.give(0, z_part)
    tiny_along()
    for i in range(1, nz - 2):
        d_z.give(i, z_part)
    for i in range(1, nz - 2):
        d_h.give(i, down_part)
    d_z.give(nz - 2, z_part)
    d_h.give(nz - 2, down_part)
    for k in range(1, nz):
        a_u.arrive(k)
    z_take()
    for k in range(1, nz):
        a_g.arrive(k)
    a_z.begin()
    a_z.forward(1)
    for k in range(1, nz):
        a_d.arrive(k)
    for k in range(2, nz - 1):
        a_z.forward(k)
    a_z.forward(nz - 1)
    h_take()
    for k in range(1, nz):
        a_z.arrive(k)
    for copy in tiny_copies[nf - 1 :]:
        copy.wait_recv()
    total = zin[0:8, :]
    for j in range(1, nz):
        total = total + zin[8 * j : 8 * j + 8, :]
    tiny_out[...] = total
    for item in (s_g, s_u, s_o, s_q, a_d, a_g, a_u, a_z, d_kv, d_h, d_z):
        item.drain()
    for copy in tiny_copies:
        copy.wait_send()


def back(dims, *args):
    nz, nf, rows, d, wide, upad, nb, ng, ch = dims
    q_width, k_width = HEADS * HEAD_DIM, KV_HEADS * HEAD_DIM
    qkv = q_width + 2 * k_width
    tokens, chips, wr = nz * rows, nf // 2, d // nf
    tiny = -(-((qkv + 2 * d) // nf) // 128) * 128
    any_, vm = pl.BlockSpec(memory_space=pl.ANY), pl.BlockSpec(memory_space=pltpu.VMEM)
    out = jax.ShapeDtypeStruct
    sems = 5 * Scatter.sems(nf) + 4 * Chain.sems(nz) + 3 * Reduce.sems(nz) + nf + nz
    pieces = [(upad, d), (wr, wide), (wr, wide)]
    return pl.pallas_call(
        functools.partial(back_kernel, dims),
        in_specs=[any_] * 8 + [vm] * 10,
        out_specs=[vm, vm] + [any_] * 4 + [vm],
        out_shape=[out((rows, d), BF), out((rows, d), BF)]
        + [out((nz * r, c), BF) for r, c in pieces]
        + [out((nz * ch, d + qkv), BF), out((8, tiny), F32)],
        scratch_shapes=[
            pltpu.VMEM((1024, qkv), BF),
            pltpu.VMEM((d, qkv), BF),
            pltpu.VMEM(((nz + 1) * rows, d), BF),
            pltpu.VMEM((rows, q_width), BF),
            pltpu.VMEM((tokens, 2 * k_width), BF),
            pltpu.VMEM((tokens, 2 * k_width), F32),
            pltpu.VMEM(((nz + 1) * rows, 2 * k_width), BF),
            pltpu.VMEM((rows, d), F32),
            pltpu.VMEM((rows, d), F32),
            pltpu.VMEM((rows, d), F32),
            pltpu.VMEM((rows, qkv), BF),
            pltpu.VMEM((rows, tokens), BF),
            pltpu.VMEM((rows, d), BF),
            pltpu.VMEM((chips * wr, d), BF),
            pltpu.VMEM(((chips - 1) * wr, d), BF),
            pltpu.VMEM((chips * wr, qkv), BF),
            pltpu.VMEM(((chips - 1) * wr, qkv), BF),
            pltpu.VMEM((nz * ch, d + qkv), BF),
            pltpu.VMEM(((nz + 1) * ch, d + qkv), BF),
            pltpu.VMEM((ch, d + qkv), BF),
            pltpu.VMEM((ch, d + qkv), F32),
            pltpu.VMEM((8, d), F32),
            pltpu.VMEM((nf * 8, tiny), F32),
            pltpu.VMEM((nf * 8, tiny), F32),
            pltpu.VMEM((nz * 8, tiny), F32),
            pltpu.VMEM((chips * wr, wide), BF),
            pltpu.VMEM((chips * wr, wide), BF),
            pltpu.VMEM(((chips - 1) * wr, wide), BF),
            pltpu.VMEM(((chips - 1) * wr, wide), BF),
            pltpu.VMEM((2 * wr, wide), BF),
            pltpu.SemaphoreType.DMA((2,)),
            pltpu.SemaphoreType.DMA((sems,)),
            pltpu.SemaphoreType.DMA((sems,)),
            pltpu.SemaphoreType.DMA((8,)),
        ],
        compiler_params=pltpu.CompilerParams(
            collective_id=1, has_side_effects=True, vmem_limit_bytes=VMEM_LIMIT
        ),
    )(*args)


def shards(
    hidden_in, w_qkv, b_qkv, w_out, w_gate_up, w_down, gain_attn, gain_mlp, block_order, cotangent
):
    nz, nf = lax.axis_size("ctx"), lax.axis_size("fsdp")
    z, me = lax.axis_index("ctx"), lax.axis_index("fsdp")
    q_width, k_width = HEADS * HEAD_DIM, KV_HEADS * HEAD_DIM
    rows = hidden_in.shape[1]
    piece_len = rows // 2
    ff = w_gate_up.shape[1] // 2
    unit = ff // (nf * nz)
    order_row = block_order[0]
    all_places = (
        order_row[:, None] * piece_len + jnp.arange(piece_len, dtype=jnp.int32)[None, :]
    ).reshape(-1)
    my_places = lax.dynamic_slice_in_dim(all_places, z * rows, rows)
    cosine, sine_table = angle_tables(my_places)
    cos2 = jnp.concatenate([cosine, cosine], 1)
    sin2 = jnp.concatenate([-sine_table, sine_table], 1)

    packed = pack(w_gate_up, nz, nf, z)
    wide = packed.shape[1] // 2
    upad = wide // nf
    down_mine = jnp.pad(
        lax.dynamic_slice_in_dim(w_down, z * unit, unit), ((0, upad - unit), (0, 0))
    )
    nb, ng = b_qkv.shape[0], gain_attn.shape[0]
    d = hidden_in.shape[2]
    small = jnp.concatenate([b_qkv, gain_attn, gain_mlp])
    small = jnp.pad(small[None], ((0, 15), (0, -small.shape[0] % 128)))
    grad_low = cotangent[0]
    (whole_qkv, whole_out, q_low, kv_all, attn_low, lse, middle, grad_normed_two, gains, gate_up_local, down_part,
     down_own, *_) = front(
        (nz, nf, rows, d, wide, upad, nb, ng),
        w_qkv, small, w_out, packed, down_mine, hidden_in[0], grad_low, cos2, sin2,
        my_places[:, None], all_places[None, :],
    )
    ch = -(-(d // (nf * nz)) // 16) * 16
    hidden, grad_hidden, down_all, gate_all, up_all, attn_all, tiny = back(
        (nz, nf, rows, d, wide, upad, nb, ng, ch),
        gate_up_local, down_own, down_part, whole_qkv, whole_out, kv_all, middle, grad_normed_two,
        hidden_in[0], grad_low, q_low, attn_low, lse, gains, cos2, sin2, my_places[:, None], all_places[None, :],
    )
    e1 = (q_width + k_width) // nf
    e2 = e1 + k_width // nf
    e3 = e2 + ng
    shard = d // nf
    return (
        hidden[None],
        grad_hidden[None],
        attn_all[:shard, d:].astype(F32),
        tiny[0, :e1],
        tiny[0, e1:e2],
        attn_all[:shard, :d].astype(F32),
        unpack(gate_all, up_all, nz, nf, ff),
        down_all.reshape(nz, upad, d)[:, :unit].reshape(nz * unit, d).astype(F32),
        tiny[0, e2:e3],
        tiny[0, e3 : e3 + ng],
    )


def solution(mesh):
    placed = (
        P("fsdp", "ctx", None),
        P("fsdp", None),
        P("fsdp"),
        P("fsdp", None),
        P("fsdp", None),
        P("fsdp", None),
        P("fsdp"),
        P("fsdp"),
        P("fsdp", None),
        P("fsdp", "ctx", None),
    )
    return jax.shard_map(
        shards,
        mesh=mesh,
        in_specs=placed,
        out_specs=(
            P("fsdp", "ctx", None),
            P("fsdp", "ctx", None),
            P("fsdp", None),
            P("fsdp"),
            P("fsdp"),
            P("fsdp", None),
            P("fsdp", None),
            P("fsdp", None),
            P("fsdp"),
            P("fsdp"),
        ),
        check_vma=False,
    )
```

time: 853 us -> 552 us (0.65)
  Pallas kernels: 253 us -> 519 us
  waiting for transfers between devices: 258 us -> 0 us
  starting transfers between devices: 161 us -> 0 us
  local copies, waits for them, and re-layouts: 71.8 us -> 9.77 us
  other arithmetic: 57.1 us -> 12.3 us
  matrix products: 39.7 us -> 0 us
    pallas_call x1 -> x2, Pallas kernels: 9.32 us -> 272 us  [the longest x1 262 us: back(): pl.pallas_call(functools.partial(back_kernel, dims), in_specs=[any_] * 8...]
    ppermute x68 -> x0, waiting for transfers between devices: 258 us -> none  [the longest x24 149 us: shift(): return lax.ppermute(x, 'ctx', [(i, (i + distance) % n) for i in range(n)])]
    ppermute x68 -> x0, starting transfers between devices: 161 us -> none  [the longest x24 109 us: shift(): return lax.ppermute(x, 'ctx', [(i, (i + distance) % n) for i in range(n)])]
    dot_general x9 -> x0, matrix products: 39.7 us -> none  [the longest x1 8.33 us: shards(): jnp.einsum('kgqt,kgqd->tkd', probs.astype(BF), grad_heads, preferred_elem...]
    convert_element_type x18 -> x3, other arithmetic: 31 us -> 8.74 us  [the longest x1 4.08 us: shards(): down_all.reshape(nz, upad, d)[:, :unit].reshape(nz * unit, d).astype(F32)]
    squeeze x10 -> x1, local copies, waits for them, and re-layouts: 18 us -> 1.4 us  [shards(): tiny[0, e1:e2]]
    dynamic_slice x8 -> x0, local copies, waits for them, and re-layouts: 12.6 us -> none  [the longest x4 8.23 us: ctx_scatter(): part = lax.dynamic_index_in_dim(low, (me + d) % n, 0, keepdims=False)]
    reshape x9 -> x0, local copies, waits for them, and re-layouts: 12.5 us -> none  [the longest x2 3.97 us: shards(): keys_all = kv_all[:, :k_width].reshape(-1, KV_HEADS, HEAD_DIM)]
  transfers between devices with their start and end apart: 68 -> 0, of which waited for: 28 -> 0; matrix products, arithmetic and copies ran while one was open for 18% -> 0% of each run, Pallas kernels for 0% -> 0%
where the time goes in v4:
time: 552 us; the launch traced here: 543 us
  Pallas kernels  519 us (94%)
  other arithmetic  12.3 us (2%)
  local copies, waits for them, and re-layouts  9.77 us (2%)
    pallas_call x1, Pallas kernels, back(): pl.pallas_call(functools.partial(back_kernel, dims), in_specs=[any_] * 8...  262 us
    pallas_call x1, Pallas kernels, front(): pl.pallas_call(functools.partial(front_kernel, dims), in_specs=[any_] * 5...  241 us

profile of v4, /device:TPU:0, one launch (start us, length us, event | category | flops | bytes accessed | tf_op | source)
XLA Modules:
  0.0 542.6 jit_solution(6828816029510877375)
XLA Ops:
  0.6 0.7 multiply_bitcast_fusion
  1.3 0.8 pad_maximum_fusion.2
  2.1 0.7 iota_add_fusion
  2.7 0.1 fusion.2
  2.8 0.6 pad.8.sm
  3.4 0.8 copy.20.qpos_ref
  4.2 0.5 fusion
  4.8 0.8 pad_maximum_fusion
  5.6 1.2 constant_dynamic-slice_fusion
  6.8 1.0 pad.9.dn
  7.8 6.0 %shard_map.177.wp = bf16[192,4608]{1,0:T(8,128)(2,1)} custom-call(s32[1]{0:T(128)} %bitcast.z_ref, bf16[192,17920]{1,0:T(8,128)(2,1)} %w_ref.1), custom_call_target="tpu_custom_call" | custom-call | tf_op jit(solution)/shard_map/pallas_call | solution.py:64
  13.8 241.4 %shard_map.178 = (bf16[1536,2048]{1,0:T(8,128)(2,1)}, bf16[1536,1536]{1,0:T(8,128)(2,1)}, bf16[256,1536]{1,0:T(8,128)(2,1)}, bf16[1024,512]{1,0:T(8,128)(2,1)}, ...) custom-call(bf16[192,2048]{1,0:T(8,128)(2,1)} %wq.1, ...), custom_call_target="tpu_custom_call" | custom-call | tf_op jit(solution)/shard_map/pallas_call | solution.py:833
  255.2 262.0 %shard_map.179 = (bf16[256,1536]{1,0:T(8,128)(2,1)}, bf16[256,1536]{1,0:T(8,128)(2,1)}, bf16[1152,1536]{1,0:T(8,128)(2,1)}, bf16[768,2304]{1,0:T(8,128)(2,1)}, b...) custom-call(bf16[1536,4608]{1,0:T(8,128)(2,1)} %get-tuple-element.29.dwgu, ...), custom_call_target="tpu_custom_call" | custom-call | tf_op jit(solution)/shard_map/pallas_call | solution.py:1259
  517.3 0.0 copy-start
  517.3 1.4 slice_bitcast_fusion
  518.7 1.3 slice.22
  520.0 1.4 fusion.3
  521.4 2.2 slice_convert_fusion.1
  523.6 2.5 slice_convert_fusion
  526.0 0.0 copy-done
  526.0 0.3 slice.28
  526.4 4.1 bitcast_convert_fusion
  530.5 0.0 copy-start.2
  530.5 0.0 copy-start.1
  530.5 9.9 %shard_map.180 = f32[192,17920]{1,0:T(8,128)} custom-call(bf16[768,2304]{1,0:T(8,128)(2,1)} %get-tuple-element.45.refs_0_.refs_1_.refs_2_.refs_3_, bf16[768,2304]{1,0:T(8,128)(2,1)} %get-tuple-element.45.refs_0_.refs_1_.refs_2_.refs_3_, bf16[768,2304]{1,0:T(8,128)(2,1)} %get-tuple-element.45.refs_0_.refs_1_.refs_2_.refs_3_, ...), custom_call_target="tpu_custom_call" | custom-call | tf_op jit(solution)/shard_map/pallas_call | solution.py:93
  540.4 0.0 copy-done.2
  540.4 0.9 copy.24
  541.3 0.0 copy-done.1
  541.3 0.9 copy.25
  (2 shorter events, 0.0 us)
Async XLA Ops:
  517.3 8.7 %copy-start = (bf16[1152,1536]{1,0:T(8,128)(2,1)S(1)}, bf16[1152,1536]{1,0:T(8,128)(2,1)}, u32[]{:S(2)}) copy-start(bf16[1152,1536]{1,0:T(8,128)(2,1)} %get-tuple-element.47) | copy-start | bytes 10616836
  530.5 9.9 %copy-start.2 = (bf16[256,1536]{1,0:T(8,128)(2,1)S(1)}, bf16[256,1536]{1,0:T(8,128)(2,1)}, u32[]{:S(2)}) copy-start(bf16[256,1536]{1,0:T(8,128)(2,1)} %get-tuple-element.41) | copy-start | bytes 2359300
  530.5 10.8 %copy-start.1 = (bf16[256,1536]{1,0:T(8,128)(2,1)S(1)}, bf16[256,1536]{1,0:T(8,128)(2,1)}, u32[]{:S(2)}) copy-start(bf16[256,1536]{1,0:T(8,128)(2,1)} %get-tuple-element.42) | copy-start | bytes 2359300
